TPU v7x, 32 devices: a whole 2x2x4 slice. The times are simulated.
32 devices in a mesh: groups: 2 (over x), tm: 8 (over z, y), space: 2 (over core).
Axes of the slice: x: 2, y: 2, z: 4, core: 2. Of those that a mesh axis runs over, the one named last changes fastest.
Arguments:
- latents: bfloat16 [32, 12, 80, 2240], P(('groups', 'tm'), 'space'), parts along dimension 0, may hold values from -8 to 8
- proj_weight: bfloat16 [2240, 3360], P('tm'), may hold values from -0.125 to 0.125
Outputs:
- attended: bfloat16 [32, 12, 80, 1120], P(('groups', 'tm'), 'space'), parts along dimension 0
There are 2 independent parts, one for each index of `groups`. A program takes and returns all parts, laid end to end along the dimension named above; an argument that names none is the same for every part. Nothing has to cross between parts.
All inputs are finite; a program needn't handle non-finite values.
Results may differ from a plain program's by a relative error of at most 0.0034.
Values may be sent and summed in bfloat16 or wider, within the bound.
No kernel may reach another device: no remote copies, remote signals or barrier semaphores. Data moves between devices by JAX's collectives and lax.ppermute only.
A program may use at most 128 MiB of HBM per device.

v0:
```python
import jax
import jax.numpy as jnp
from jax import lax
from jax.sharding import PartitionSpec as P

HEADS = 10
HEAD = 112


def entering(value, axis, join, neutral):
    count, mine = (lax.axis_size(axis), lax.axis_index(axis))
    pieces = jax.tree.map(lambda part: lax.all_gather(part, axis), value)
    subtotal = jax.tree.map(
        lambda part, zero: jnp.full_like(part, 0) + jnp.asarray(zero, part.dtype), value, neutral
    )

    def hop(position, subtotal):
        longer = join(subtotal, jax.tree.map(lambda part: part[position], pieces))
        return jax.tree.map(lambda new, old: jnp.where(position < mine, new, old), longer, subtotal)

    return lax.fori_loop(0, count - 1, hop, subtotal)


def add_pairs(earlier, later):
    return (earlier[0] + later[0], earlier[1] + later[1])


def make_adder(flat, shard_rows):
    return jnp.dot(flat, shard_rows, preferred_element_type=jnp.float32)


def project_rows(flat, columns):
    return make_adder(flat, lax.all_gather(columns, "tm", axis=0, tiled=True))


def local_states(projected, heads_here):
    count = projected.shape[0]
    split = projected.astype(jnp.bfloat16).reshape(count, 3, heads_here, HEAD)
    queries = jax.nn.relu(split[:, 0])
    key_feats = jax.nn.relu(split[:, 1])
    values = split[:, 2]
    states = jnp.einsum("nhe,nhf->hef", key_feats, values, preferred_element_type=jnp.float32)
    key_sums = jnp.sum(key_feats, axis=0, dtype=jnp.float32)
    return (queries, states, key_sums)


def apply_states(queries, states, key_sums):
    numerator = jnp.einsum(
        "nhe,hef->nhf", queries, states.astype(jnp.bfloat16), preferred_element_type=jnp.float32
    )
    denominator = jnp.einsum(
        "nhe,he->nh", queries.astype(jnp.float32), key_sums, precision=lax.Precision.HIGHEST
    )
    return (numerator / (denominator[:, :, None] + 1.0)).astype(jnp.bfloat16)


def on_device(latents, proj_weight):
    frame_count, band_rows, column_count, channels = latents.shape
    shard_depth = proj_weight.shape[0]
    band_count = lax.axis_size("space")
    band_index = lax.axis_index("space")
    heads_here = HEADS // band_count
    grouped = proj_weight.reshape(shard_depth, 3, band_count, heads_here * HEAD)
    own_columns = lax.dynamic_index_in_dim(grouped, band_index, 2, keepdims=False)
    own_columns = own_columns.reshape(shard_depth, 3 * heads_here * HEAD)
    both_bands = lax.all_gather(latents, "space", axis=1, tiled=True)
    joined_rows = both_bands.shape[1]
    count = frame_count * joined_rows * column_count
    flat = both_bands.reshape(count, channels)
    projected = project_rows(flat, own_columns)
    queries, states, key_sums = local_states(projected, heads_here)
    identity = (jnp.zeros_like(states), jnp.zeros_like(key_sums))
    earlier = entering((states, key_sums), "tm", add_pairs, identity)
    attended = apply_states(queries, states + earlier[0], key_sums + earlier[1])
    attended = attended.reshape(frame_count, joined_rows, column_count, heads_here * HEAD)
    return lax.all_to_all(attended, "space", split_axis=1, concat_axis=3, tiled=True)


def solution(mesh):
    return jax.shard_map(
        on_device,
        mesh=mesh,
        in_specs=(P(("groups", "tm"), "space", None, None), P("tm", None)),
        out_specs=P(("groups", "tm"), "space", None, None),
        check_vma=False,
    )
```

profile of v0, /device:TPU:27, one launch (start us, length us, event | category | flops | bytes accessed | tf_op | source)
XLA Modules:
  0.0 272.5 jit_solution(16868224540163675632)
XLA Ops:
  6.5 0.0 all-gather.9.cloned.1.call-start
  6.5 0.7 all-gather.9.cloned.1.call-update
  7.3 0.0 all-gather.7.cloned.1.call-start
  7.3 5.4 %reshape.22 = bf16[280,3,2,560]{3,2,1,0:T(2,128)(2,1)S(1)} reshape(bf16[280,3360]{1,0:T(8,128)(2,1)} %param.5) | data formatting | bytes 3763200 | tf_op jit(solution)/shard_map/reshape | solution.py:63
  12.7 3.6 %constant_dynamic-slice_fusion = bf16[280,3,1,560]{3,2,1,0:T(2,128)(2,1)} fusion(bf16[280,3,2,560]{3,2,1,0:T(2,128)(2,1)S(1)} %reshape.22, s32[]{:T(128)S(6)} %select_n.42), kind=kLoop, calls=%fused_computation.21 | loop fusion | bytes 1881604 | tf_op jit(solution)/shard_map/jit(dynamic_index_in_dim)/dynamic_slice | solution.py:64
  16.3 6.2 %copy.25 = bf16[280,3,1,560]{0,3,1,2:T(8,128)(2,1)S(1)} copy(bf16[280,3,1,560]{3,2,1,0:T(2,128)(2,1)} %constant_dynamic-slice_fusion) | data formatting | bytes 1881600
  22.5 2.3 copy.13
  24.8 0.0 all-gather.7.cloned.1.call-update
  24.8 0.0 all-gather.11.cloned.1.call-start
  24.9 5.2 %all-gather.9.cloned.1.call-done = bf16[2,12,80,2240]{3,2,1,0:T(8,128)(2,1)} async-done(((bf16[2,6,80,2240]{3,2,1,0:T(8,128)(2,1)}), bf16[2,12,80,2240]{3,2,1,0:T(8,128)(2,1)}) %all-gather.9.cloned.1.call-update) | async-done | bytes 8601616 | tf_op jit(solution)/shard_map/all_gather | solution.py:66
  30.0 121.3 %all-gather.7.cloned.1.call-done = bf16[2240,1680]{1,0:T(8,128)(2,1)} async-done(((bf16[280,1680]{1,0:T(8,128)(2,1)}), bf16[2240,1680]{1,0:T(8,128)(2,1)}) %all-gather.7.cloned.1.call-update) | async-done | bytes 7526416 | tf_op jit(solution)/shard_map/all_gather | solution.py:33
  151.4 22.4 %convolution_convert_fusion = bf16[1680,1920]{1,0:T(8,128)(2,1)S(1)} fusion(bf16[2240,1680]{1,0:T(8,128)(2,1)} %all-gather.7.cloned.1.call-done, bf16[1920,2240]{1,0:T(8,128)(2,1)} %bitcast.54), kind=kOutput, calls=%fused_computation.2 | convolution fusion | flops 14453913600 | bytes 22579200 | tf_op jit(solution)/shard_map/dot_general | solution.py:29
  173.8 0.0 copy-start
  173.8 2.7 copy-done
  176.5 1.5 fusion.2
  178.0 0.0 all-gather.11.cloned.1.call-update
  178.0 2.1 convert_reduce_fusion
  180.1 22.8 %all-gather.2 = f32[8,5,112]{2,1,0:T(8,128)S(1)} all-gather(f32[1,5,112]{2,1,0:T(8,128)S(1)} %bitcast.53), channel_id=3, replica_groups=mesh['groups'=2,'tm'=8,'space'=2] {'tm'}, dimensions={0}, use_global_device_ids=true | all-gather | bytes 20160 | tf_op jit(solution)/shard_map/all_gather | solution.py:12
  202.9 24.9 %all-gather.11.cloned.1.call-done = f32[40,112,112]{2,1,0:T(8,128)} async-done(((f32[5,112,112]{2,1,0:T(8,128)}), f32[40,112,112]{2,1,0:T(8,128)}) %all-gather.11.cloned.1.call-update) | async-done | bytes 2007056 | tf_op jit(solution)/shard_map/all_gather | solution.py:12
  227.9 7.6 %while.16 = (s32[]{:T(128)}, f32[5,112,112]{2,1,0:T(8,128)S(1)}, f32[5,112]{1,0:T(8,128)S(1)}, s32[]{:T(128)}, f32[8,5,112,112]{3,2,1,0:T(8,128)}, /*index=5*/f32[8,5,112]{2,1,0:T(8,128)S(1)}, s32[]{:T(128)}, s32[]{:T(128)}) while((s32[]{:T(128)}, f32[5,112,112]{2,1,0:T(8,128)S(1)}, f32[5,112]{1,0:T(8,128)S(1)}, s32[]{:T(128)}, ...), condition=%wide.region_2.3_spmd.clone, body=%wide.region_1.2_spmd.clone.sunk | while | flops 189844 | bytes 759475 | solution.py:21
  227.9 1.0 add_select_fusion.4
  228.9 1.0 add_select_fusion.4
  230.0 1.0 add_select_fusion.4
  231.1 1.0 add_select_fusion.4
  232.2 1.0 add_select_fusion.4
  233.3 1.0 add_select_fusion.4
  234.4 1.0 add_select_fusion.4
  235.5 0.0 copy-start.1
  235.5 2.6 fusion.5
  238.2 0.0 copy-done.1
  238.2 2.4 fusion
  240.6 8.0 %reshape.34 = bf16[2,12,80,560]{2,1,0,3:T(8,128)(2,1)} reshape(bf16[1920,5,112]{0,2,1:T(8,128)(2,1)S(1)} %fusion) | data formatting | bytes 4300800 | tf_op jit(solution)/shard_map/reshape | solution.py:75
  248.6 6.0 %copy.16 = bf16[2,12,80,560]{3,2,0,1:T(8,128)(2,1)S(1)} copy(bf16[2,12,80,560]{2,1,0,3:T(8,128)(2,1)} %reshape.34) | data formatting | bytes 4300800 | tf_op jit(solution)/shard_map/reshape | solution.py:75
  254.6 6.0 %all_to_all.18 = bf16[2,12,80,560]{3,2,0,1:T(8,128)(2,1)S(1)} all-to-all(bf16[2,12,80,560]{3,2,0,1:T(8,128)(2,1)S(1)} %copy.16), channel_id=1, replica_groups=mesh['groups'=2,'tm'=8,'space'=2] {'space'}, dimensions={1} | all-to-all | bytes 4300800 | tf_op jit(solution)/shard_map/all_to_all | solution.py:76
  260.6 2.5 copy.18
  263.1 2.9 %all_to_all.16 = bf16[2,6,80,1120]{3,2,1,0:T(8,128)(2,1)} reshape(bf16[2,6,80,2,560]{4,3,2,1,0:T(2,128)(2,1)S(1)} %copy.18) | data formatting | bytes 4300800 | tf_op jit(solution)/shard_map/all_to_all | solution.py:76
  (11 shorter events, 0.1 us)
Async XLA Ops:
  6.5 23.5 %all-gather.9.cloned.1.call-start = ((), (), s32[]{:S(2)}) async-start(), calls=%async_computation.2 | async-start | bytes 13271040 | tf_op jit(solution)/shard_map/all_gather | solution.py:66
  7.3 144.1 %all-gather.7.cloned.1.call-start = ((), (), s32[]{:S(2)}) async-start(), calls=%async_computation.1 | async-start | bytes 9031680 | tf_op jit(solution)/shard_map/all_gather | solution.py:33
  24.8 203.0 %all-gather.11.cloned.1.call-start = ((), (), s32[]{:S(2)}) async-start(), calls=%async_computation.3 | async-start | bytes 2580480 | tf_op jit(solution)/shard_map/all_gather | solution.py:12
  173.8 2.7 copy-start
  235.5 2.7 copy-start.1
Sparse Core Ops, SparseCore 0:
  8.9 21.0 all-gather.8
  32.2 119.1 all-gather.6
  178.1 49.6 all-gather.10
where the time goes:
time: 276 us; the launch traced here: 273 us
  waiting for transfers between devices  152 us (55%)
  local copies, waits for them, and re-layouts  39.6 us (14%)
  matrix products  28.9 us (10%)
  blocking collectives  28.8 us (10%)
  between operations  13.2 us (5%)
  other arithmetic  9.53 us (3%)
    all_gather x1, waiting for transfers between devices, project_rows(): return make_adder(flat, lax.all_gather(columns, 'tm', axis=0, tiled=True))  121 us
    all_gather x1, waiting for transfers between devices, entering(): pieces = jax.tree.map(lambda part: lax.all_gather(part, axis), value)  24.9 us
    all_gather x1, blocking collectives, entering(): pieces = jax.tree.map(lambda part: lax.all_gather(part, axis), value)  22.8 us
    dot_general x1, matrix products, make_adder(): return jnp.dot(flat, shard_rows, preferred_element_type=jnp.float32)  22.4 us
    reshape x2, local copies, waits for them, and re-layouts, on_device(): attended.reshape(frame_count, joined_rows, column_count, heads_here * HEAD)  14 us
    unnamed x5, local copies, waits for them, and re-layouts  8.93 us
    select_n x14, other arithmetic, hop(): jnp.where(position < mine, new, old)  7.4 us
    all_to_all x1, blocking collectives, on_device(): lax.all_to_all(attended, 'space', split_axis=1, concat_axis=3, tiled=True)  6.01 us
  transfers between devices with their start and end apart: 3, of which 3 were waited for; matrix products, arithmetic and copies ran while one was open for 7% of the time, Pallas kernels for 0%

commit v1 on v0

v1 whole, which is shorter than its diff:
```python
import functools

import jax
import jax.numpy as jnp
import numpy as np
from jax import lax
from jax.experimental import pallas as pl
from jax.experimental.pallas import tpu as pltpu
from jax.sharding import PartitionSpec as P

HEADS = 10
HEAD = 112
LANES = 128
DEPTH = 256
BF = jnp.bfloat16
F32 = jnp.float32
LIMIT = 44 * 1024 * 1024


def ceil_to(value, step):
    return -(-value // step) * step


def dot(a, b):
    return jnp.dot(a, b, preferred_element_type=F32)


def params():
    return pltpu.CompilerParams(vmem_limit_bytes=LIMIT, dimension_semantics=("arbitrary",))


def cost(flops, moved):
    return pl.CostEstimate(flops=int(flops), bytes_accessed=int(moved), transcendentals=0)


def whole(shape):
    return pl.BlockSpec(shape, lambda i, *_: (0,) * len(shape))


def ring_order(count):
    if count % 2:
        return list(range(count))
    return list(range(0, count, 2)) + list(range(count - 1, 0, -2))


def slot_table(count):
    order = ring_order(count)
    up, down = count // 2, (count - 1) // 2
    table = np.zeros((count, count), np.int32)
    for at, index in enumerate(order):
        slots = [0]
        for step in range(1, up + 1):
            slots.append(-step)
            if step <= down:
                slots.append(step)
        table[index] = [order[(at + s) % count] for s in slots]
    return table


def pack_weight_kernel(meta, w_ref, p_ref, o_ref, qm_ref, qt_ref, rem_ref, *, main, heads_here):
    wide = heads_here * HEAD
    model = HEADS * HEAD
    rows = w_ref.shape[0]
    near = main // 2

    def columns(core):
        def place(ref, value, at):
            ref[:, at : at + value.shape[1]] = value

        k_at, v_at = model + core * wide, 2 * model + core * wide
        if main:
            p_rows = pl.ds(pl.multiple_of(meta[0] * near, near), near)
            o_rows = pl.ds(pl.multiple_of((1 - meta[0]) * near, near), near)
            for ref, take in ((p_ref, p_rows), (o_ref, o_rows)):
                place(ref, w_ref[take, k_at : k_at + wide], 0)
                place(ref, w_ref[take, v_at : v_at + wide], wide)
            qm_ref[...] = w_ref[core * near : (core + 1) * near, :model]
            qt_ref[...] = w_ref[(1 - core) * near : (2 - core) * near, :model]
        rem_ref[...] = jnp.zeros_like(rem_ref)
        place(rem_ref, w_ref[main:rows, k_at : k_at + wide], 0)
        place(rem_ref, w_ref[main:rows, v_at : v_at + wide], wide)
        place(rem_ref, w_ref[main:rows, :model], ceil_to(2 * wide, LANES))

    for core in range(HEADS // heads_here):
        pl.when(meta[1] == core)(functools.partial(columns, core))


def pack_weight(meta, w, main, heads_here):
    rows, wide = w.shape
    model = HEADS * HEAD
    kv = 2 * heads_here * HEAD
    near = max(main // 2, 16)
    shapes = [(near, kv), (near, kv), (near, model), (near, model)]
    shapes.append((rows - main, ceil_to(kv, LANES) + ceil_to(model, LANES)))
    return pl.pallas_call(
        functools.partial(pack_weight_kernel, main=main, heads_here=heads_here),
        grid_spec=pltpu.PrefetchScalarGridSpec(
            num_scalar_prefetch=1,
            grid=(1,),
            in_specs=[whole(w.shape)],
            out_specs=[whole(s) for s in shapes],
        ),
        out_shape=[jax.ShapeDtypeStruct(s, BF) for s in shapes],
        compiler_params=params(),
        cost_estimate=cost(0, 2 * w.size * 2),
        name="pack_weight",
    )(meta, w)


def pack_tokens_kernel(x_ref, o_ref, *, rows, main, count):
    rest = rows - main
    if main:
        for j in range(count):
            o_ref[:, j * main : (j + 1) * main] = x_ref[:, j * rows : j * rows + main]
    if rest:
        at = count * main
        pieces = [x_ref[:, j * rows + main : (j + 1) * rows] for j in range(count)]
        o_ref[:, at : at + count * rest] = jnp.concatenate(pieces, axis=1)


def pack_tokens(x, rows, main, count, block):
    if main == 0:
        return x
    tokens, channels = x.shape
    spec = pl.BlockSpec((block, channels), lambda i: (i, 0))
    return pl.pallas_call(
        functools.partial(pack_tokens_kernel, rows=rows, main=main, count=count),
        grid=(tokens // block,),
        in_specs=[spec],
        out_specs=spec,
        out_shape=jax.ShapeDtypeStruct(x.shape, BF),
        compiler_params=params(),
        cost_estimate=cost(0, 4 * x.size),
        name="pack_tokens",
    )(x)


def fill(weights, meta, which, pieces, main):
    near = main // 2
    first = meta[which]
    for s in range(len(pieces) // 2):
        at = pl.multiple_of(s * main + first * near, near)
        weights[pl.ds(at, near), :] = pieces[2 * s][...]
        at = pl.multiple_of(s * main + (1 - first) * near, near)
        weights[pl.ds(at, near), :] = pieces[2 * s + 1][...]


def project(meta, slots, x_ref, weights, main):
    taken = []
    for s in slots:
        at = pl.multiple_of(meta[2 + s] * main, main)
        taken.append(x_ref[:, pl.ds(at, main)])
    x = taken[0] if len(taken) == 1 else jnp.concatenate(taken, axis=1)
    return dot(x, weights[...])


def early_kernel(meta, x_ref, *refs, slots, main, which):
    pieces, out_ref, weights = refs[:-2], refs[-2], refs[-1]

    @pl.when(pl.program_id(0) == 0)
    def _():
        fill(weights, meta, which, pieces, main)

    out_ref[...] = project(meta, slots, x_ref, weights, main)


def early(meta, x, pieces, slots, main, which, block, name):
    tokens, channels = x.shape
    wide = pieces[0].shape[1]
    return pl.pallas_call(
        functools.partial(early_kernel, slots=slots, main=main, which=which),
        grid_spec=pltpu.PrefetchScalarGridSpec(
            num_scalar_prefetch=1,
            grid=(tokens // block,),
            in_specs=[pl.BlockSpec((block, channels), lambda i, *_: (i, 0))]
            + [whole(p.shape) for p in pieces],
            out_specs=pl.BlockSpec((block, wide), lambda i, *_: (i, 0)),
            scratch_shapes=[pltpu.VMEM((len(slots) * main, wide), BF)],
        ),
        out_shape=jax.ShapeDtypeStruct((tokens, wide), F32),
        compiler_params=params(),
        cost_estimate=cost(2 * tokens * len(slots) * main * wide, tokens * (channels * 2 + wide * 4)),
        name=name,
    )(meta, x, *pieces)


def projected_block(meta, x_ref, rem_ref, acc_ref, weights, slots, main, rest, wide):
    count_main = x_ref.shape[1] - rest
    total = dot(x_ref[:, count_main:], rem_ref[:, :wide])
    if slots:
        total = total + project(meta, slots, x_ref, weights, main)
    if acc_ref is not None:
        total = total + acc_ref[...]
    return total.astype(BF)


def states_kernel(meta, x_ref, rem_ref, prior_ref, *refs, slots, main, rest, has_acc, heads_here):
    acc_ref = refs[0] if has_acc else None
    pieces = refs[has_acc : has_acc + 2 * len(slots)]
    out_ref, weights, values, total = refs[has_acc + 2 * len(slots) :]
    wide = heads_here * HEAD
    step = pl.program_id(0)

    @pl.when(step == 0)
    def _():
        if slots:
            fill(weights, meta, 0, pieces, main)
        values[...] = jnp.ones_like(values)
        total[...] = jnp.zeros_like(total)

    projected = projected_block(meta, x_ref, rem_ref, acc_ref, weights, slots, main, rest, 2 * wide)
    feats = jnp.maximum(projected[:, :wide], 0)
    values[:, :wide] = projected[:, wide:]
    total[...] += lax.dot_general(
        feats, values[...], (((0,), (0,)), ((), ())), preferred_element_type=F32
    )

    @pl.when(step == pl.num_programs(0) - 1)
    def _():
        sums = total[:, wide : wide + LANES - HEAD]
        for h in range(heads_here):
            rows = slice(h * HEAD, (h + 1) * HEAD)
            out_ref[rows, :HEAD] = total[rows, rows] + prior_ref[rows, :HEAD]
        out_ref[:, HEAD:] = sums + prior_ref[:, HEAD:]


def block_states(meta, x, rem, prior, acc, pieces, slots, main, rest, heads_here, block):
    tokens, channels = x.shape
    wide = heads_here * HEAD
    kv = 2 * wide
    room = ceil_to(wide + LANES, 256)
    given = ([acc] if acc is not None else []) + list(pieces)
    specs = [pl.BlockSpec((block, kv), lambda i, *_: (i, 0))] if acc is not None else []
    specs += [whole(p.shape) for p in pieces]
    depth = len(slots) * main + rest
    return pl.pallas_call(
        functools.partial(
            states_kernel,
            slots=slots,
            main=main,
            rest=rest,
            has_acc=int(acc is not None),
            heads_here=heads_here,
        ),
        grid_spec=pltpu.PrefetchScalarGridSpec(
            num_scalar_prefetch=1,
            grid=(tokens // block,),
            in_specs=[
                pl.BlockSpec((block, channels), lambda i, *_: (i, 0)),
                whole((rem.shape[0], ceil_to(kv, LANES))),
                whole(prior.shape),
            ]
            + specs,
            out_specs=whole((wide, LANES)),
            scratch_shapes=[
                pltpu.VMEM((max(len(slots) * main, 16), kv), BF),
                pltpu.VMEM((block, room), BF),
                pltpu.VMEM((wide, room), F32),
            ],
        ),
        out_shape=jax.ShapeDtypeStruct((wide, LANES), F32),
        compiler_params=params(),
        cost_estimate=cost(2 * tokens * (depth * kv + wide * room), tokens * (channels * 2 + kv * 4)),
        name="states",
    )(meta, x, rem, prior, *given)


def bands():
    model = HEADS * HEAD
    found = []
    for left in range(0, model, 256):
        right = min(left + 256, model)
        heads = range(left // HEAD, -(-right // HEAD))
        low = heads[0] * HEAD // LANES * LANES
        high = min(ceil_to((heads[-1] + 1) * HEAD, LANES), model)
        found.append((left, right, low, high, heads))
    return found


def expand_kernel(meta, mine_ref, theirs_ref, s_ref, hi_ref, lo_ref, *, heads_here):
    for ref in (s_ref, hi_ref, lo_ref):
        ref[...] = jnp.zeros_like(ref)
    halves = []
    for half in range(HEADS // heads_here):
        halves.append(jnp.where(meta[1] == half, mine_ref[...], theirs_ref[...]))
    base = 0
    for left, right, low, high, heads in bands():
        for h in heads:
            block = halves[h // heads_here]
            at = (h % heads_here) * HEAD
            states = block[at : at + HEAD, :HEAD]
            sums = jnp.broadcast_to(block[at : at + HEAD, HEAD : HEAD + 1], (HEAD, HEAD))
            high_part = sums.astype(BF)
            low_part = (sums - high_part.astype(F32)).astype(BF)
            begin, end = max(h * HEAD, left), min((h + 1) * HEAD, right)
            rows = slice(base + h * HEAD - low, base + (h + 1) * HEAD - low)
            cols = slice(begin - left, end - left)
            take = slice(begin - h * HEAD, end - h * HEAD)
            s_ref[rows, cols] = states[:, take].astype(BF)
            hi_ref[rows, cols] = high_part[:, take]
            lo_ref[rows, cols] = low_part[:, take]
        base += high - low


def expand(meta, mine, theirs, heads_here):
    rows = sum(high - low for _, _, low, high, _ in bands())
    shape = (rows, 256)
    return pl.pallas_call(
        functools.partial(expand_kernel, heads_here=heads_here),
        grid_spec=pltpu.PrefetchScalarGridSpec(
            num_scalar_prefetch=1,
            grid=(1,),
            in_specs=[whole(mine.shape), whole(theirs.shape)],
            out_specs=[whole(shape)] * 3,
        ),
        out_shape=[jax.ShapeDtypeStruct(shape, BF)] * 3,
        compiler_params=params(),
        cost_estimate=cost(0, 6 * rows * 256),
        name="expand",
    )(meta, mine, theirs)


def attend_kernel(meta, x_ref, rem_ref, s_ref, hi_ref, lo_ref, *refs, slots, main, rest, has_acc):
    acc_ref = refs[0] if has_acc else None
    pieces = refs[has_acc : has_acc + 2 * len(slots)]
    out_ref, weights, queries = refs[has_acc + 2 * len(slots) :]
    model = HEADS * HEAD

    @pl.when(pl.program_id(0) == 0)
    def _():
        if slots:
            fill(weights, meta, 1, pieces, main)

    projected = projected_block(meta, x_ref, rem_ref, acc_ref, weights, slots, main, rest, model)
    queries[...] = jnp.maximum(projected, 0)
    base = 0
    for left, right, low, high, _ in bands():
        rows = slice(base, base + high - low)
        q = queries[:, low:high]
        numerator = dot(q, s_ref[rows, :])
        denominator = dot(q, hi_ref[rows, :]) + dot(q, lo_ref[rows, :]) + 1.0
        out_ref[:, left:right] = (numerator / denominator).astype(BF)[:, : right - left]
        base += high - low


def attend(meta, x, rem, banded, acc, pieces, slots, main, rest, kv_wide, block):
    tokens, channels = x.shape
    model = HEADS * HEAD
    room = ceil_to(model, LANES)
    given = ([acc] if acc is not None else []) + list(pieces)
    specs = [pl.BlockSpec((block, model), lambda i, *_: (i, 0))] if acc is not None else []
    specs += [whole(p.shape) for p in pieces]
    depth = len(slots) * main + rest
    return pl.pallas_call(
        functools.partial(
            attend_kernel, slots=slots, main=main, rest=rest, has_acc=int(acc is not None)
        ),
        grid_spec=pltpu.PrefetchScalarGridSpec(
            num_scalar_prefetch=1,
            grid=(tokens // block,),
            in_specs=[
                pl.BlockSpec((block, channels), lambda i, *_: (i, 0)),
                pl.BlockSpec((rem.shape[0], room), lambda i, *_: (0, ceil_to(kv_wide, LANES) // room)),
            ]
            + [whole(b.shape) for b in banded]
            + specs,
            out_specs=pl.BlockSpec((block, model), lambda i, *_: (i, 0)),
            scratch_shapes=[
                pltpu.VMEM((max(len(slots) * main, 16), model), BF),
                pltpu.VMEM((block, model), BF),
            ],
        ),
        out_shape=jax.ShapeDtypeStruct((tokens, model), BF),
        compiler_params=params(),
        cost_estimate=cost(2 * tokens * model * (depth + 1500), tokens * (channels * 2 + model * 6)),
        name="attend",
    )(meta, x, rem, *banded, *given)


def swap_pairs(count):
    return [(i, i ^ 1) for i in range(count)]


def ring_steps(count):
    order = ring_order(count)
    forward = [(order[i], order[(i + 1) % count]) for i in range(count)]
    return forward, [(b, a) for a, b in forward]


def gather_columns(near, other, count, groups):
    forward, backward = ring_steps(count)
    slots = [(near, other)]
    up_near = down_near = near
    up_other = down_other = other
    for step in range(1, count // 2 + 1):
        down_here = step <= (count - 1) // 2
        up_near = lax.ppermute(up_near, "tm", forward)
        if down_here:
            down_near = lax.ppermute(down_near, "tm", backward)
        if step <= 1:
            up_other = lax.ppermute(up_other, "tm", forward)
        else:
            up_other = lax.ppermute(up_near, "groups", swap_pairs(groups))
        slots.append((up_near, up_other))
        if down_here:
            if step <= 2:
                down_other = lax.ppermute(down_other, "tm", backward)
            else:
                down_other = lax.ppermute(down_near, "groups", swap_pairs(groups))
            slots.append((down_near, down_other))
    return slots


def gather_queries(mine, theirs, count):
    forward, backward = ring_steps(count)
    slots = [(mine, theirs)]
    up = down = mine
    for step in range(1, count // 2 + 1):
        up = lax.ppermute(up, "tm", forward)
        slots.append((up, lax.ppermute(up, "space", swap_pairs(2))))
        if step <= (count - 1) // 2:
            down = lax.ppermute(down, "tm", backward)
            slots.append((down, lax.ppermute(down, "space", swap_pairs(2))))
    return slots


def running_total(value, count):
    reach = 1
    while reach < count:
        pairs = [(i, i + reach) for i in range(count - reach)]
        value = value + lax.ppermute(value, "tm", pairs)
        reach *= 2
    return value


def flat(slots):
    return [part for slot in slots for part in slot]


def on_device(latents, proj_weight):
    frame_count, band_rows, column_count, channels = latents.shape
    rows = proj_weight.shape[0]
    count = lax.axis_size("tm")
    groups = lax.axis_size("groups")
    bands_here = lax.axis_size("space")
    heads_here = HEADS // bands_here
    kv_wide = 2 * heads_here * HEAD
    main = DEPTH if rows >= DEPTH and groups % 2 == 0 else 0
    rest = (rows - main) * count
    tokens = frame_count * band_rows * column_count
    block = 240 if tokens % 240 == 0 else tokens

    here = jnp.asarray(slot_table(count))[lax.axis_index("tm")]
    plane = lax.rem(lax.axis_index("groups"), 2)
    meta = jnp.concatenate([jnp.stack([plane, lax.axis_index("space")]), here]).astype(jnp.int32)

    near, other, q_mine, q_theirs, left_over = pack_weight(meta, proj_weight, main, heads_here)
    rem = lax.all_gather(left_over, "tm", axis=0, tiled=True)
    x = pack_tokens(latents.reshape(tokens, channels), rows, main, count, block)
    x_other = lax.ppermute(x, "space", swap_pairs(bands_here))

    prior = jnp.zeros((heads_here * HEAD, LANES), F32)
    if main:
        kv = gather_columns(near, other, count, groups)
        queries = gather_queries(q_mine, q_theirs, count)
        cut = (5 * count) // 8
        first, last = tuple(range(cut)), tuple(range(cut, count))
        kv_acc = [early(meta, t, flat(kv[:cut]), first, main, 0, block, "kv_early") for t in (x, x_other)]
        q_acc = early(meta, x, flat(queries[:cut]), first, main, 1, block, "q_early")
        kv_late, q_late = flat(kv[cut:]), flat(queries[cut:])
    else:
        kv_acc, q_acc, kv_late, q_late, last = [None, None], None, [], [], ()
    for tok, acc in zip((x, x_other), kv_acc):
        prior = block_states(meta, tok, rem, prior, acc, kv_late, last, main, rest, heads_here, block)
    total = running_total(prior, count)
    total_other = lax.ppermute(total, "space", swap_pairs(bands_here))
    banded = expand(meta, total, total_other, heads_here)
    out = attend(meta, x, rem, banded, q_acc, q_late, last, main, rest, kv_wide, block)
    return out.reshape(frame_count, band_rows, column_count, HEADS * HEAD)


def solution(mesh):
    return jax.shard_map(
        on_device,
        mesh=mesh,
        in_specs=(P(("groups", "tm"), "space", None, None), P("tm", None)),
        out_specs=P(("groups", "tm"), "space", None, None),
        check_vma=False,
    )
```

time: 276 us -> 180 us (0.65)
  the two profiles are of different devices: /device:TPU:27 before, /device:TPU:17 now
where the time goes in v1:
time: 180 us; the launch traced here: 179 us
  starting transfers between devices  52.2 us (29%)
  Pallas kernels  51.3 us (28%)
  waiting for transfers between devices  42.9 us (24%)
  blocking collectives  23.2 us (13%)
  local copies, waits for them, and re-layouts  9.35 us (5%)
    all_gather x1, blocking collectives, on_device(): rem = lax.all_gather(left_over, 'tm', axis=0, tiled=True)  23.2 us
    pallas_call x3, Pallas kernels, early(): pl.pallas_call(functools.partial(early_kernel, slots=slots, main=main, wh...  18.9 us
    pallas_call x2, Pallas kernels, block_states(): pl.pallas_call(functools.partial(states_kernel, slots=slots, main=main, r...  16.9 us
    ppermute x4, waiting for transfers between devices, gather_columns(): up_near = lax.ppermute(up_near, 'tm', forward)  13.3 us
    ppermute x4, starting transfers between devices, gather_queries(): slots.append((up, lax.ppermute(up, 'space', swap_pairs(2))))  12.6 us
    pallas_call x1, Pallas kernels, attend(): pl.pallas_call(functools.partial(attend_kernel, slots=slots, main=main, r...  10 us
    ppermute x3, waiting for transfers between devices, gather_columns(): down_near = lax.ppermute(down_near, 'tm', backward)  9.65 us
    ppermute x3, starting transfers between devices, gather_queries(): slots.append((down, lax.ppermute(down, 'space', swap_pairs(2))))  9.58 us
  transfers between devices with their start and end apart: 33, of which 8 were waited for; matrix products, arithmetic and copies ran while one was open for 1% of the time, Pallas kernels for 21%

profile of v1, /device:TPU:17, one launch (start us, length us, event | category | flops | bytes accessed | tf_op | source)
XLA Modules:
  0.0 179.3 jit_solution(12766878533367751370)
XLA Ops:
  0.0 2.3 %copy-done.3 = bf16[2,6,80,2240]{3,2,1,0:T(8,128)(2,1)S(1)} copy-done((bf16[2,6,80,2240]{3,2,1,0:T(8,128)(2,1)S(1)}, bf16[2,6,80,2240]{3,2,1,0:T(8,128)(2,1)}, u32[]{:S(2)}) %copy-start.3) | copy-done | bytes 4300824
  2.3 3.6 %pack_tokens.1.x_ref = bf16[960,2240]{1,0:T(8,128)(2,1)} custom-call(bf16[960,2240]{1,0:T(8,128)(2,1)S(1)} %bitcast.6), custom_call_target="tpu_custom_call" | custom-call | bytes 8601600 | tf_op jit(solution)/shard_map/pack_tokens/pallas_call | solution.py:126
  5.8 0.7 collective-permute-start
  6.5 0.7 dynamic-slice_bitcast_fusion
  7.3 0.8 pack_weight.1
  8.1 1.3 collective-permute-start.1
  9.6 7.2 %collective-permute-done.1.refs_2_ = bf16[128,1120]{1,0:T(8,128)(2,1)S(1)} collective-permute-done((bf16[128,1120]{1,0:T(8,128)(2,1)S(1)}, bf16[128,1120]{1,0:T(8,128)(2,1)S(1)}, u32[]{:S(2)}, u32[]{:S(2)}) %collective-permute-start.1) | collective-permute-done | bytes 286752 | tf_op jit(solution)/shard_map/ppermute | solution.py:397
  16.8 1.3 collective-permute-start.5
  18.4 6.1 %collective-permute-done.5.refs_6_ = bf16[128,1120]{1,0:T(8,128)(2,1)S(1)} collective-permute-done((bf16[128,1120]{1,0:T(8,128)(2,1)S(1)}, bf16[128,1120]{1,0:T(8,128)(2,1)S(1)}, u32[]{:S(2)}, u32[]{:S(2)}) %collective-permute-start.5) | collective-permute-done | bytes 286752 | tf_op jit(solution)/shard_map/ppermute | solution.py:397
  24.6 1.3 collective-permute-start.9
  25.9 1.2 collective-permute-start.2
  27.1 0.2 collective-permute-start.8
  27.3 4.5 %collective-permute-done.7.refs_8_ = bf16[128,1120]{1,0:T(8,128)(2,1)S(1)} collective-permute-done((bf16[128,1120]{1,0:T(8,128)(2,1)S(1)}, bf16[128,1120]{1,0:T(8,128)(2,1)S(1)}, u32[]{:S(2)}, u32[]{:S(2)}) %collective-permute-start.7) | collective-permute-done | bytes 286752 | tf_op jit(solution)/shard_map/ppermute | solution.py:399
  32.0 1.3 collective-permute-start.13
  33.3 4.4 %collective-permute-done.2.refs_3_ = bf16[128,1120]{1,0:T(8,128)(2,1)S(1)} collective-permute-done((bf16[128,1120]{1,0:T(8,128)(2,1)S(1)}, bf16[128,1120]{1,0:T(8,128)(2,1)S(1)}, u32[]{:S(2)}, u32[]{:S(2)}) %collective-permute-start.2) | collective-permute-done | bytes 286752 | tf_op jit(solution)/shard_map/ppermute | solution.py:401
  37.7 1.2 collective-permute-start.6
  38.9 0.5 collective-permute-start.10
  39.4 5.1 %collective-permute-done.11.refs_3_ = bf16[128,1120]{1,0:T(8,128)(2,1)S(1)} collective-permute-done((bf16[128,1120]{1,0:T(8,128)(2,1)S(1)}, bf16[128,1120]{1,0:T(8,128)(2,1)S(1)}, u32[]{:S(2)}, u32[]{:S(2)}) %collective-permute-start.11) | collective-permute-done | bytes 286752 | tf_op jit(solution)/shard_map/ppermute | solution.py:399
  44.5 1.2 collective-permute-start.12
  45.7 0.3 collective-permute-start.14
  46.0 23.2 %all_gather.3.rem_ref = bf16[192,2304]{1,0:T(8,128)(2,1)S(1)} all-gather(bf16[24,2304]{1,0:T(8,128)(2,1)S(1)} %get-tuple-element.13), channel_id=1, replica_groups=mesh['groups'=2,'tm'=8,'space'=2] {'tm'}, dimensions={0}, use_global_device_ids=true | all-gather | bytes 995328 | tf_op jit(solution)/shard_map/all_gather | solution.py:458
  69.2 2.2 %collective-permute-start.19 = (bf16[128,1120]{1,0:T(8,128)(2,1)S(1)}, bf16[128,1120]{1,0:T(8,128)(2,1)S(1)}, u32[]{:S(2)}, u32[]{:S(2)}) collective-permute-start(bf16[128,1120]{1,0:T(8,128)(2,1)S(1)} %get-tuple-element.19.refs_0_), channel_id=1, source_target_pairs={{0,4},{4,8},{8,12},{12,14},{14,10},{10,6},{6,2},{2,0},{1,5},{5,9},... | collective-permute-start | bytes 860168 | tf_op jit(solution)/shard_map/ppermute | solution.py:419
  71.4 6.3 %kv_early.2.refs_0_ = f32[960,1120]{1,0:T(8,128)S(1)} custom-call(s32[10]{0:T(128)S(1)} %pad_add_fusion.meta, bf16[960,2240]{1,0:T(8,128)(2,1)} %pack_tokens.1.x_ref, bf16[128,1120]{1,0:T(8,128)(2,1)S(1)} %get-tuple-element.14.refs_0_, bf16[128,1120]{1,0:T(8,128)(2,1)S(1)} %get-tuple-element.15.refs_1_, ...), custom_call_target="tpu_custom_call" | custom-call | flops 2752512000 | bytes 8601600 | tf_op jit(solution)/shard_map/kv_early/pallas_call | solution.py:170
  77.7 2.2 %copy-done.1 = f32[960,1120]{1,0:T(8,128)} copy-done((f32[960,1120]{1,0:T(8,128)}, f32[960,1120]{1,0:T(8,128)S(1)}, u32[]{:S(2)}) %copy-start.1) | copy-done | bytes 4300824
  79.9 8.4 %states.2.prior_ref = f32[560,128]{1,0:T(8,128)S(1)} custom-call(s32[10]{0:T(128)S(1)} %pad_add_fusion.meta, bf16[960,2240]{1,0:T(8,128)(2,1)} %pack_tokens.1.x_ref, bf16[192,2304]{1,0:T(8,128)(2,1)S(1)} %all_gather.3.rem_ref, f32[560,128]{1,0:T(8,128)S(1)} %broadcast_in_dim.3.prior_ref, f32[960,1120]{1,0:T(8,128)} %copy-done.1, ...), custom_call_target="tpu_custom_call" | custom-call | flops 2890137600 | bytes 8601600 | tf_op jit(solution)/shard_map/states/pallas_call | solution.py:236
  88.4 6.3 %kv_early.3.refs_0_ = f32[960,1120]{1,0:T(8,128)S(1)} custom-call(s32[10]{0:T(128)S(1)} %pad_add_fusion.meta, bf16[960,2240]{1,0:T(8,128)(2,1)} %collective-permute-done.x_ref, bf16[128,1120]{1,0:T(8,128)(2,1)S(1)} %get-tuple-element.14.refs_0_, bf16[128,1120]{1,0:T(8,128)(2,1)S(1)} %get-tuple-element.15.refs_1_, ...), custom_call_target="tpu_custom_call" | custom-call | flops 2752512000 | bytes 8601600 | tf_op jit(solution)/shard_map/kv_early/pallas_call | solution.py:170
  94.7 2.2 %copy-done = f32[960,1120]{1,0:T(8,128)} copy-done((f32[960,1120]{1,0:T(8,128)}, f32[960,1120]{1,0:T(8,128)S(1)}, u32[]{:S(2)}) %copy-start) | copy-done | bytes 4300824
  96.8 8.4 %states.3 = f32[560,128]{1,0:T(8,128)S(1)} custom-call(s32[10]{0:T(128)S(1)} %pad_add_fusion.meta, bf16[960,2240]{1,0:T(8,128)(2,1)} %collective-permute-done.x_ref, bf16[192,2304]{1,0:T(8,128)(2,1)S(1)} %all_gather.3.rem_ref, f32[560,128]{1,0:T(8,128)S(1)} %states.2.prior_ref, f32[960,1120]{1,0:T(8,128)} %copy-done, ...), custom_call_target="tpu_custom_call" | custom-call | flops 2890137600 | bytes 8601600 | tf_op jit(solution)/shard_map/states/pallas_call | solution.py:236
  105.3 3.2 %collective-permute-start.15 = (f32[560,128]{1,0:T(8,128)S(1)}, f32[560,128]{1,0:T(8,128)S(1)}, u32[]{:S(2)}, u32[]{:S(2)}) collective-permute-start(f32[560,128]{1,0:T(8,128)S(1)} %states.3), channel_id=1, source_target_pairs={{0,2},{2,4},{4,6},{6,8},{8,10},{10,12},{12,14},{1,3},{3,5},{5,7},{... | collective-permute-start | bytes 860168 | tf_op jit(solution)/shard_map/ppermute | solution.py:431
  108.5 1.8 %collective-permute-start.21 = (bf16[128,1120]{1,0:T(8,128)(2,1)S(1)}, bf16[128,1120]{1,0:T(8,128)(2,1)S(1)}, u32[]{:S(2)}, u32[]{:S(2)}) collective-permute-start(bf16[128,1120]{1,0:T(8,128)(2,1)S(1)} %get-tuple-element.19.refs_0_), channel_id=1, source_target_pairs={{4,0},{8,4},{12,8},{14,12},{10,14},{6,10},{2,6},{0,2},{5,1},{9,5},... | collective-permute-start | bytes 860168 | tf_op jit(solution)/shard_map/ppermute | solution.py:422
  110.3 0.4 collective-permute-start.23
  110.7 3.3 %collective-permute-done.15 = f32[560,128]{1,0:T(8,128)S(1)} collective-permute-done((f32[560,128]{1,0:T(8,128)S(1)}, f32[560,128]{1,0:T(8,128)S(1)}, u32[]{:S(2)}, u32[]{:S(2)}) %collective-permute-start.15) | collective-permute-done | bytes 286752 | tf_op jit(solution)/shard_map/ppermute | solution.py:431
  114.0 5.0 %collective-permute-start.16 = (f32[560,128]{1,0:T(8,128)S(1)}, f32[560,128]{1,0:T(8,128)S(1)}, u32[]{:S(2)}, u32[]{:S(2)}) collective-permute-start(f32[560,128]{1,0:T(8,128)S(1)} %add.13), channel_id=1, source_target_pairs={{0,4},{2,6},{4,8},{6,10},{8,12},{10,14},{1,5},{3,7},{5,9},{7,11},{... | collective-permute-start | bytes 860168 | tf_op jit(solution)/shard_map/ppermute | solution.py:431
  119.0 10.4 %collective-permute-start.20 = (bf16[128,1120]{1,0:T(8,128)(2,1)S(1)}, bf16[128,1120]{1,0:T(8,128)(2,1)S(1)}, u32[]{:S(2)}, u32[]{:S(2)}) collective-permute-start(bf16[128,1120]{1,0:T(8,128)(2,1)S(1)} %collective-permute-done.19.refs_2_), channel_id=1, source_target_pairs={{0,1},{1,0},{2,3},{3,2},{4,5},{5,4},{6,7},{7,6},{8,9},{9,8},{10,11... | collective-permute-start | bytes 860168 | tf_op jit(solution)/shard_map/ppermute | solution.py:420
  129.4 0.6 collective-permute-start.25
  130.0 0.8 collective-permute-start.27
  130.9 1.3 collective-permute-start.17
  132.2 5.7 %collective-permute-start.22 = (bf16[128,1120]{1,0:T(8,128)(2,1)S(1)}, bf16[128,1120]{1,0:T(8,128)(2,1)S(1)}, u32[]{:S(2)}, u32[]{:S(2)}) collective-permute-start(bf16[128,1120]{1,0:T(8,128)(2,1)S(1)} %collective-permute-done.21.refs_4_), channel_id=1, source_target_pairs={{0,1},{1,0},{2,3},{3,2},{4,5},{5,4},{6,7},{7,6},{8,9},{9,8},{10,11... | collective-permute-start | bytes 860168 | tf_op jit(solution)/shard_map/ppermute | solution.py:423
  138.0 2.9 %collective-permute-start.29 = (bf16[128,1120]{1,0:T(8,128)(2,1)S(1)}, bf16[128,1120]{1,0:T(8,128)(2,1)S(1)}, u32[]{:S(2)}, u32[]{:S(2)}) collective-permute-start(bf16[128,1120]{1,0:T(8,128)(2,1)S(1)} %collective-permute-done.25.refs_8_), channel_id=1, source_target_pairs={{4,0},{8,4},{12,8},{14,12},{10,14},{6,10},{2,6},{0,2},{5,1},{9,5},... | collective-permute-start | bytes 860168 | tf_op jit(solution)/shard_map/ppermute | solution.py:422
  140.9 4.4 %collective-permute-done.17 = f32[560,128]{1,0:T(8,128)S(1)} collective-permute-done((f32[560,128]{1,0:T(8,128)S(1)}, f32[560,128]{1,0:T(8,128)S(1)}, u32[]{:S(2)}, u32[]{:S(2)}) %collective-permute-start.17) | collective-permute-done | bytes 286752 | tf_op jit(solution)/shard_map/ppermute | solution.py:431
  145.3 3.8 %collective-permute-start.26 = (bf16[128,1120]{1,0:T(8,128)(2,1)S(1)}, bf16[128,1120]{1,0:T(8,128)(2,1)S(1)}, u32[]{:S(2)}, u32[]{:S(2)}) collective-permute-start(bf16[128,1120]{1,0:T(8,128)(2,1)S(1)} %collective-permute-done.25.refs_8_), channel_id=1, source_target_pairs={{0,1},{1,0},{2,3},{3,2},{4,5},{5,4},{6,7},{7,6},{8,9},{9,8},{10,11... | collective-permute-start | bytes 860168 | tf_op jit(solution)/shard_map/ppermute | solution.py:423
  149.3 0.5 collective-permute-start.18
  149.8 7.9 %collective-permute-done.31.refs_5_ = bf16[128,1120]{1,0:T(8,128)(2,1)S(1)} collective-permute-done((bf16[128,1120]{1,0:T(8,128)(2,1)S(1)}, bf16[128,1120]{1,0:T(8,128)(2,1)S(1)}, u32[]{:S(2)}, u32[]{:S(2)}) %collective-permute-start.31) | collective-permute-done | bytes 286752 | tf_op jit(solution)/shard_map/ppermute | solution.py:419
  157.7 2.0 %collective-permute-start.32 = (bf16[128,1120]{1,0:T(8,128)(2,1)S(1)}, bf16[128,1120]{1,0:T(8,128)(2,1)S(1)}, u32[]{:S(2)}, u32[]{:S(2)}) collective-permute-start(bf16[128,1120]{1,0:T(8,128)(2,1)S(1)} %collective-permute-done.31.refs_5_), channel_id=1, source_target_pairs={{0,1},{1,0},{2,3},{3,2},{4,5},{5,4},{6,7},{7,6},{8,9},{9,8},{10,11... | collective-permute-start | bytes 860168 | tf_op jit(solution)/shard_map/ppermute | solution.py:420
  159.8 6.3 %q_early.1.refs_0_ = f32[960,1120]{1,0:T(8,128)S(1)} custom-call(s32[10]{0:T(128)S(1)} %pad_add_fusion.meta, bf16[960,2240]{1,0:T(8,128)(2,1)} %pack_tokens.1.x_ref, bf16[128,1120]{1,0:T(8,128)(2,1)S(1)} %get-tuple-element.19.refs_0_, bf16[128,1120]{1,0:T(8,128)(2,1)S(1)} %get-tuple-element.20.refs_1_, ...), custom_call_target="tpu_custom_call" | custom-call | flops 2752512000 | bytes 8601600 | tf_op jit(solution)/shard_map/q_early/pallas_call | solution.py:170
  166.1 2.1 %copy-done.2 = f32[960,1120]{1,0:T(8,128)} copy-done((f32[960,1120]{1,0:T(8,128)}, f32[960,1120]{1,0:T(8,128)S(1)}, u32[]{:S(2)}) %copy-start.2) | copy-done | bytes 4300824
  168.2 1.1 expand.1
  169.3 10.0 %attend.1 = bf16[960,1120]{1,0:T(8,128)(2,1)} custom-call(s32[10]{0:T(128)S(1)} %pad_add_fusion.meta, bf16[960,2240]{1,0:T(8,128)(2,1)} %pack_tokens.1.x_ref, bf16[192,2304]{1,0:T(8,128)(2,1)S(1)} %all_gather.3.rem_ref, bf16[2112,256]{1,0:T(8,128)(2,1)S(1)} %get-tuple-element.16.s_ref, bf16[2112,256]{1,0:T(8,128)(2,1)S(1)} %get-tuple-element.17.hi_ref, ...), custom_call_target="tpu_custom_call" | custom-call | flops 5289984000 | bytes 10752000 | tf_op jit(solution)/shard_map/attend/pallas_call | solution.py:354
  (44 shorter events, 1.2 us)
Async XLA Ops:
  0.0 2.3 %copy-start.3 = (bf16[2,6,80,2240]{3,2,1,0:T(8,128)(2,1)S(1)}, bf16[2,6,80,2240]{3,2,1,0:T(8,128)(2,1)}, u32[]{:S(2)}) copy-start(bf16[2,6,80,2240]{3,2,1,0:T(8,128)(2,1)} %param.3) | copy-start | bytes 12902404
  2.3 5.0 %copy-start.4 = (bf16[280,3360]{1,0:T(8,128)(2,1)S(1)}, bf16[280,3360]{1,0:T(8,128)(2,1)}, u32[]{:S(2)}) copy-start(bf16[280,3360]{1,0:T(8,128)(2,1)} %w_ref.1) | copy-start | bytes 5644804
  5.8 82.5 %collective-permute-start = (bf16[960,2240]{1,0:T(8,128)(2,1)}, bf16[960,2240]{1,0:T(8,128)(2,1)}, u32[]{:S(2)}, u32[]{:S(2)}) collective-permute-start(bf16[960,2240]{1,0:T(8,128)(2,1)} %pack_tokens.1.x_ref), channel_id=1, source_target_pairs={{0,1},{1,0},{2,3},{3,2},{4,5},{5,4},{6,7},{7,6},{8,9},{9,8},{10,11... | collective-permute-start | bytes 12902408 | tf_op jit(solution)/shard_map/ppermute | solution.py:460
  8.1 8.7 %collective-permute-start.1 = (bf16[128,1120]{1,0:T(8,128)(2,1)S(1)}, bf16[128,1120]{1,0:T(8,128)(2,1)S(1)}, u32[]{:S(2)}, u32[]{:S(2)}) collective-permute-start(bf16[128,1120]{1,0:T(8,128)(2,1)S(1)} %get-tuple-element.14.refs_0_), channel_id=1, source_target_pairs={{0,4},{4,8},{8,12},{12,14},{14,10},{10,6},{6,2},{2,0},{1,5},{5,9},... | collective-permute-start | bytes 860168 | tf_op jit(solution)/shard_map/ppermute | solution.py:397
  9.5 8.8 %collective-permute-start.3 = (bf16[128,1120]{1,0:T(8,128)(2,1)S(1)}, bf16[128,1120]{1,0:T(8,128)(2,1)S(1)}, u32[]{:S(2)}, u32[]{:S(2)}) collective-permute-start(bf16[128,1120]{1,0:T(8,128)(2,1)S(1)} %get-tuple-element.14.refs_0_), channel_id=1, source_target_pairs={{4,0},{8,4},{12,8},{14,12},{10,14},{6,10},{2,6},{0,2},{5,1},{9,5},... | collective-permute-start | bytes 860168 | tf_op jit(solution)/shard_map/ppermute | solution.py:399
  16.8 7.8 %collective-permute-start.5 = (bf16[128,1120]{1,0:T(8,128)(2,1)S(1)}, bf16[128,1120]{1,0:T(8,128)(2,1)S(1)}, u32[]{:S(2)}, u32[]{:S(2)}) collective-permute-start(bf16[128,1120]{1,0:T(8,128)(2,1)S(1)} %collective-permute-done.1.refs_2_), channel_id=1, source_target_pairs={{0,4},{4,8},{8,12},{12,14},{14,10},{10,6},{6,2},{2,0},{1,5},{5,9},... | collective-permute-start | bytes 860168 | tf_op jit(solution)/shard_map/ppermute | solution.py:397
  18.1 9.0 %collective-permute-start.4 = (bf16[128,1120]{1,0:T(8,128)(2,1)S(1)}, bf16[128,1120]{1,0:T(8,128)(2,1)S(1)}, u32[]{:S(2)}, u32[]{:S(2)}) collective-permute-start(bf16[128,1120]{1,0:T(8,128)(2,1)S(1)} %get-tuple-element.15.refs_1_), channel_id=1, source_target_pairs={{4,0},{8,4},{12,8},{14,12},{10,14},{6,10},{2,6},{0,2},{5,1},{9,5},... | collective-permute-start | bytes 860168 | tf_op jit(solution)/shard_map/ppermute | solution.py:407
  18.3 13.6 %collective-permute-start.7 = (bf16[128,1120]{1,0:T(8,128)(2,1)S(1)}, bf16[128,1120]{1,0:T(8,128)(2,1)S(1)}, u32[]{:S(2)}, u32[]{:S(2)}) collective-permute-start(bf16[128,1120]{1,0:T(8,128)(2,1)S(1)} %collective-permute-done.3.refs_4_), channel_id=1, source_target_pairs={{4,0},{8,4},{12,8},{14,12},{10,14},{6,10},{2,6},{0,2},{5,1},{9,5},... | collective-permute-start | bytes 860168 | tf_op jit(solution)/shard_map/ppermute | solution.py:399
  24.6 7.5 %collective-permute-start.9 = (bf16[128,1120]{1,0:T(8,128)(2,1)S(1)}, bf16[128,1120]{1,0:T(8,128)(2,1)S(1)}, u32[]{:S(2)}, u32[]{:S(2)}) collective-permute-start(bf16[128,1120]{1,0:T(8,128)(2,1)S(1)} %collective-permute-done.5.refs_6_), channel_id=1, source_target_pairs={{0,4},{4,8},{8,12},{12,14},{14,10},{10,6},{6,2},{2,0},{1,5},{5,9},... | collective-permute-start | bytes 860168 | tf_op jit(solution)/shard_map/ppermute | solution.py:397
  25.9 11.9 %collective-permute-start.2 = (bf16[128,1120]{1,0:T(8,128)(2,1)S(1)}, bf16[128,1120]{1,0:T(8,128)(2,1)S(1)}, u32[]{:S(2)}, u32[]{:S(2)}) collective-permute-start(bf16[128,1120]{1,0:T(8,128)(2,1)S(1)} %get-tuple-element.15.refs_1_), channel_id=1, source_target_pairs={{0,4},{4,8},{8,12},{12,14},{14,10},{10,6},{6,2},{2,0},{1,5},{5,9},... | collective-permute-start | bytes 860168 | tf_op jit(solution)/shard_map/ppermute | solution.py:401
  27.1 11.8 %collective-permute-start.8 = (bf16[128,1120]{1,0:T(8,128)(2,1)S(1)}, bf16[128,1120]{1,0:T(8,128)(2,1)S(1)}, u32[]{:S(2)}, u32[]{:S(2)}) collective-permute-start(bf16[128,1120]{1,0:T(8,128)(2,1)S(1)} %collective-permute-done.4.refs_5_), channel_id=1, source_target_pairs={{4,0},{8,4},{12,8},{14,12},{10,14},{6,10},{2,6},{0,2},{5,1},{9,5},... | collective-permute-start | bytes 860168 | tf_op jit(solution)/shard_map/ppermute | solution.py:407
  31.9 12.6 %collective-permute-start.11 = (bf16[128,1120]{1,0:T(8,128)(2,1)S(1)}, bf16[128,1120]{1,0:T(8,128)(2,1)S(1)}, u32[]{:S(2)}, u32[]{:S(2)}) collective-permute-start(bf16[128,1120]{1,0:T(8,128)(2,1)S(1)} %collective-permute-done.7.refs_8_), channel_id=1, source_target_pairs={{4,0},{8,4},{12,8},{14,12},{10,14},{6,10},{2,6},{0,2},{5,1},{9,5},... | collective-permute-start | bytes 860168 | tf_op jit(solution)/shard_map/ppermute | solution.py:399
  32.0 13.7 %collective-permute-start.13 = (bf16[128,1120]{1,0:T(8,128)(2,1)S(1)}, bf16[128,1120]{1,0:T(8,128)(2,1)S(1)}, u32[]{:S(2)}, u32[]{:S(2)}) collective-permute-start(bf16[128,1120]{1,0:T(8,128)(2,1)S(1)} %collective-permute-done.9.refs_1_), channel_id=1, source_target_pairs={{0,4},{4,8},{8,12},{12,14},{14,10},{10,6},{6,2},{2,0},{1,5},{5,9},... | collective-permute-start | bytes 860168 | tf_op jit(solution)/shard_map/ppermute | solution.py:397
  37.7 31.5 %collective-permute-start.6 = (bf16[128,1120]{1,0:T(8,128)(2,1)S(1)}, bf16[128,1120]{1,0:T(8,128)(2,1)S(1)}, u32[]{:S(2)}, u32[]{:S(2)}) collective-permute-start(bf16[128,1120]{1,0:T(8,128)(2,1)S(1)} %collective-permute-done.5.refs_6_), channel_id=1, source_target_pairs={{0,16},{16,0},{1,17},{17,1},{2,18},{18,2},{3,19},{19,3},{4,20},{20... | collective-permute-start | bytes 860168 | tf_op jit(solution)/shard_map/ppermute | solution.py:403
  38.9 40.9 %collective-permute-start.10 = (bf16[128,1120]{1,0:T(8,128)(2,1)S(1)}, bf16[128,1120]{1,0:T(8,128)(2,1)S(1)}, u32[]{:S(2)}, u32[]{:S(2)}) collective-permute-start(bf16[128,1120]{1,0:T(8,128)(2,1)S(1)} %collective-permute-done.9.refs_1_), channel_id=1, source_target_pairs={{0,16},{16,0},{1,17},{17,1},{2,18},{18,2},{3,19},{19,3},{4,20},{20... | collective-permute-start | bytes 860168 | tf_op jit(solution)/shard_map/ppermute | solution.py:403
  44.5 35.4 %collective-permute-start.12 = (bf16[128,1120]{1,0:T(8,128)(2,1)S(1)}, bf16[128,1120]{1,0:T(8,128)(2,1)S(1)}, u32[]{:S(2)}, u32[]{:S(2)}) collective-permute-start(bf16[128,1120]{1,0:T(8,128)(2,1)S(1)} %collective-permute-done.11.refs_3_), channel_id=1, source_target_pairs={{0,16},{16,0},{1,17},{17,1},{2,18},{18,2},{3,19},{19,3},{4,20},{20... | collective-permute-start | bytes 860168 | tf_op jit(solution)/shard_map/ppermute | solution.py:409
  45.7 34.2 %collective-permute-start.14 = (bf16[128,1120]{1,0:T(8,128)(2,1)S(1)}, bf16[128,1120]{1,0:T(8,128)(2,1)S(1)}, u32[]{:S(2)}, u32[]{:S(2)}) collective-permute-start(bf16[128,1120]{1,0:T(8,128)(2,1)S(1)} %collective-permute-done.13.refs_5_), channel_id=1, source_target_pairs={{0,16},{16,0},{1,17},{17,1},{2,18},{18,2},{3,19},{19,3},{4,20},{20... | collective-permute-start | bytes 860168 | tf_op jit(solution)/shard_map/ppermute | solution.py:403
  69.2 41.1 %collective-permute-start.19 = (bf16[128,1120]{1,0:T(8,128)(2,1)S(1)}, bf16[128,1120]{1,0:T(8,128)(2,1)S(1)}, u32[]{:S(2)}, u32[]{:S(2)}) collective-permute-start(bf16[128,1120]{1,0:T(8,128)(2,1)S(1)} %get-tuple-element.19.refs_0_), channel_id=1, source_target_pairs={{0,4},{4,8},{8,12},{12,14},{14,10},{10,6},{6,2},{2,0},{1,5},{5,9},... | collective-permute-start | bytes 860168 | tf_op jit(solution)/shard_map/ppermute | solution.py:419
  77.7 2.2 %copy-start.1 = (f32[960,1120]{1,0:T(8,128)}, f32[960,1120]{1,0:T(8,128)S(1)}, u32[]{:S(2)}) copy-start(f32[960,1120]{1,0:T(8,128)S(1)} %kv_early.2.refs_0_) | copy-start | bytes 12902404
  94.7 2.2 %copy-start = (f32[960,1120]{1,0:T(8,128)}, f32[960,1120]{1,0:T(8,128)S(1)}, u32[]{:S(2)}) copy-start(f32[960,1120]{1,0:T(8,128)S(1)} %kv_early.3.refs_0_) | copy-start | bytes 12902404
  105.3 8.7 %collective-permute-start.15 = (f32[560,128]{1,0:T(8,128)S(1)}, f32[560,128]{1,0:T(8,128)S(1)}, u32[]{:S(2)}, u32[]{:S(2)}) collective-permute-start(f32[560,128]{1,0:T(8,128)S(1)} %states.3), channel_id=1, source_target_pairs={{0,2},{2,4},{4,6},{6,8},{8,10},{10,12},{12,14},{1,3},{3,5},{5,7},{... | collective-permute-start | bytes 860168 | tf_op jit(solution)/shard_map/ppermute | solution.py:431
  108.5 20.9 %collective-permute-start.21 = (bf16[128,1120]{1,0:T(8,128)(2,1)S(1)}, bf16[128,1120]{1,0:T(8,128)(2,1)S(1)}, u32[]{:S(2)}, u32[]{:S(2)}) collective-permute-start(bf16[128,1120]{1,0:T(8,128)(2,1)S(1)} %get-tuple-element.19.refs_0_), channel_id=1, source_target_pairs={{4,0},{8,4},{12,8},{14,12},{10,14},{6,10},{2,6},{0,2},{5,1},{9,5},... | collective-permute-start | bytes 860168 | tf_op jit(solution)/shard_map/ppermute | solution.py:422
  110.3 19.7 %collective-permute-start.23 = (bf16[128,1120]{1,0:T(8,128)(2,1)S(1)}, bf16[128,1120]{1,0:T(8,128)(2,1)S(1)}, u32[]{:S(2)}, u32[]{:S(2)}) collective-permute-start(bf16[128,1120]{1,0:T(8,128)(2,1)S(1)} %collective-permute-done.19.refs_2_), channel_id=1, source_target_pairs={{0,4},{4,8},{8,12},{12,14},{14,10},{10,6},{6,2},{2,0},{1,5},{5,9},... | collective-permute-start | bytes 860168 | tf_op jit(solution)/shard_map/ppermute | solution.py:419
  114.0 16.8 %collective-permute-start.16 = (f32[560,128]{1,0:T(8,128)S(1)}, f32[560,128]{1,0:T(8,128)S(1)}, u32[]{:S(2)}, u32[]{:S(2)}) collective-permute-start(f32[560,128]{1,0:T(8,128)S(1)} %add.13), channel_id=1, source_target_pairs={{0,4},{2,6},{4,8},{6,10},{8,12},{10,14},{1,5},{3,7},{5,9},{7,11},{... | collective-permute-start | bytes 860168 | tf_op jit(solution)/shard_map/ppermute | solution.py:431
  119.0 18.9 %collective-permute-start.20 = (bf16[128,1120]{1,0:T(8,128)(2,1)S(1)}, bf16[128,1120]{1,0:T(8,128)(2,1)S(1)}, u32[]{:S(2)}, u32[]{:S(2)}) collective-permute-start(bf16[128,1120]{1,0:T(8,128)(2,1)S(1)} %collective-permute-done.19.refs_2_), channel_id=1, source_target_pairs={{0,1},{1,0},{2,3},{3,2},{4,5},{5,4},{6,7},{7,6},{8,9},{9,8},{10,11... | collective-permute-start | bytes 860168 | tf_op jit(solution)/shard_map/ppermute | solution.py:420
  129.4 8.6 %collective-permute-start.25 = (bf16[128,1120]{1,0:T(8,128)(2,1)S(1)}, bf16[128,1120]{1,0:T(8,128)(2,1)S(1)}, u32[]{:S(2)}, u32[]{:S(2)}) collective-permute-start(bf16[128,1120]{1,0:T(8,128)(2,1)S(1)} %collective-permute-done.21.refs_4_), channel_id=1, source_target_pairs={{4,0},{8,4},{12,8},{14,12},{10,14},{6,10},{2,6},{0,2},{5,1},{9,5},... | collective-permute-start | bytes 860168 | tf_op jit(solution)/shard_map/ppermute | solution.py:422
  130.0 10.9 %collective-permute-start.27 = (bf16[128,1120]{1,0:T(8,128)(2,1)S(1)}, bf16[128,1120]{1,0:T(8,128)(2,1)S(1)}, u32[]{:S(2)}, u32[]{:S(2)}) collective-permute-start(bf16[128,1120]{1,0:T(8,128)(2,1)S(1)} %collective-permute-done.23.refs_6_), channel_id=1, source_target_pairs={{0,4},{4,8},{8,12},{12,14},{14,10},{10,6},{6,2},{2,0},{1,5},{5,9},... | collective-permute-start | bytes 860168 | tf_op jit(solution)/shard_map/ppermute | solution.py:419
  130.9 14.4 %collective-permute-start.17 = (f32[560,128]{1,0:T(8,128)S(1)}, f32[560,128]{1,0:T(8,128)S(1)}, u32[]{:S(2)}, u32[]{:S(2)}) collective-permute-start(f32[560,128]{1,0:T(8,128)S(1)} %add.14), channel_id=1, source_target_pairs={{0,8},{2,10},{4,12},{6,14},{1,9},{3,11},{5,13},{7,15},{16,24},{18,... | collective-permute-start | bytes 860168 | tf_op jit(solution)/shard_map/ppermute | solution.py:431
  132.2 17.0 %collective-permute-start.22 = (bf16[128,1120]{1,0:T(8,128)(2,1)S(1)}, bf16[128,1120]{1,0:T(8,128)(2,1)S(1)}, u32[]{:S(2)}, u32[]{:S(2)}) collective-permute-start(bf16[128,1120]{1,0:T(8,128)(2,1)S(1)} %collective-permute-done.21.refs_4_), channel_id=1, source_target_pairs={{0,1},{1,0},{2,3},{3,2},{4,5},{5,4},{6,7},{7,6},{8,9},{9,8},{10,11... | collective-permute-start | bytes 860168 | tf_op jit(solution)/shard_map/ppermute | solution.py:423
  137.9 11.4 %collective-permute-start.24 = (bf16[128,1120]{1,0:T(8,128)(2,1)S(1)}, bf16[128,1120]{1,0:T(8,128)(2,1)S(1)}, u32[]{:S(2)}, u32[]{:S(2)}) collective-permute-start(bf16[128,1120]{1,0:T(8,128)(2,1)S(1)} %collective-permute-done.23.refs_6_), channel_id=1, source_target_pairs={{0,1},{1,0},{2,3},{3,2},{4,5},{5,4},{6,7},{7,6},{8,9},{9,8},{10,11... | collective-permute-start | bytes 860168 | tf_op jit(solution)/shard_map/ppermute | solution.py:420
  138.0 11.8 %collective-permute-start.29 = (bf16[128,1120]{1,0:T(8,128)(2,1)S(1)}, bf16[128,1120]{1,0:T(8,128)(2,1)S(1)}, u32[]{:S(2)}, u32[]{:S(2)}) collective-permute-start(bf16[128,1120]{1,0:T(8,128)(2,1)S(1)} %collective-permute-done.25.refs_8_), channel_id=1, source_target_pairs={{4,0},{8,4},{12,8},{14,12},{10,14},{6,10},{2,6},{0,2},{5,1},{9,5},... | collective-permute-start | bytes 860168 | tf_op jit(solution)/shard_map/ppermute | solution.py:422
  140.9 16.8 %collective-permute-start.31 = (bf16[128,1120]{1,0:T(8,128)(2,1)S(1)}, bf16[128,1120]{1,0:T(8,128)(2,1)S(1)}, u32[]{:S(2)}, u32[]{:S(2)}) collective-permute-start(bf16[128,1120]{1,0:T(8,128)(2,1)S(1)} %collective-permute-done.27.refs_1_), channel_id=1, source_target_pairs={{0,4},{4,8},{8,12},{12,14},{14,10},{10,6},{6,2},{2,0},{1,5},{5,9},... | collective-permute-start | bytes 860168 | tf_op jit(solution)/shard_map/ppermute | solution.py:419
  145.3 14.5 %collective-permute-start.26 = (bf16[128,1120]{1,0:T(8,128)(2,1)S(1)}, bf16[128,1120]{1,0:T(8,128)(2,1)S(1)}, u32[]{:S(2)}, u32[]{:S(2)}) collective-permute-start(bf16[128,1120]{1,0:T(8,128)(2,1)S(1)} %collective-permute-done.25.refs_8_), channel_id=1, source_target_pairs={{0,1},{1,0},{2,3},{3,2},{4,5},{5,4},{6,7},{7,6},{8,9},{9,8},{10,11... | collective-permute-start | bytes 860168 | tf_op jit(solution)/shard_map/ppermute | solution.py:423
  149.2 20.1 %collective-permute-start.28 = (bf16[128,1120]{1,0:T(8,128)(2,1)S(1)}, bf16[128,1120]{1,0:T(8,128)(2,1)S(1)}, u32[]{:S(2)}, u32[]{:S(2)}) collective-permute-start(bf16[128,1120]{1,0:T(8,128)(2,1)S(1)} %collective-permute-done.27.refs_1_), channel_id=1, source_target_pairs={{0,1},{1,0},{2,3},{3,2},{4,5},{5,4},{6,7},{7,6},{8,9},{9,8},{10,11... | collective-permute-start | bytes 860168 | tf_op jit(solution)/shard_map/ppermute | solution.py:420
  149.3 18.9 %collective-permute-start.18 = (f32[560,128]{1,0:T(8,128)S(1)}, f32[560,128]{1,0:T(8,128)S(1)}, u32[]{:S(2)}, u32[]{:S(2)}) collective-permute-start(f32[560,128]{1,0:T(8,128)S(1)} %add.15.mine_ref), channel_id=1, source_target_pairs={{0,1},{1,0},{2,3},{3,2},{4,5},{5,4},{6,7},{7,6},{8,9},{9,8},{10,11... | collective-permute-start | bytes 860168 | tf_op jit(solution)/shard_map/ppermute | solution.py:476
  149.8 19.5 %collective-permute-start.30 = (bf16[128,1120]{1,0:T(8,128)(2,1)S(1)}, bf16[128,1120]{1,0:T(8,128)(2,1)S(1)}, u32[]{:S(2)}, u32[]{:S(2)}) collective-permute-start(bf16[128,1120]{1,0:T(8,128)(2,1)S(1)} %collective-permute-done.29.refs_3_), channel_id=1, source_target_pairs={{0,1},{1,0},{2,3},{3,2},{4,5},{5,4},{6,7},{7,6},{8,9},{9,8},{10,11... | collective-permute-start | bytes 860168 | tf_op jit(solution)/shard_map/ppermute | solution.py:423
  157.7 11.5 %collective-permute-start.32 = (bf16[128,1120]{1,0:T(8,128)(2,1)S(1)}, bf16[128,1120]{1,0:T(8,128)(2,1)S(1)}, u32[]{:S(2)}, u32[]{:S(2)}) collective-permute-start(bf16[128,1120]{1,0:T(8,128)(2,1)S(1)} %collective-permute-done.31.refs_5_), channel_id=1, source_target_pairs={{0,1},{1,0},{2,3},{3,2},{4,5},{5,4},{6,7},{7,6},{8,9},{9,8},{10,11... | collective-permute-start | bytes 860168 | tf_op jit(solution)/shard_map/ppermute | solution.py:420
  166.1 2.1 %copy-start.2 = (f32[960,1120]{1,0:T(8,128)}, f32[960,1120]{1,0:T(8,128)S(1)}, u32[]{:S(2)}) copy-start(f32[960,1120]{1,0:T(8,128)S(1)} %q_early.1.refs_0_) | copy-start | bytes 12902404

commit v2 on v0

v2 whole, which is shorter than its diff:
```python
import functools

import jax
import jax.numpy as jnp
import numpy as np
from jax import lax
from jax.experimental import pallas as pl
from jax.experimental.pallas import tpu as pltpu
from jax.sharding import PartitionSpec as P

HEADS = 10
HEAD = 112
LANES = 128
DEPTH = 256
BF = jnp.bfloat16
F32 = jnp.float32
LIMIT = 16 * 1024 * 1024


def ceil_to(value, step):
    return -(-value // step) * step


def dot(a, b):
    return jnp.dot(a, b, preferred_element_type=F32)


def params():
    return pltpu.CompilerParams(vmem_limit_bytes=LIMIT, dimension_semantics=("arbitrary",))


def cost(flops, moved):
    return pl.CostEstimate(flops=int(flops), bytes_accessed=int(moved), transcendentals=0)


def whole(shape):
    return pl.BlockSpec(shape, lambda i, *_: (0,) * len(shape))


def ring_order(count):
    if count % 2:
        return list(range(count))
    return list(range(0, count, 2)) + list(range(count - 1, 0, -2))


def slot_table(count):
    order = ring_order(count)
    up, down = count // 2, (count - 1) // 2
    table = np.zeros((count, count), np.int32)
    for at, index in enumerate(order):
        slots = [0]
        for step in range(1, up + 1):
            slots.append(-step)
            if step <= down:
                slots.append(step)
        table[index] = [order[(at + s) % count] for s in slots]
    return table


def split_rows(rows):
    third = ceil_to(DEPTH // 3, 16)
    spare = ceil_to((rows - DEPTH + 1) // 2, 16)
    return third, DEPTH - 2 * third, spare


def resident(kernel, meta, operands, outs, scratch, flops, name, aliases=None):
    in_vmem = pl.BlockSpec(memory_space=pltpu.VMEM)
    return pl.pallas_call(
        kernel,
        in_specs=[pl.BlockSpec(memory_space=pltpu.SMEM)] + [in_vmem] * len(operands),
        out_specs=[in_vmem] * len(outs),
        out_shape=outs,
        scratch_shapes=scratch,
        input_output_aliases=aliases or {},
        compiler_params=pltpu.CompilerParams(vmem_limit_bytes=LIMIT),
        cost_estimate=cost(flops, 0),
        name=name,
    )(meta, *operands)


def key_value_columns(meta, heads_here, run):
    wide, model = heads_here * HEAD, HEADS * HEAD

    def on_core(core):
        for part in (1, 2):
            begin = part * model + core * wide
            run(slice(begin, begin + wide), slice((part - 1) * wide, part * wide))

    for core in range(HEADS // heads_here):
        pl.when(meta[1] == core)(functools.partial(on_core, core))


def pack_first_kernel(meta, w_ref, out_ref, *, heads_here):
    rows = w_ref.shape[0]
    third, shared, _ = split_rows(rows)
    own_rows = pl.ds(pl.multiple_of(meta[0] * third, 16), third)
    filled = third + shared + rows - DEPTH
    out_ref[third + shared :, :] = jnp.zeros((out_ref.shape[0] - third - shared, out_ref.shape[1]), BF)

    def run(of, to):
        out_ref[:third, to] = w_ref[own_rows, of]
        out_ref[third : third + shared, to] = w_ref[2 * third : DEPTH, of]
        out_ref[third + shared : filled, to] = w_ref[DEPTH:, of]

    key_value_columns(meta, heads_here, run)


def pack_rest_kernel(meta, w_ref, after_ref, other_ref, mine_ref, theirs_ref, *, heads_here):
    rows = w_ref.shape[0]
    third, _, spare = split_rows(rows)
    half, model = DEPTH // 2, HEADS * HEAD
    other_rows = pl.ds(pl.multiple_of((1 - meta[0]) * third, 16), third)

    def run(of, to):
        other_ref[:, to] = w_ref[other_rows, of]

    key_value_columns(meta, heads_here, run)

    def queries(out_ref, core):
        out_ref[:half, :] = w_ref[core * half : (core + 1) * half, :model]
        out_ref[half:, :] = jnp.zeros((spare, model), BF)
        begin = DEPTH + core * spare
        count = min(spare, rows - begin)
        out_ref[half : half + count, :] = w_ref[begin : begin + count, :model]

    for core in range(2):
        pl.when(meta[1] == core)(functools.partial(queries, mine_ref, core))
        pl.when(meta[1] == 1 - core)(functools.partial(queries, theirs_ref, core))


def pack_first(meta, w, heads_here):
    third, shared, spare = split_rows(w.shape[0])
    wide = 2 * heads_here * HEAD
    out = jax.ShapeDtypeStruct((third + shared + 2 * spare, wide), BF)
    kernel = functools.partial(pack_first_kernel, heads_here=heads_here)
    return resident(kernel, meta, [w], [out], [], 1e9, "pack_first")[0]


def pack_rest(meta, w, after, heads_here):
    third, _, spare = split_rows(w.shape[0])
    half = DEPTH // 2 + spare
    outs = [jax.ShapeDtypeStruct((third, 2 * heads_here * HEAD), BF)]
    outs += [jax.ShapeDtypeStruct((half, HEADS * HEAD), BF)] * 2
    kernel = functools.partial(pack_rest_kernel, heads_here=heads_here)
    return resident(kernel, meta, [w, after], outs, [], 1e9, "pack_rest")


def pack_tokens_kernel(x_ref, after_ref, o_ref, *, rows, count):
    spare = split_rows(rows)[2]
    rest = rows - DEPTH
    blank = jnp.zeros((x_ref.shape[0], 2 * spare - rest), x_ref.dtype)
    left_over = []
    for j in range(count):
        at = j * rows
        o_ref[:, j * DEPTH : (j + 1) * DEPTH] = x_ref[:, at : at + DEPTH]
        left_over += [x_ref[:, at + DEPTH : at + rows], blank]
    o_ref[:, count * DEPTH :] = jnp.concatenate(left_over, axis=1)


def pack_tokens(x, after, rows, count, block):
    tokens, channels = x.shape
    depth = count * (DEPTH + 2 * split_rows(rows)[2])
    return pl.pallas_call(
        functools.partial(pack_tokens_kernel, rows=rows, count=count),
        grid=(tokens // block,),
        in_specs=[
            pl.BlockSpec((block, channels), lambda i: (i, 0)),
            pl.BlockSpec(memory_space=pl.ANY),
        ],
        out_specs=pl.BlockSpec((block, depth), lambda i: (i, 0)),
        out_shape=jax.ShapeDtypeStruct((tokens, depth), BF),
        compiler_params=params(),
        cost_estimate=cost(0, 4 * x.size),
        name="pack_tokens",
    )(x, after)


def put(weights, at, step, value):
    weights[pl.ds(pl.multiple_of(at, step), value.shape[0]), :] = value


def fill_keys_values(weights, meta, slots, pieces, rows):
    third, shared, spare = split_rows(rows)
    for s in range(len(slots)):
        own, other, common = pieces[3 * s : 3 * s + 3]
        put(weights, s * DEPTH + meta[0] * third, 16, own[:third, :])
        put(weights, s * DEPTH + (1 - meta[0]) * third, 16, other[...])
        at = common.shape[0] - shared - 2 * spare
        weights[s * DEPTH + 2 * third : (s + 1) * DEPTH, :] = common[at : at + shared, :]


def fill_queries(weights, meta, slots, pieces, rows):
    half = DEPTH // 2
    for s in range(len(slots)):
        mine, theirs = pieces[2 * s : 2 * s + 2]
        put(weights, s * DEPTH + meta[1] * half, 16, mine[:half, :])
        put(weights, s * DEPTH + (1 - meta[1]) * half, 16, theirs[:half, :])


def fill_left_over(weights, meta, base, pieces, rows, of_keys):
    spare = split_rows(rows)[2]
    if of_keys:
        for s, common in enumerate(pieces):
            put(weights, base + meta[2 + s] * 2 * spare, 16, common[common.shape[0] - 2 * spare :, :])
        return
    for s in range(len(pieces) // 2):
        at = base + meta[2 + s] * 2 * spare
        put(weights, at + meta[1] * spare, 16, pieces[2 * s][DEPTH // 2 :, :])
        put(weights, at + (1 - meta[1]) * spare, 16, pieces[2 * s + 1][DEPTH // 2 :, :])


def token_columns(x_ref, rows, meta, slots, count, with_rest):
    taken = [x_ref[rows, pl.ds(pl.multiple_of(meta[2 + s] * DEPTH, DEPTH), DEPTH)] for s in slots]
    if with_rest:
        taken.append(x_ref[rows, count * DEPTH :])
    return jnp.concatenate(taken, axis=1)


def every_block(xs, block, run):
    tokens = xs[0].shape[0]
    for band, x_ref in enumerate(xs):

        def step(i, carry, band=band, x_ref=x_ref):
            at = pl.multiple_of(i * block, block)
            run(x_ref, pl.ds(at, block), pl.ds(pl.multiple_of(at + band * tokens, block), block))
            return carry

        lax.fori_loop(0, tokens // block, step, 0)


def project_kernel(meta, *refs, plan, finish):
    bands_in, slots, count, rows, of_keys, has_acc, with_rest, block = plan
    xs, refs = refs[:bands_in], refs[bands_in:]
    acc_ref, refs = (refs[0], refs[1:]) if has_acc else (None, refs)
    many = (3 if of_keys else 2) * len(slots)
    pieces, refs = refs[:many], refs[many:]
    lasts = (1 if of_keys else 2) * count if with_rest else 0
    rest_pieces, refs = refs[:lasts], refs[lasts:]
    weights, refs = refs[-1], refs[:-1]
    (fill_keys_values if of_keys else fill_queries)(weights, meta, slots, pieces, rows)
    if with_rest:
        fill_left_over(weights, meta, len(slots) * DEPTH, rest_pieces, rows, of_keys)

    def run(x_ref, rows_here, rows_of_all):
        x = token_columns(x_ref, rows_here, meta, slots, count, with_rest)
        total = dot(x, weights[...])
        if has_acc:
            total = total + acc_ref[rows_of_all, :]
        finish(refs, total, rows_of_all)

    every_block(xs, block, run)


def keep(refs, total, rows):
    refs[0][rows, :] = total


def keep_features(refs, total, rows):
    refs[0][rows, :] = jnp.maximum(total.astype(BF), 0)


def project(meta, xs, acc, pieces, rest_pieces, plan, finish, outs, scratch, more_flops, name):
    bands_in, slots, count, rows, of_keys, has_acc, with_rest, block = plan
    wide = pieces[0].shape[1]
    depth = len(slots) * DEPTH + with_rest * count * 2 * split_rows(rows)[2]
    tokens = bands_in * xs[0].shape[0]
    operands = [*xs, *([acc] if has_acc else []), *pieces, *rest_pieces]
    return resident(
        functools.partial(project_kernel, plan=plan, finish=finish),
        meta,
        operands,
        outs,
        [*scratch, pltpu.VMEM((depth, wide), BF)],
        2 * tokens * depth * wide + more_flops,
        name,
        {1 + bands_in: 0} if has_acc and outs[0].shape == acc.shape and outs[0].dtype == acc.dtype else None,
    )[0]


def states_kernel(meta, *refs, plan, heads_here):
    out_ref, values, total, weights = refs[-4:]
    wide = heads_here * HEAD
    values[...] = jnp.ones_like(values)
    total[...] = jnp.zeros_like(total)

    def finish(_, projected, rows):
        projected = projected.astype(BF)
        feats = jnp.maximum(projected[:, :wide], 0)
        values[:, :wide] = projected[:, wide:]
        total[...] += lax.dot_general(
            feats, values[...], (((0,), (0,)), ((), ())), preferred_element_type=F32
        )

    project_kernel(meta, *refs, plan=plan, finish=finish)
    for h in range(heads_here):
        rows = slice(h * HEAD, (h + 1) * HEAD)
        out_ref[rows, :HEAD] = total[rows, rows]
    out_ref[:, HEAD:] = total[:, wide : wide + LANES - HEAD]


def block_states(meta, xs, acc, pieces, rest_pieces, plan, heads_here):
    wide = heads_here * HEAD
    room = ceil_to(wide + LANES, 256)
    bands_in, slots, count, rows, _, has_acc, with_rest, block = plan
    depth = len(slots) * DEPTH + with_rest * count * 2 * split_rows(rows)[2]
    tokens = bands_in * xs[0].shape[0]
    operands = [*xs, acc, *pieces, *rest_pieces]
    return resident(
        functools.partial(states_kernel, plan=plan, heads_here=heads_here),
        meta,
        operands,
        [jax.ShapeDtypeStruct((wide, LANES), F32)],
        [
            pltpu.VMEM((block, room), BF),
            pltpu.VMEM((wide, room), F32),
            pltpu.VMEM((depth, 2 * wide), BF),
        ],
        2 * tokens * (depth * 2 * wide + wide * room),
        "states",
    )[0]


def bands():
    model = HEADS * HEAD
    found = []
    for left in range(0, model, 256):
        right = min(left + 256, model)
        heads = range(left // HEAD, -(-right // HEAD))
        low = heads[0] * HEAD // LANES * LANES
        high = min(ceil_to((heads[-1] + 1) * HEAD, LANES), model)
        found.append((left, right, low, high, heads))
    return found


def attend_kernel(meta, q_ref, mine_ref, theirs_ref, out_ref, states, sums, spread, *, heads_here):
    @pl.when(pl.program_id(0) == 0)
    def _():
        states[...] = jnp.zeros_like(states)
        sums[...] = jnp.zeros_like(sums)
        mine, theirs = mine_ref[...], theirs_ref[...]
        parts = [jnp.where(meta[1] == k, mine, theirs) for k in range(HEADS // heads_here)]
        base = 0
        for left, right, low, high, heads in bands():
            for h in heads:
                at = (h % heads_here) * HEAD
                begin, end = max(h * HEAD, left), min((h + 1) * HEAD, right)
                rows = slice(base + h * HEAD - low, base + (h + 1) * HEAD - low)
                block = parts[h // heads_here][at : at + HEAD, begin - h * HEAD : end - h * HEAD]
                states[rows, begin - left : end - left] = block.astype(BF)
            base += high - low
        lane = lax.broadcasted_iota(jnp.int32, (HEAD, LANES), 1)
        for h in range(HEADS):
            at = (h % heads_here) * HEAD
            key_sums = parts[h // heads_here][at : at + HEAD, HEAD : HEAD + 1]
            key_sums = jnp.broadcast_to(key_sums, (HEAD, LANES))
            upper = key_sums.astype(BF).astype(F32)
            chosen = jnp.where(lane == h, upper, jnp.where(lane == h + 64, key_sums - upper, 0.0))
            sums[h * HEAD : (h + 1) * HEAD, :] = chosen.astype(BF)
        head = lax.broadcasted_iota(jnp.int32, spread.shape, 0) % 64 * HEAD
        column = lax.broadcasted_iota(jnp.int32, spread.shape, 1)
        spread[...] = jnp.where((column >= head) & (column < head + HEAD), 1.0, 0.0).astype(BF)

    rows_here = pl.ds(pl.multiple_of(pl.program_id(0) * out_ref.shape[0], 16), out_ref.shape[0])
    total = dot(q_ref[rows_here, :], sums[...])
    low_lane = lax.broadcasted_iota(jnp.int32, total.shape, 1) >= 64
    denominator = total + pltpu.roll(total, 64, 1) + 1.0
    share = 1.0 / denominator
    upper = share.astype(BF).astype(F32)
    share = jnp.where(low_lane, share - upper, upper).astype(BF)
    base = 0
    for left, right, low, high, _ in bands():
        numerator = dot(q_ref[rows_here, low:high], states[base : base + high - low, :])
        scale = dot(share, spread[:, left : left + 256])
        out_ref[:, left:right] = (numerator * scale).astype(BF)[:, : right - left]
        base += high - low


def attend(meta, queries, mine, theirs, heads_here, block):
    tokens, model = queries.shape
    rows = sum(high - low for _, _, low, high, _ in bands())
    spec = pl.BlockSpec((block, model), lambda i, *_: (i, 0))
    return pl.pallas_call(
        functools.partial(attend_kernel, heads_here=heads_here),
        grid_spec=pltpu.PrefetchScalarGridSpec(
            num_scalar_prefetch=1,
            grid=(tokens // block,),
            in_specs=[pl.BlockSpec(memory_space=pltpu.VMEM)] * 3,
            out_specs=spec,
            scratch_shapes=[
                pltpu.VMEM((rows, 256), BF),
                pltpu.VMEM((model, LANES), BF),
                pltpu.VMEM((LANES, ceil_to(model, 256)), BF),
            ],
        ),
        out_shape=jax.ShapeDtypeStruct((tokens, model), BF),
        compiler_params=params(),
        cost_estimate=cost(2 * tokens * model * 800, tokens * model * 4),
        name="attend",
    )(meta, queries, mine, theirs)


def swap_pairs(count):
    return [(i, i ^ 1) for i in range(count)]


def ring_steps(count):
    order = ring_order(count)
    forward = [(order[i], order[(i + 1) % count]) for i in range(count)]
    return forward, [(b, a) for a, b in forward]


def running_total(states, sums, count, alongside=None):
    reach, hop = 1, 0
    wide, room = states.shape[-1], sums.shape[-1]
    while reach < count:
        pairs = [(i, i + reach) for i in range(count - reach)]
        upper = sums.astype(BF)
        lower = (sums - upper.astype(F32)).astype(BF)
        sent = jnp.concatenate([states.astype(BF), upper, lower], axis=-1)
        got = lax.ppermute(sent, "tm", pairs)
        if alongside is not None:
            got = alongside(hop, got)
        got = got.astype(F32)
        states = states + got[..., :wide]
        sums = sums + (got[..., wide : wide + room] + got[..., wide + room :])
        reach, hop = reach * 2, hop + 1
    return states, sums


def tie(*values):
    return lax.optimization_barrier(values)


def ring_form(latents, proj_weight):
    frame_count, band_rows, column_count, channels = latents.shape
    rows = proj_weight.shape[0]
    third = split_rows(rows)[0]
    count, groups = lax.axis_size("tm"), lax.axis_size("groups")
    heads_here = HEADS // 2
    tokens = frame_count * band_rows * column_count
    block = 480 if tokens % 480 == 0 else tokens

    forward, backward = ring_steps(count)
    across, over = swap_pairs(groups), swap_pairs(2)
    up_last, down_last = count // 2, (count - 1) // 2

    def ring(value, up):
        return lax.ppermute(value, "tm", forward if up else backward)

    def plane_swap(value):
        return lax.ppermute(value[:third], "groups", across)

    def core_swap(value):
        return lax.ppermute(value, "space", over)

    here = jnp.asarray(slot_table(count))[lax.axis_index("tm")]
    plane = lax.rem(lax.axis_index("groups"), 2)
    meta = jnp.concatenate([jnp.stack([plane, lax.axis_index("space")]), here]).astype(jnp.int32)

    own = pack_first(meta, proj_weight, heads_here)
    other, mine, theirs = pack_rest(meta, proj_weight, own, heads_here)
    x = pack_tokens(latents.reshape(tokens, channels), mine, rows, count, block)

    queries_up, queries_down = [mine], [mine]

    def next_queries():
        if len(queries_up) <= up_last - (up_last > down_last):
            queries_up.append(ring(queries_up[-1], True))
        if len(queries_down) <= up_last:
            queries_down.append(ring(queries_down[-1], False))

    def with_queries(*values):
        *values, queries_up[-1], queries_down[-1] = tie(*values, queries_up[-1], queries_down[-1])
        next_queries()
        return values

    def plan(bands_in, which, of_keys, has_acc, with_rest):
        return (bands_in, tuple(which), count, rows, of_keys, has_acc, with_rest, block)

    kv_shape = jax.ShapeDtypeStruct((2 * tokens, 2 * heads_here * HEAD), F32)

    def add_keys_values(acc, which):
        pieces = [part for s in which for part in slots[s]]
        settings = plan(2, which, True, acc is not None, False)
        return project(meta, both, acc, pieces, [], settings, keep, [kv_shape], [], 0, "kv_part")

    slots = [[own, other, own]]
    up = down = own
    swapping, acc = [], None
    for step in range(1, up_last + 1):
        full = step <= down_last
        up = ring(up if full else up[:third], True)
        down = ring(down if full else down[third:], False)
        if step == 1:
            x = tie(x, up, down)[0]
            x_other = core_swap(x)
            both = (x, x_other)
        elif step == up_last:
            acc = add_keys_values(None, range(len(slots) - 2))
            acc, up, down, *swapping = with_queries(acc, up, down, *swapping)
        else:
            x_other, up, down, *swapping = tie(x_other, up, down, *swapping)
            both = (x, x_other)
        if swapping:
            slots[-2][1], slots[-1][1] = swapping
        swapping = [plane_swap(up)] + ([plane_swap(down)] if full else [])
        if full:
            slots += [[up, swapping[0], up], [down, swapping[1], down]]
        else:
            slots += [[up, swapping[0], down]]
        if step + 1 == up_last:
            next_queries()
    final = range(len(slots) - len(swapping), len(slots))
    acc = add_keys_values(acc, range(final[0] - 2, final[0]))
    acc, *swapping = with_queries(acc, *swapping)
    for s, value in zip(final, swapping):
        slots[s][1] = value

    pieces = [part for s in final for part in slots[s]]
    commons = [slot[2] for slot in slots]
    payload = block_states(meta, both, acc, pieces, commons, plan(2, final, True, True, True), heads_here)
    (payload,) = with_queries(payload)

    found = [[mine, theirs]]
    cut = (5 * count) // 8

    def query_slots(step):
        for way in (queries_up, queries_down):
            if step < len(way):
                found.append([way[step], core_swap(way[step])])

    def project_queries(acc, which, finish, dtype, name):
        last = which[-1] == count - 1
        pieces = [part for s in which for part in found[s]]
        every = [part for s in found for part in s] if last else []
        settings = plan(1, which, False, acc is not None, last)
        out = jax.ShapeDtypeStruct((tokens, HEADS * HEAD), dtype)
        return project(meta, (x,), acc, pieces, every, settings, finish, [out], [], 0, name)

    held = {}

    def alongside(hop, got):
        if hop == 0:
            query_slots(1)
            query_slots(2)
            (got,) = with_queries(got)
        if hop == 1:
            early = project_queries(None, range(cut), keep, F32, "q_early")
            for step in range(3, up_last + 1):
                query_slots(step)
            got, held["q"] = tie(got, early)
        if hop == 2:
            late = project_queries(held["q"], range(cut, count), keep_features, BF, "q_late")
            got, held["q"] = tie(got, late)
        return got

    states, sums = payload[:, :HEAD], payload[:, HEAD : HEAD + 8]
    total = jnp.concatenate([*running_total(states, sums, count, alongside), sums], axis=1)
    out = attend(meta, held["q"], total, core_swap(total), heads_here, block)
    return out.reshape(frame_count, band_rows, column_count, HEADS * HEAD)


def gathered_form(latents, proj_weight):
    frame_count, band_rows, column_count, channels = latents.shape
    shard_rows = proj_weight.shape[0]
    band_count, band = lax.axis_size("space"), lax.axis_index("space")
    heads_here = HEADS // band_count
    own = proj_weight.reshape(shard_rows, 3, band_count, heads_here * HEAD)
    own = lax.dynamic_index_in_dim(own, band, 2, keepdims=False)
    own = own.reshape(shard_rows, 3 * heads_here * HEAD)
    weight = lax.all_gather(own, "tm", axis=0, tiled=True)
    tokens = lax.all_gather(latents, "space", axis=1, tiled=True)
    joined = tokens.shape[1]
    projected = dot(tokens.reshape(-1, channels), weight).astype(BF)
    split = projected.reshape(-1, 3, heads_here, HEAD)
    queries, feats, values = jax.nn.relu(split[:, 0]), jax.nn.relu(split[:, 1]), split[:, 2]
    states = jnp.einsum("nhe,nhf->hef", feats, values, preferred_element_type=F32)
    key_sums = jnp.sum(feats, axis=0, dtype=F32)
    states, key_sums = running_total(states, key_sums[:, :, None], lax.axis_size("tm"))
    states, key_sums = states.astype(BF), key_sums[:, :, 0]
    numerator = jnp.einsum("nhe,hef->nhf", queries, states, preferred_element_type=F32)
    denominator = jnp.einsum(
        "nhe,he->nh", queries.astype(F32), key_sums, precision=lax.Precision.HIGHEST
    )
    out = (numerator / (denominator[:, :, None] + 1.0)).astype(BF)
    out = out.reshape(frame_count, joined, column_count, heads_here * HEAD)
    return lax.all_to_all(out, "space", split_axis=1, concat_axis=3, tiled=True)


def on_device(latents, proj_weight):
    even = lax.axis_size("groups") % 2 == 0 and lax.axis_size("space") == 2
    if even and proj_weight.shape[0] // DEPTH == 1 and lax.axis_size("tm") > 2:
        return ring_form(latents, proj_weight)
    return gathered_form(latents, proj_weight)


def solution(mesh):
    return jax.shard_map(
        on_device,
        mesh=mesh,
        in_specs=(P(("groups", "tm"), "space", None, None), P("tm", None)),
        out_specs=P(("groups", "tm"), "space", None, None),
        check_vma=False,
    )
```

time: 276 us -> 114 us (0.41); the launches traced: 273 us -> 114 us
  waiting for transfers between devices: 152 us -> 31.6 us
  starting transfers between devices: 0.08 us -> 40.5 us
  Pallas kernels: 0 us -> 37.2 us
  local copies, waits for them, and re-layouts: 39.6 us -> 2.74 us
  matrix products: 28.9 us -> 0 us
  blocking collectives: 28.8 us -> 0 us
  between operations: 13.2 us -> 0.31 us
  other arithmetic: 9.53 us -> 1.89 us
    all_gather x3 -> x0, waiting for transfers between devices: 151 us -> none  [the longest x1 121 us: project_rows(): return make_adder(flat, lax.all_gather(columns, 'tm', axis=0, tiled=True))]
    ppermute x0 -> x34, starting transfers between devices: none -> 40.5 us  [the longest x9 18.8 us: core_swap(): return lax.ppermute(value, 'space', over)]
    pallas_call x0 -> x9, Pallas kernels: none -> 37.2 us  [the longest x7 28.8 us: resident(): pl.pallas_call(kernel, in_specs=[pl.BlockSpec(memory_space=pltpu.SMEM)] +...]
    ppermute x0 -> x34, waiting for transfers between devices: none -> 31.6 us  [the longest x7 16.6 us: plane_swap(): return lax.ppermute(value[:third], 'groups', across)]
    dot_general x4 -> x0, matrix products: 28.9 us -> none  [the longest x1 22.4 us: make_adder(): return jnp.dot(flat, shard_rows, preferred_element_type=jnp.float32)]
    all_gather x1 -> x0, blocking collectives: 22.8 us -> none  [entering(): pieces = jax.tree.map(lambda part: lax.all_gather(part, axis), value)]
    reshape x4 -> x0, local copies, waits for them, and re-layouts: 21.7 us -> none  [the longest x2 14 us: on_device(): attended.reshape(frame_count, joined_rows, column_count, heads_here * HEAD)]
    select_n x14 -> x0, other arithmetic: 7.4 us -> none  [hop(): jnp.where(position < mine, new, old)]
  transfers between devices with their start and end apart: 3 -> 34, of which waited for: 3 -> 11; matrix products, arithmetic and copies ran while one was open for 7% -> 1% of each run, Pallas kernels for 0% -> 27%
where the time goes in v2:
time: 114 us
  starting transfers between devices  40.5 us (36%)
  Pallas kernels  37.2 us (33%)
  waiting for transfers between devices  31.6 us (28%)
  local copies, waits for them, and re-layouts  2.74 us (2%)
  other arithmetic  1.89 us (2%)
    pallas_call x7, Pallas kernels, resident(): pl.pallas_call(kernel, in_specs=[pl.BlockSpec(memory_space=pltpu.SMEM)] +...  28.8 us
    ppermute x9, starting transfers between devices, core_swap(): return lax.ppermute(value, 'space', over)  18.8 us
    ppermute x7, waiting for transfers between devices, plane_swap(): return lax.ppermute(value[:third], 'groups', across)  16.6 us
    ppermute x15, waiting for transfers between devices, ring(): return lax.ppermute(value, 'tm', forward if up else backward)  11.5 us
    ppermute x15, starting transfers between devices, ring(): return lax.ppermute(value, 'tm', forward if up else backward)  10.6 us
    ppermute x3, starting transfers between devices, running_total(): got = lax.ppermute(sent, 'tm', pairs)  5.97 us
    pallas_call x1, Pallas kernels, attend(): pl.pallas_call(functools.partial(attend_kernel, heads_here=heads_here), g...  5.85 us
    ppermute x7, starting transfers between devices, plane_swap(): return lax.ppermute(value[:third], 'groups', across)  5.05 us
  transfers between devices with their start and end apart: 34, of which 11 were waited for; matrix products, arithmetic and copies ran while one was open for 1% of the time, Pallas kernels for 27%

profile of v2, /device:TPU:27, one launch (start us, length us, event | category | flops | bytes accessed | tf_op | source)
XLA Modules:
  0.0 114.1 jit_solution(8242509093752994174)
XLA Ops:
  0.0 0.8 dynamic-slice_bitcast_fusion
  0.9 1.8 %copy-done.1 = bf16[280,3360]{1,0:T(8,128)(2,1)S(1)} copy-done((bf16[280,3360]{1,0:T(8,128)(2,1)S(1)}, bf16[280,3360]{1,0:T(8,128)(2,1)}, u32[]{:S(2)}) %copy-start.1) | copy-done | bytes 1881624
  2.7 0.8 pack_first.1.after_ref.refs_2_.refs_4_.refs_6_
  3.5 0.2 collective-permute-start.1
  3.7 1.3 %collective-permute-start = (bf16[192,1120]{1,0:T(8,128)(2,1)S(1)}, bf16[192,1120]{1,0:T(8,128)(2,1)S(1)}, u32[]{:S(2)}, u32[]{:S(2)}) collective-permute-start(bf16[192,1120]{1,0:T(8,128)(2,1)S(1)} %pack_first.1.after_ref.refs_2_.refs_4_.refs_6_), channel_id=1, source_target_pairs={{0,4},{4,8},{8,12},{12,14},{14,10},{10,6},{6,2},{2,0},{1,5},{5,9},... | collective-permute-start | bytes 1290248 | tf_op jit(solution)/shard_map/ppermute | solution.py:448
  5.0 0.8 pack_rest.1
  5.8 2.5 %pack_tokens.1.refs_0_ = bf16[960,2304]{1,0:T(8,128)(2,1)S(1)} custom-call(bf16[960,2240]{1,0:T(8,128)(2,1)S(1)} %bitcast.6, bf16[144,1120]{1,0:T(8,128)(2,1)S(1)} %get-tuple-element.40.after_ref.refs_1_.refs_8_), custom_call_target="tpu_custom_call" | custom-call | bytes 8601600 | tf_op jit(solution)/shard_map/pack_tokens/pallas_call | solution.py:163
  8.2 6.3 %collective-permute-done.1.refs_8_.refs_10_ = bf16[192,1120]{1,0:T(8,128)(2,1)S(1)} collective-permute-done((bf16[192,1120]{1,0:T(8,128)(2,1)S(1)}, bf16[192,1120]{1,0:T(8,128)(2,1)S(1)}, u32[]{:S(2)}, u32[]{:S(2)}) %collective-permute-start.1) | collective-permute-done | bytes 430112 | tf_op jit(solution)/shard_map/ppermute | solution.py:448
  14.5 1.7 %collective-permute-start.2 = (bf16[960,2304]{1,0:T(8,128)(2,1)S(1)}, bf16[960,2304]{1,0:T(8,128)(2,1)S(1)}, u32[]{:S(2)}, u32[]{:S(2)}) collective-permute-start(bf16[960,2304]{1,0:T(8,128)(2,1)S(1)} %pack_tokens.1.refs_0_), channel_id=1, source_target_pairs={{0,1},{1,0},{2,3},{3,2},{4,5},{5,4},{6,7},{7,6},{8,9},{9,8},{10,11... | collective-permute-start | bytes 13271048 | tf_op jit(solution)/shard_map/ppermute | solution.py:454
  16.4 1.3 %collective-permute-start.3 = (bf16[192,1120]{1,0:T(8,128)(2,1)S(1)}, bf16[192,1120]{1,0:T(8,128)(2,1)S(1)}, u32[]{:S(2)}, u32[]{:S(2)}) collective-permute-start(bf16[192,1120]{1,0:T(8,128)(2,1)S(1)} %collective-permute-done.refs_5_.refs_7_), channel_id=1, source_target_pairs={{0,4},{4,8},{8,12},{12,14},{14,10},{10,6},{6,2},{2,0},{1,5},{5,9},... | collective-permute-start | bytes 1290248 | tf_op jit(solution)/shard_map/ppermute | solution.py:448
  17.7 0.3 collective-permute-start.6
  18.1 1.3 %collective-permute-start.5 = (bf16[96,1120]{1,0:T(8,128)(2,1)S(1)}, bf16[96,1120]{1,0:T(8,128)(2,1)S(1)}, u32[]{:S(2)}, u32[]{:S(2)}) collective-permute-start(bf16[96,1120]{1,0:T(8,128)(2,1)S(1)} %slice.73), channel_id=1, source_target_pairs={{0,16},{16,0},{1,17},{17,1},{2,18},{18,2},{3,19},{19,3},{4,20},{20... | collective-permute-start | bytes 645128 | tf_op jit(solution)/shard_map/ppermute | solution.py:451
  19.4 4.9 %collective-permute-done.6.refs_9_ = bf16[96,1120]{1,0:T(8,128)(2,1)S(1)} collective-permute-done((bf16[96,1120]{1,0:T(8,128)(2,1)S(1)}, bf16[96,1120]{1,0:T(8,128)(2,1)S(1)}, u32[]{:S(2)}, u32[]{:S(2)}) %collective-permute-start.6) | collective-permute-done | bytes 215072 | tf_op jit(solution)/shard_map/ppermute | solution.py:451
  24.2 4.7 %collective-permute-done.5.refs_6_ = bf16[96,1120]{1,0:T(8,128)(2,1)S(1)} collective-permute-done((bf16[96,1120]{1,0:T(8,128)(2,1)S(1)}, bf16[96,1120]{1,0:T(8,128)(2,1)S(1)}, u32[]{:S(2)}, u32[]{:S(2)}) %collective-permute-start.5) | collective-permute-done | bytes 215072 | tf_op jit(solution)/shard_map/ppermute | solution.py:451
  29.0 1.3 %collective-permute-start.7 = (bf16[192,1120]{1,0:T(8,128)(2,1)S(1)}, bf16[192,1120]{1,0:T(8,128)(2,1)S(1)}, u32[]{:S(2)}, u32[]{:S(2)}) collective-permute-start(bf16[192,1120]{1,0:T(8,128)(2,1)S(1)} %collective-permute-done.3.refs_11_.refs_13_.refs_9_), channel_id=1, source_target_pairs={{0,4},{4,8},{8,12},{12,14},{14,10},{10,6},{6,2},{2,0},{1,5},{5,9},... | collective-permute-start | bytes 1290248 | tf_op jit(solution)/shard_map/ppermute | solution.py:448
  30.5 0.3 collective-permute-start.10
  30.9 1.3 %collective-permute-start.9 = (bf16[96,1120]{1,0:T(8,128)(2,1)S(1)}, bf16[96,1120]{1,0:T(8,128)(2,1)S(1)}, u32[]{:S(2)}, u32[]{:S(2)}) collective-permute-start(bf16[96,1120]{1,0:T(8,128)(2,1)S(1)} %slice.57), channel_id=1, source_target_pairs={{0,16},{16,0},{1,17},{17,1},{2,18},{18,2},{3,19},{19,3},{4,20},{20... | collective-permute-start | bytes 645128 | tf_op jit(solution)/shard_map/ppermute | solution.py:451
  32.3 3.4 %collective-permute-done.10.refs_15_ = bf16[96,1120]{1,0:T(8,128)(2,1)S(1)} collective-permute-done((bf16[96,1120]{1,0:T(8,128)(2,1)S(1)}, bf16[96,1120]{1,0:T(8,128)(2,1)S(1)}, u32[]{:S(2)}, u32[]{:S(2)}) %collective-permute-start.10) | collective-permute-done | bytes 215072 | tf_op jit(solution)/shard_map/ppermute | solution.py:451
  35.7 1.3 %collective-permute-start.15 = (bf16[144,1120]{1,0:T(8,128)(2,1)S(1)}, bf16[144,1120]{1,0:T(8,128)(2,1)S(1)}, u32[]{:S(2)}, u32[]{:S(2)}) collective-permute-start(bf16[144,1120]{1,0:T(8,128)(2,1)S(1)} %get-tuple-element.40.after_ref.refs_1_.refs_8_), channel_id=1, source_target_pairs={{0,4},{4,8},{8,12},{12,14},{14,10},{10,6},{6,2},{2,0},{1,5},{5,9},... | collective-permute-start | bytes 967688 | tf_op jit(solution)/shard_map/ppermute | solution.py:448
  37.0 3.3 %collective-permute-done.9.refs_12_ = bf16[96,1120]{1,0:T(8,128)(2,1)S(1)} collective-permute-done((bf16[96,1120]{1,0:T(8,128)(2,1)S(1)}, bf16[96,1120]{1,0:T(8,128)(2,1)S(1)}, u32[]{:S(2)}, u32[]{:S(2)}) %collective-permute-start.9) | collective-permute-done | bytes 215072 | tf_op jit(solution)/shard_map/ppermute | solution.py:451
  40.3 0.3 collective-permute-start.13
  40.6 1.3 %collective-permute-start.11 = (bf16[96,1120]{1,0:T(8,128)(2,1)S(1)}, bf16[96,1120]{1,0:T(8,128)(2,1)S(1)}, u32[]{:S(2)}, u32[]{:S(2)}) collective-permute-start(bf16[96,1120]{1,0:T(8,128)(2,1)S(1)} %slice.59), channel_id=1, source_target_pairs={{0,4},{4,8},{8,12},{12,14},{14,10},{10,6},{6,2},{2,0},{1,5},{5,9},... | collective-permute-start | bytes 645128 | tf_op jit(solution)/shard_map/ppermute | solution.py:448
  42.0 1.3 %collective-permute-start.14 = (bf16[96,1120]{1,0:T(8,128)(2,1)S(1)}, bf16[96,1120]{1,0:T(8,128)(2,1)S(1)}, u32[]{:S(2)}, u32[]{:S(2)}) collective-permute-start(bf16[96,1120]{1,0:T(8,128)(2,1)S(1)} %get-tuple-element.83), channel_id=1, source_target_pairs={{0,16},{16,0},{1,17},{17,1},{2,18},{18,2},{3,19},{19,3},{4,20},{20... | collective-permute-start | bytes 645128 | tf_op jit(solution)/shard_map/ppermute | solution.py:451
  43.2 4.2 %collective-permute-done.16.refs_5_.refs_12_ = bf16[144,1120]{1,0:T(8,128)(2,1)S(1)} collective-permute-done((bf16[144,1120]{1,0:T(8,128)(2,1)S(1)}, bf16[144,1120]{1,0:T(8,128)(2,1)S(1)}, u32[]{:S(2)}, u32[]{:S(2)}) %collective-permute-start.16) | collective-permute-done | bytes 322592 | tf_op jit(solution)/shard_map/ppermute | solution.py:448
  47.6 7.9 %kv_part.2.refs_2_ = f32[1920,1120]{1,0:T(8,128)S(1)} custom-call(s32[10]{0:T(128)S(1)} %pad_add_fusion.meta, bf16[960,2304]{1,0:T(8,128)(2,1)S(1)} %pack_tokens.1.refs_0_, bf16[960,2304]{1,0:T(8,128)(2,1)S(1)} %collective-permute-done.2.refs_1_, bf16[192,1120]{1,0:T(8,128)(2,1)S(1)} %pack_first.1.after_ref.refs_2_.refs_4_.refs_6_, ...), custom_call_target="tpu_custom_call" | custom-call | flops 5505024000 | tf_op jit(solution)/shard_map/kv_part/pallas_call | solution.py:68
  55.5 1.3 %collective-permute-start.18 = (bf16[144,1120]{1,0:T(8,128)(2,1)S(1)}, bf16[144,1120]{1,0:T(8,128)(2,1)S(1)}, u32[]{:S(2)}, u32[]{:S(2)}) collective-permute-start(bf16[144,1120]{1,0:T(8,128)(2,1)S(1)} %collective-permute-done.15.refs_3_.refs_10_), channel_id=1, source_target_pairs={{0,4},{4,8},{8,12},{12,14},{14,10},{10,6},{6,2},{2,0},{1,5},{5,9},... | collective-permute-start | bytes 967688 | tf_op jit(solution)/shard_map/ppermute | solution.py:448
  57.0 0.3 collective-permute-start.17
  57.3 4.5 %kv_part.3.refs_2_ = f32[1920,1120]{1,0:T(8,128)S(1)} custom-call(s32[10]{0:T(128)S(1)} %pad_add_fusion.meta, bf16[960,2304]{1,0:T(8,128)(2,1)S(1)} %pack_tokens.1.refs_0_, bf16[960,2304]{1,0:T(8,128)(2,1)S(1)} %collective-permute-done.2.refs_1_, f32[1920,1120]{1,0:T(8,128)S(1)} %kv_part.2.refs_2_, ...), custom_call_target="tpu_custom_call", output_to_operand_aliasing={{}: (3, {})} | custom-call | flops 2202009600 | tf_op jit(solution)/shard_map/kv_part/pallas_call | solution.py:68
  61.8 0.3 collective-permute-done.17.refs_4_
  62.1 1.0 collective-permute-done.19.refs_9_.refs_16_
  63.1 1.2 %collective-permute-start.20 = (bf16[144,1120]{1,0:T(8,128)(2,1)S(1)}, bf16[144,1120]{1,0:T(8,128)(2,1)S(1)}, u32[]{:S(2)}, u32[]{:S(2)}) collective-permute-start(bf16[144,1120]{1,0:T(8,128)(2,1)S(1)} %collective-permute-done.18.refs_7_.refs_14_), channel_id=1, source_target_pairs={{0,4},{4,8},{8,12},{12,14},{14,10},{10,6},{6,2},{2,0},{1,5},{5,9},... | collective-permute-start | bytes 967688 | tf_op jit(solution)/shard_map/ppermute | solution.py:448
  64.3 0.2 collective-permute-start.21
  64.6 6.9 %states.1 = f32[560,128]{1,0:T(8,128)S(1)} custom-call(s32[10]{0:T(128)S(1)} %pad_add_fusion.meta, bf16[960,2304]{1,0:T(8,128)(2,1)S(1)} %pack_tokens.1.refs_0_, bf16[960,2304]{1,0:T(8,128)(2,1)S(1)} %collective-permute-done.2.refs_1_, f32[1920,1120]{1,0:T(8,128)S(1)} %kv_part.3.refs_2_, bf16[96,1120]{1,0:T(8,128)(2,1)S(1)} %collective-permute-done.11.refs_3_, ...), custom_call_target="tpu_custom_call" | custom-call | flops 3853516800 | tf_op jit(solution)/shard_map/states/pallas_call | solution.py:68
  72.1 3.4 %collective-permute-start.22 = (bf16[560,128]{1,0:T(8,128)(2,1)S(1)}, bf16[560,128]{1,0:T(8,128)(2,1)S(1)}, u32[]{:S(2)}, u32[]{:S(2)}) collective-permute-start(bf16[560,128]{1,0:T(8,128)(2,1)S(1)} %pad_maximum_fusion.1), channel_id=1, source_target_pairs={{0,2},{2,4},{4,6},{6,8},{8,10},{10,12},{12,14},{1,3},{3,5},{5,7},{... | collective-permute-start | bytes 430088 | tf_op jit(solution)/shard_map/ppermute | solution.py:420
  75.5 7.0 %collective-permute-start.25 = (bf16[144,1120]{1,0:T(8,128)(2,1)S(1)}, bf16[144,1120]{1,0:T(8,128)(2,1)S(1)}, u32[]{:S(2)}, u32[]{:S(2)}) collective-permute-start(bf16[144,1120]{1,0:T(8,128)(2,1)S(1)} %collective-permute-done.15.refs_3_.refs_10_), channel_id=1, source_target_pairs={{0,1},{1,0},{2,3},{3,2},{4,5},{5,4},{6,7},{7,6},{8,9},{9,8},{10,11... | collective-permute-start | bytes 967688 | tf_op jit(solution)/shard_map/ppermute | solution.py:454
  82.6 0.4 collective-permute-start.27
  83.0 3.5 %collective-permute-start.28 = (bf16[144,1120]{1,0:T(8,128)(2,1)S(1)}, bf16[144,1120]{1,0:T(8,128)(2,1)S(1)}, u32[]{:S(2)}, u32[]{:S(2)}) collective-permute-start(bf16[144,1120]{1,0:T(8,128)(2,1)S(1)} %collective-permute-done.19.refs_9_.refs_16_), channel_id=1, source_target_pairs={{0,1},{1,0},{2,3},{3,2},{4,5},{5,4},{6,7},{7,6},{8,9},{9,8},{10,11... | collective-permute-start | bytes 967688 | tf_op jit(solution)/shard_map/ppermute | solution.py:454
  86.7 0.3 subtract_convert_fusion.1
  87.2 1.3 %collective-permute-start.24 = (bf16[560,128]{1,0:T(8,128)(2,1)S(1)}, bf16[560,128]{1,0:T(8,128)(2,1)S(1)}, u32[]{:S(2)}, u32[]{:S(2)}) collective-permute-start(bf16[560,128]{1,0:T(8,128)(2,1)S(1)} %pad_maximum_fusion.2), channel_id=1, source_target_pairs={{0,4},{2,6},{4,8},{6,10},{8,12},{10,14},{1,5},{3,7},{5,9},{7,11},{... | collective-permute-start | bytes 430088 | tf_op jit(solution)/shard_map/ppermute | solution.py:420
  88.5 4.3 %q_early.1.refs_1_ = f32[960,1120]{1,0:T(8,128)S(1)} custom-call(s32[10]{0:T(128)S(1)} %pad_add_fusion.meta, bf16[960,2304]{1,0:T(8,128)(2,1)S(1)} %pack_tokens.1.refs_0_, bf16[144,1120]{1,0:T(8,128)(2,1)S(1)} %get-tuple-element.40.after_ref.refs_1_.refs_8_, bf16[144,1120]{1,0:T(8,128)(2,1)S(1)} %get-tuple-element.68.refs_2_.refs_9_, ...), custom_call_target="tpu_custom_call" | custom-call | flops 2752512000 | tf_op jit(solution)/shard_map/q_early/pallas_call | solution.py:68
  92.8 0.5 collective-permute-start.30
  93.4 0.5 collective-permute-done.24
  94.4 1.3 %collective-permute-start.29 = (bf16[560,128]{1,0:T(8,128)(2,1)S(1)}, bf16[560,128]{1,0:T(8,128)(2,1)S(1)}, u32[]{:S(2)}, u32[]{:S(2)}) collective-permute-start(bf16[560,128]{1,0:T(8,128)(2,1)S(1)} %pad_maximum_fusion.3), channel_id=1, source_target_pairs={{0,8},{2,10},{4,12},{6,14},{1,9},{3,11},{5,13},{7,15},{16,24},{18,... | collective-permute-start | bytes 430088 | tf_op jit(solution)/shard_map/ppermute | solution.py:420
  95.7 3.7 %q_late.1.q_ref = bf16[960,1120]{1,0:T(8,128)(2,1)S(1)} custom-call(s32[10]{0:T(128)S(1)} %pad_add_fusion.meta, bf16[960,2304]{1,0:T(8,128)(2,1)S(1)} %pack_tokens.1.refs_0_, f32[960,1120]{1,0:T(8,128)S(1)} %q_early.1.refs_1_, bf16[144,1120]{1,0:T(8,128)(2,1)S(1)} %collective-permute-done.20.refs_2_.refs_18_, ...), custom_call_target="tpu_custom_call" | custom-call | flops 2202009600 | tf_op jit(solution)/shard_map/q_late/pallas_call | solution.py:68
  99.4 1.7 %collective-permute-done.29 = bf16[560,128]{1,0:T(8,128)(2,1)S(1)} collective-permute-done((bf16[560,128]{1,0:T(8,128)(2,1)S(1)}, bf16[560,128]{1,0:T(8,128)(2,1)S(1)}, u32[]{:S(2)}, u32[]{:S(2)}) %collective-permute-start.29) | collective-permute-done | bytes 143392 | tf_op jit(solution)/shard_map/ppermute | solution.py:420
  101.7 5.4 %collective-permute-start.33 = (f32[560,128]{1,0:T(8,128)S(1)}, f32[560,128]{1,0:T(8,128)S(1)}, u32[]{:S(2)}, u32[]{:S(2)}) collective-permute-start(f32[560,128]{1,0:T(8,128)S(1)} %pad_maximum_fusion.mine_ref), channel_id=1, source_target_pairs={{0,1},{1,0},{2,3},{3,2},{4,5},{5,4},{6,7},{7,6},{8,9},{9,8},{10,11... | collective-permute-start | bytes 860168 | tf_op jit(solution)/shard_map/ppermute | solution.py:454
  107.1 1.2 %collective-permute-done.33.theirs_ref = f32[560,128]{1,0:T(8,128)S(1)} collective-permute-done((f32[560,128]{1,0:T(8,128)S(1)}, f32[560,128]{1,0:T(8,128)S(1)}, u32[]{:S(2)}, u32[]{:S(2)}) %collective-permute-start.33) | collective-permute-done | bytes 286752 | tf_op jit(solution)/shard_map/ppermute | solution.py:454
  108.3 5.8 %attend.1 = bf16[960,1120]{1,0:T(8,128)(2,1)} custom-call(s32[10]{0:T(128)S(1)} %pad_add_fusion.meta, bf16[960,1120]{1,0:T(8,128)(2,1)S(1)} %q_late.1.q_ref, f32[560,128]{1,0:T(8,128)S(1)} %pad_maximum_fusion.mine_ref, f32[560,128]{1,0:T(8,128)S(1)} %collective-permute-done.33.theirs_ref), custom_call_target="tpu_custom_call" | custom-call | flops 1720320000 | bytes 4300800 | tf_op jit(solution)/shard_map/attend/pallas_call | solution.py:382
  (56 shorter events, 3.1 us)
Async XLA Ops:
  0.0 5.7 %copy-start = (bf16[2,6,80,2240]{3,2,1,0:T(8,128)(2,1)S(1)}, bf16[2,6,80,2240]{3,2,1,0:T(8,128)(2,1)}, u32[]{:S(2)}) copy-start(bf16[2,6,80,2240]{3,2,1,0:T(8,128)(2,1)} %param.3) | copy-start | bytes 12902404
  0.9 1.8 %copy-start.1 = (bf16[280,3360]{1,0:T(8,128)(2,1)S(1)}, bf16[280,3360]{1,0:T(8,128)(2,1)}, u32[]{:S(2)}) copy-start(bf16[280,3360]{1,0:T(8,128)(2,1)} %w_ref.3) | copy-start | bytes 5644804
  3.5 11.1 %collective-permute-start.1 = (bf16[192,1120]{1,0:T(8,128)(2,1)S(1)}, bf16[192,1120]{1,0:T(8,128)(2,1)S(1)}, u32[]{:S(2)}, u32[]{:S(2)}) collective-permute-start(bf16[192,1120]{1,0:T(8,128)(2,1)S(1)} %pack_first.1.after_ref.refs_2_.refs_4_.refs_6_), channel_id=1, source_target_pairs={{4,0},{8,4},{12,8},{14,12},{10,14},{6,10},{2,6},{0,2},{5,1},{9,5},... | collective-permute-start | bytes 1290248 | tf_op jit(solution)/shard_map/ppermute | solution.py:448
  3.7 10.9 %collective-permute-start = (bf16[192,1120]{1,0:T(8,128)(2,1)S(1)}, bf16[192,1120]{1,0:T(8,128)(2,1)S(1)}, u32[]{:S(2)}, u32[]{:S(2)}) collective-permute-start(bf16[192,1120]{1,0:T(8,128)(2,1)S(1)} %pack_first.1.after_ref.refs_2_.refs_4_.refs_6_), channel_id=1, source_target_pairs={{0,4},{4,8},{8,12},{12,14},{14,10},{10,6},{6,2},{2,0},{1,5},{5,9},... | collective-permute-start | bytes 1290248 | tf_op jit(solution)/shard_map/ppermute | solution.py:448
  14.5 14.4 %collective-permute-start.2 = (bf16[960,2304]{1,0:T(8,128)(2,1)S(1)}, bf16[960,2304]{1,0:T(8,128)(2,1)S(1)}, u32[]{:S(2)}, u32[]{:S(2)}) collective-permute-start(bf16[960,2304]{1,0:T(8,128)(2,1)S(1)} %pack_tokens.1.refs_0_), channel_id=1, source_target_pairs={{0,1},{1,0},{2,3},{3,2},{4,5},{5,4},{6,7},{7,6},{8,9},{9,8},{10,11... | collective-permute-start | bytes 13271048 | tf_op jit(solution)/shard_map/ppermute | solution.py:454
  16.3 12.7 %collective-permute-start.4 = (bf16[192,1120]{1,0:T(8,128)(2,1)S(1)}, bf16[192,1120]{1,0:T(8,128)(2,1)S(1)}, u32[]{:S(2)}, u32[]{:S(2)}) collective-permute-start(bf16[192,1120]{1,0:T(8,128)(2,1)S(1)} %collective-permute-done.1.refs_8_.refs_10_), channel_id=1, source_target_pairs={{4,0},{8,4},{12,8},{14,12},{10,14},{6,10},{2,6},{0,2},{5,1},{9,5},... | collective-permute-start | bytes 1290248 | tf_op jit(solution)/shard_map/ppermute | solution.py:448
  16.4 12.6 %collective-permute-start.3 = (bf16[192,1120]{1,0:T(8,128)(2,1)S(1)}, bf16[192,1120]{1,0:T(8,128)(2,1)S(1)}, u32[]{:S(2)}, u32[]{:S(2)}) collective-permute-start(bf16[192,1120]{1,0:T(8,128)(2,1)S(1)} %collective-permute-done.refs_5_.refs_7_), channel_id=1, source_target_pairs={{0,4},{4,8},{8,12},{12,14},{14,10},{10,6},{6,2},{2,0},{1,5},{5,9},... | collective-permute-start | bytes 1290248 | tf_op jit(solution)/shard_map/ppermute | solution.py:448
  17.7 6.5 %collective-permute-start.6 = (bf16[96,1120]{1,0:T(8,128)(2,1)S(1)}, bf16[96,1120]{1,0:T(8,128)(2,1)S(1)}, u32[]{:S(2)}, u32[]{:S(2)}) collective-permute-start(bf16[96,1120]{1,0:T(8,128)(2,1)S(1)} %slice.74), channel_id=1, source_target_pairs={{0,16},{16,0},{1,17},{17,1},{2,18},{18,2},{3,19},{19,3},{4,20},{20... | collective-permute-start | bytes 645128 | tf_op jit(solution)/shard_map/ppermute | solution.py:451
  18.1 10.9 %collective-permute-start.5 = (bf16[96,1120]{1,0:T(8,128)(2,1)S(1)}, bf16[96,1120]{1,0:T(8,128)(2,1)S(1)}, u32[]{:S(2)}, u32[]{:S(2)}) collective-permute-start(bf16[96,1120]{1,0:T(8,128)(2,1)S(1)} %slice.73), channel_id=1, source_target_pairs={{0,16},{16,0},{1,17},{17,1},{2,18},{18,2},{3,19},{19,3},{4,20},{20... | collective-permute-start | bytes 645128 | tf_op jit(solution)/shard_map/ppermute | solution.py:451
  29.0 11.3 %collective-permute-start.7 = (bf16[192,1120]{1,0:T(8,128)(2,1)S(1)}, bf16[192,1120]{1,0:T(8,128)(2,1)S(1)}, u32[]{:S(2)}, u32[]{:S(2)}) collective-permute-start(bf16[192,1120]{1,0:T(8,128)(2,1)S(1)} %collective-permute-done.3.refs_11_.refs_13_.refs_9_), channel_id=1, source_target_pairs={{0,4},{4,8},{8,12},{12,14},{14,10},{10,6},{6,2},{2,0},{1,5},{5,9},... | collective-permute-start | bytes 1290248 | tf_op jit(solution)/shard_map/ppermute | solution.py:448
  30.3 10.0 %collective-permute-start.8 = (bf16[192,1120]{1,0:T(8,128)(2,1)S(1)}, bf16[192,1120]{1,0:T(8,128)(2,1)S(1)}, u32[]{:S(2)}, u32[]{:S(2)}) collective-permute-start(bf16[192,1120]{1,0:T(8,128)(2,1)S(1)} %collective-permute-done.4.refs_14_.refs_16_.refs_10_), channel_id=1, source_target_pairs={{4,0},{8,4},{12,8},{14,12},{10,14},{6,10},{2,6},{0,2},{5,1},{9,5},... | collective-permute-start | bytes 1290248 | tf_op jit(solution)/shard_map/ppermute | solution.py:448
  30.5 5.1 %collective-permute-start.10 = (bf16[96,1120]{1,0:T(8,128)(2,1)S(1)}, bf16[96,1120]{1,0:T(8,128)(2,1)S(1)}, u32[]{:S(2)}, u32[]{:S(2)}) collective-permute-start(bf16[96,1120]{1,0:T(8,128)(2,1)S(1)} %slice.58), channel_id=1, source_target_pairs={{0,16},{16,0},{1,17},{17,1},{2,18},{18,2},{3,19},{19,3},{4,20},{20... | collective-permute-start | bytes 645128 | tf_op jit(solution)/shard_map/ppermute | solution.py:451
  30.9 9.4 %collective-permute-start.9 = (bf16[96,1120]{1,0:T(8,128)(2,1)S(1)}, bf16[96,1120]{1,0:T(8,128)(2,1)S(1)}, u32[]{:S(2)}, u32[]{:S(2)}) collective-permute-start(bf16[96,1120]{1,0:T(8,128)(2,1)S(1)} %slice.57), channel_id=1, source_target_pairs={{0,16},{16,0},{1,17},{17,1},{2,18},{18,2},{3,19},{19,3},{4,20},{20... | collective-permute-start | bytes 645128 | tf_op jit(solution)/shard_map/ppermute | solution.py:451
  32.1 15.3 %collective-permute-start.16 = (bf16[144,1120]{1,0:T(8,128)(2,1)S(1)}, bf16[144,1120]{1,0:T(8,128)(2,1)S(1)}, u32[]{:S(2)}, u32[]{:S(2)}) collective-permute-start(bf16[144,1120]{1,0:T(8,128)(2,1)S(1)} %get-tuple-element.40.after_ref.refs_1_.refs_8_), channel_id=1, source_target_pairs={{4,0},{8,4},{12,8},{14,12},{10,14},{6,10},{2,6},{0,2},{5,1},{9,5},... | collective-permute-start | bytes 967688 | tf_op jit(solution)/shard_map/ppermute | solution.py:448
  35.7 19.8 %collective-permute-start.15 = (bf16[144,1120]{1,0:T(8,128)(2,1)S(1)}, bf16[144,1120]{1,0:T(8,128)(2,1)S(1)}, u32[]{:S(2)}, u32[]{:S(2)}) collective-permute-start(bf16[144,1120]{1,0:T(8,128)(2,1)S(1)} %get-tuple-element.40.after_ref.refs_1_.refs_8_), channel_id=1, source_target_pairs={{0,4},{4,8},{8,12},{12,14},{14,10},{10,6},{6,2},{2,0},{1,5},{5,9},... | collective-permute-start | bytes 967688 | tf_op jit(solution)/shard_map/ppermute | solution.py:448
  40.3 15.1 %collective-permute-start.13 = (bf16[96,1120]{1,0:T(8,128)(2,1)S(1)}, bf16[96,1120]{1,0:T(8,128)(2,1)S(1)}, u32[]{:S(2)}, u32[]{:S(2)}) collective-permute-start(bf16[96,1120]{1,0:T(8,128)(2,1)S(1)} %slice.59), channel_id=1, source_target_pairs={{0,16},{16,0},{1,17},{17,1},{2,18},{18,2},{3,19},{19,3},{4,20},{20... | collective-permute-start | bytes 645128 | tf_op jit(solution)/shard_map/ppermute | solution.py:451
  40.6 14.8 %collective-permute-start.11 = (bf16[96,1120]{1,0:T(8,128)(2,1)S(1)}, bf16[96,1120]{1,0:T(8,128)(2,1)S(1)}, u32[]{:S(2)}, u32[]{:S(2)}) collective-permute-start(bf16[96,1120]{1,0:T(8,128)(2,1)S(1)} %slice.59), channel_id=1, source_target_pairs={{0,4},{4,8},{8,12},{12,14},{14,10},{10,6},{6,2},{2,0},{1,5},{5,9},... | collective-permute-start | bytes 645128 | tf_op jit(solution)/shard_map/ppermute | solution.py:448
  42.0 13.5 %collective-permute-start.14 = (bf16[96,1120]{1,0:T(8,128)(2,1)S(1)}, bf16[96,1120]{1,0:T(8,128)(2,1)S(1)}, u32[]{:S(2)}, u32[]{:S(2)}) collective-permute-start(bf16[96,1120]{1,0:T(8,128)(2,1)S(1)} %get-tuple-element.83), channel_id=1, source_target_pairs={{0,16},{16,0},{1,17},{17,1},{2,18},{18,2},{3,19},{19,3},{4,20},{20... | collective-permute-start | bytes 645128 | tf_op jit(solution)/shard_map/ppermute | solution.py:451
  47.4 8.1 %collective-permute-start.12 = (bf16[96,1120]{1,0:T(8,128)(2,1)S(1)}, bf16[96,1120]{1,0:T(8,128)(2,1)S(1)}, u32[]{:S(2)}, u32[]{:S(2)}) collective-permute-start(bf16[96,1120]{1,0:T(8,128)(2,1)S(1)} %get-tuple-element.84), channel_id=1, source_target_pairs={{4,0},{8,4},{12,8},{14,12},{10,14},{6,10},{2,6},{0,2},{5,1},{9,5},... | collective-permute-start | bytes 645128 | tf_op jit(solution)/shard_map/ppermute | solution.py:448
  55.5 6.6 %collective-permute-start.18 = (bf16[144,1120]{1,0:T(8,128)(2,1)S(1)}, bf16[144,1120]{1,0:T(8,128)(2,1)S(1)}, u32[]{:S(2)}, u32[]{:S(2)}) collective-permute-start(bf16[144,1120]{1,0:T(8,128)(2,1)S(1)} %collective-permute-done.15.refs_3_.refs_10_), channel_id=1, source_target_pairs={{0,4},{4,8},{8,12},{12,14},{14,10},{10,6},{6,2},{2,0},{1,5},{5,9},... | collective-permute-start | bytes 967688 | tf_op jit(solution)/shard_map/ppermute | solution.py:448
  56.8 6.3 %collective-permute-start.19 = (bf16[144,1120]{1,0:T(8,128)(2,1)S(1)}, bf16[144,1120]{1,0:T(8,128)(2,1)S(1)}, u32[]{:S(2)}, u32[]{:S(2)}) collective-permute-start(bf16[144,1120]{1,0:T(8,128)(2,1)S(1)} %collective-permute-done.16.refs_5_.refs_12_), channel_id=1, source_target_pairs={{4,0},{8,4},{12,8},{14,12},{10,14},{6,10},{2,6},{0,2},{5,1},{9,5},... | collective-permute-start | bytes 967688 | tf_op jit(solution)/shard_map/ppermute | solution.py:448
  57.0 5.1 %collective-permute-start.17 = (bf16[96,1120]{1,0:T(8,128)(2,1)S(1)}, bf16[96,1120]{1,0:T(8,128)(2,1)S(1)}, u32[]{:S(2)}, u32[]{:S(2)}) collective-permute-start(bf16[96,1120]{1,0:T(8,128)(2,1)S(1)} %collective-permute-done.11.refs_3_), channel_id=1, source_target_pairs={{0,16},{16,0},{1,17},{17,1},{2,18},{18,2},{3,19},{19,3},{4,20},{20... | collective-permute-start | bytes 645128 | tf_op jit(solution)/shard_map/ppermute | solution.py:451
  63.1 8.4 %collective-permute-start.20 = (bf16[144,1120]{1,0:T(8,128)(2,1)S(1)}, bf16[144,1120]{1,0:T(8,128)(2,1)S(1)}, u32[]{:S(2)}, u32[]{:S(2)}) collective-permute-start(bf16[144,1120]{1,0:T(8,128)(2,1)S(1)} %collective-permute-done.18.refs_7_.refs_14_), channel_id=1, source_target_pairs={{0,4},{4,8},{8,12},{12,14},{14,10},{10,6},{6,2},{2,0},{1,5},{5,9},... | collective-permute-start | bytes 967688 | tf_op jit(solution)/shard_map/ppermute | solution.py:448
  64.3 7.2 %collective-permute-start.21 = (bf16[144,1120]{1,0:T(8,128)(2,1)S(1)}, bf16[144,1120]{1,0:T(8,128)(2,1)S(1)}, u32[]{:S(2)}, u32[]{:S(2)}) collective-permute-start(bf16[144,1120]{1,0:T(8,128)(2,1)S(1)} %collective-permute-done.19.refs_9_.refs_16_), channel_id=1, source_target_pairs={{4,0},{8,4},{12,8},{14,12},{10,14},{6,10},{2,6},{0,2},{5,1},{9,5},... | collective-permute-start | bytes 967688 | tf_op jit(solution)/shard_map/ppermute | solution.py:448
  71.5 15.1 %collective-permute-start.23 = (bf16[144,1120]{1,0:T(8,128)(2,1)S(1)}, bf16[144,1120]{1,0:T(8,128)(2,1)S(1)}, u32[]{:S(2)}, u32[]{:S(2)}) collective-permute-start(bf16[144,1120]{1,0:T(8,128)(2,1)S(1)} %collective-permute-done.21.refs_4_.refs_20_), channel_id=1, source_target_pairs={{4,0},{8,4},{12,8},{14,12},{10,14},{6,10},{2,6},{0,2},{5,1},{9,5},... | collective-permute-start | bytes 967688 | tf_op jit(solution)/shard_map/ppermute | solution.py:448
  72.1 10.9 %collective-permute-start.22 = (bf16[560,128]{1,0:T(8,128)(2,1)S(1)}, bf16[560,128]{1,0:T(8,128)(2,1)S(1)}, u32[]{:S(2)}, u32[]{:S(2)}) collective-permute-start(bf16[560,128]{1,0:T(8,128)(2,1)S(1)} %pad_maximum_fusion.1), channel_id=1, source_target_pairs={{0,2},{2,4},{4,6},{6,8},{8,10},{10,12},{12,14},{1,3},{3,5},{5,7},{... | collective-permute-start | bytes 430088 | tf_op jit(solution)/shard_map/ppermute | solution.py:420
  75.5 11.7 %collective-permute-start.25 = (bf16[144,1120]{1,0:T(8,128)(2,1)S(1)}, bf16[144,1120]{1,0:T(8,128)(2,1)S(1)}, u32[]{:S(2)}, u32[]{:S(2)}) collective-permute-start(bf16[144,1120]{1,0:T(8,128)(2,1)S(1)} %collective-permute-done.15.refs_3_.refs_10_), channel_id=1, source_target_pairs={{0,1},{1,0},{2,3},{3,2},{4,5},{5,4},{6,7},{7,6},{8,9},{9,8},{10,11... | collective-permute-start | bytes 967688 | tf_op jit(solution)/shard_map/ppermute | solution.py:454
  82.5 5.9 %collective-permute-start.26 = (bf16[144,1120]{1,0:T(8,128)(2,1)S(1)}, bf16[144,1120]{1,0:T(8,128)(2,1)S(1)}, u32[]{:S(2)}, u32[]{:S(2)}) collective-permute-start(bf16[144,1120]{1,0:T(8,128)(2,1)S(1)} %collective-permute-done.16.refs_5_.refs_12_), channel_id=1, source_target_pairs={{0,1},{1,0},{2,3},{3,2},{4,5},{5,4},{6,7},{7,6},{8,9},{9,8},{10,11... | collective-permute-start | bytes 967688 | tf_op jit(solution)/shard_map/ppermute | solution.py:454
  82.6 5.9 %collective-permute-start.27 = (bf16[144,1120]{1,0:T(8,128)(2,1)S(1)}, bf16[144,1120]{1,0:T(8,128)(2,1)S(1)}, u32[]{:S(2)}, u32[]{:S(2)}) collective-permute-start(bf16[144,1120]{1,0:T(8,128)(2,1)S(1)} %collective-permute-done.18.refs_7_.refs_14_), channel_id=1, source_target_pairs={{0,1},{1,0},{2,3},{3,2},{4,5},{5,4},{6,7},{7,6},{8,9},{9,8},{10,11... | collective-permute-start | bytes 967688 | tf_op jit(solution)/shard_map/ppermute | solution.py:454
  83.0 5.5 %collective-permute-start.28 = (bf16[144,1120]{1,0:T(8,128)(2,1)S(1)}, bf16[144,1120]{1,0:T(8,128)(2,1)S(1)}, u32[]{:S(2)}, u32[]{:S(2)}) collective-permute-start(bf16[144,1120]{1,0:T(8,128)(2,1)S(1)} %collective-permute-done.19.refs_9_.refs_16_), channel_id=1, source_target_pairs={{0,1},{1,0},{2,3},{3,2},{4,5},{5,4},{6,7},{7,6},{8,9},{9,8},{10,11... | collective-permute-start | bytes 967688 | tf_op jit(solution)/shard_map/ppermute | solution.py:454
  86.6 9.1 %collective-permute-start.31 = (bf16[144,1120]{1,0:T(8,128)(2,1)S(1)}, bf16[144,1120]{1,0:T(8,128)(2,1)S(1)}, u32[]{:S(2)}, u32[]{:S(2)}) collective-permute-start(bf16[144,1120]{1,0:T(8,128)(2,1)S(1)} %collective-permute-done.21.refs_4_.refs_20_), channel_id=1, source_target_pairs={{0,1},{1,0},{2,3},{3,2},{4,5},{5,4},{6,7},{7,6},{8,9},{9,8},{10,11... | collective-permute-start | bytes 967688 | tf_op jit(solution)/shard_map/ppermute | solution.py:454
  87.2 6.8 %collective-permute-start.24 = (bf16[560,128]{1,0:T(8,128)(2,1)S(1)}, bf16[560,128]{1,0:T(8,128)(2,1)S(1)}, u32[]{:S(2)}, u32[]{:S(2)}) collective-permute-start(bf16[560,128]{1,0:T(8,128)(2,1)S(1)} %pad_maximum_fusion.2), channel_id=1, source_target_pairs={{0,4},{2,6},{4,8},{6,10},{8,12},{10,14},{1,5},{3,7},{5,9},{7,11},{... | collective-permute-start | bytes 430088 | tf_op jit(solution)/shard_map/ppermute | solution.py:420
  92.8 2.9 %collective-permute-start.30 = (bf16[144,1120]{1,0:T(8,128)(2,1)S(1)}, bf16[144,1120]{1,0:T(8,128)(2,1)S(1)}, u32[]{:S(2)}, u32[]{:S(2)}) collective-permute-start(bf16[144,1120]{1,0:T(8,128)(2,1)S(1)} %collective-permute-done.20.refs_2_.refs_18_), channel_id=1, source_target_pairs={{0,1},{1,0},{2,3},{3,2},{4,5},{5,4},{6,7},{7,6},{8,9},{9,8},{10,11... | collective-permute-start | bytes 967688 | tf_op jit(solution)/shard_map/ppermute | solution.py:454
  93.3 2.4 %collective-permute-start.32 = (bf16[144,1120]{1,0:T(8,128)(2,1)S(1)}, bf16[144,1120]{1,0:T(8,128)(2,1)S(1)}, u32[]{:S(2)}, u32[]{:S(2)}) collective-permute-start(bf16[144,1120]{1,0:T(8,128)(2,1)S(1)} %collective-permute-done.23.refs_6_.refs_22_), channel_id=1, source_target_pairs={{0,1},{1,0},{2,3},{3,2},{4,5},{5,4},{6,7},{7,6},{8,9},{9,8},{10,11... | collective-permute-start | bytes 967688 | tf_op jit(solution)/shard_map/ppermute | solution.py:454
  94.4 6.7 %collective-permute-start.29 = (bf16[560,128]{1,0:T(8,128)(2,1)S(1)}, bf16[560,128]{1,0:T(8,128)(2,1)S(1)}, u32[]{:S(2)}, u32[]{:S(2)}) collective-permute-start(bf16[560,128]{1,0:T(8,128)(2,1)S(1)} %pad_maximum_fusion.3), channel_id=1, source_target_pairs={{0,8},{2,10},{4,12},{6,14},{1,9},{3,11},{5,13},{7,15},{16,24},{18,... | collective-permute-start | bytes 430088 | tf_op jit(solution)/shard_map/ppermute | solution.py:420
  101.7 6.6 %collective-permute-start.33 = (f32[560,128]{1,0:T(8,128)S(1)}, f32[560,128]{1,0:T(8,128)S(1)}, u32[]{:S(2)}, u32[]{:S(2)}) collective-permute-start(f32[560,128]{1,0:T(8,128)S(1)} %pad_maximum_fusion.mine_ref), channel_id=1, source_target_pairs={{0,1},{1,0},{2,3},{3,2},{4,5},{5,4},{6,7},{7,6},{8,9},{9,8},{10,11... | collective-permute-start | bytes 860168 | tf_op jit(solution)/shard_map/ppermute | solution.py:454

commit v3 on v2

v3 whole, which is shorter than its diff:
```python
import functools

import jax
import jax.numpy as jnp
import numpy as np
from jax import lax
from jax.experimental import pallas as pl
from jax.experimental.pallas import tpu as pltpu
from jax.sharding import PartitionSpec as P

HEADS = 10
HEAD = 112
LANES = 128
DEPTH = 256
BF = jnp.bfloat16
F32 = jnp.float32
LIMIT = 16 * 1024 * 1024


def ceil_to(value, step):
    return -(-value // step) * step


def dot(a, b):
    return jnp.dot(a, b, preferred_element_type=F32)


def params():
    return pltpu.CompilerParams(vmem_limit_bytes=LIMIT, dimension_semantics=("arbitrary",))


def cost(flops, moved):
    return pl.CostEstimate(flops=int(flops), bytes_accessed=int(moved), transcendentals=0)


def whole(shape):
    return pl.BlockSpec(shape, lambda i, *_: (0,) * len(shape))


def ring_order(count):
    if count % 2:
        return list(range(count))
    return list(range(0, count, 2)) + list(range(count - 1, 0, -2))


def slot_table(count):
    order = ring_order(count)
    up, down = count // 2, (count - 1) // 2
    table = np.zeros((count, count), np.int32)
    for at, index in enumerate(order):
        slots = [0]
        for step in range(1, up + 1):
            slots.append(-step)
            if step <= down:
                slots.append(step)
        table[index] = [order[(at + s) % count] for s in slots]
    return table


def split_rows(rows):
    third = DEPTH // 48 * 16
    spare = ceil_to((rows - DEPTH + 1) // 2, 16)
    return third, DEPTH - 2 * third, spare


def resident(kernel, meta, operands, outs, scratch, flops, name, aliases=None):
    in_vmem = pl.BlockSpec(memory_space=pltpu.VMEM)
    return pl.pallas_call(
        kernel,
        in_specs=[pl.BlockSpec(memory_space=pltpu.SMEM)] + [in_vmem] * len(operands),
        out_specs=[in_vmem] * len(outs),
        out_shape=outs,
        scratch_shapes=scratch,
        input_output_aliases=aliases or {},
        compiler_params=pltpu.CompilerParams(vmem_limit_bytes=LIMIT),
        cost_estimate=cost(flops, 0),
        name=name,
    )(meta, *operands)


def key_value_columns(meta, heads_here, run):
    wide, model = heads_here * HEAD, HEADS * HEAD

    def on_core(core):
        for part in (1, 2):
            begin = part * model + core * wide
            run(slice(begin, begin + wide), slice((part - 1) * wide, part * wide))

    for core in range(HEADS // heads_here):
        pl.when(meta[1] == core)(functools.partial(on_core, core))


def pack_first_kernel(meta, w_ref, up_ref, down_ref, *, heads_here):
    rows = w_ref.shape[0]
    third, shared, spare = split_rows(rows)
    own, other = (pl.ds(pl.multiple_of(p * third, 16), third) for p in (meta[0], 1 - meta[0]))
    end = up_ref.shape[0]
    blank = 2 * spare - (rows - DEPTH)
    common = shared + 2 * spare
    for ref, at in ((up_ref, end - blank), (down_ref, common - blank)):
        ref[at : at + blank, :] = jnp.zeros((blank, ref.shape[1]), BF)

    def run(of, to):
        for ref, take, at, common_at in ((up_ref, own, 0, third), (down_ref, other, common, 0)):
            ref[at : at + third, to] = w_ref[take, of]
            ref[common_at : common_at + common - blank, to] = w_ref[2 * third :, of]

    key_value_columns(meta, heads_here, run)


def pack_rest_kernel(meta, w_ref, after_ref, mine_ref, theirs_ref):
    rows = w_ref.shape[0]
    spare = split_rows(rows)[2]
    half, model = DEPTH // 2, HEADS * HEAD

    def queries(out_ref, core):
        out_ref[:half, :] = w_ref[core * half : (core + 1) * half, :model]
        out_ref[half:, :] = jnp.zeros((spare, model), BF)
        begin = DEPTH + core * spare
        count = min(spare, rows - begin)
        out_ref[half : half + count, :] = w_ref[begin : begin + count, :model]

    for core in range(2):
        pl.when(meta[1] == core)(functools.partial(queries, mine_ref, core))
        pl.when(meta[1] == 1 - core)(functools.partial(queries, theirs_ref, core))


def pack_first(meta, w, heads_here):
    third, shared, spare = split_rows(w.shape[0])
    out = jax.ShapeDtypeStruct((third + shared + 2 * spare, 2 * heads_here * HEAD), BF)
    kernel = functools.partial(pack_first_kernel, heads_here=heads_here)
    return resident(kernel, meta, [w], [out] * 2, [], 1e9, "pack_first")


def pack_rest(meta, w, after):
    half = DEPTH // 2 + split_rows(w.shape[0])[2]
    outs = [jax.ShapeDtypeStruct((half, HEADS * HEAD), BF)] * 2
    return resident(pack_rest_kernel, meta, [w, after], outs, [], 1e9, "pack_rest")


def pack_tokens_kernel(x_ref, after_ref, o_ref, *, rows, count):
    spare = split_rows(rows)[2]
    rest = rows - DEPTH
    blank = jnp.zeros((x_ref.shape[0], 2 * spare - rest), x_ref.dtype)
    left_over = []
    for j in range(count):
        at = j * rows
        o_ref[:, j * DEPTH : (j + 1) * DEPTH] = x_ref[:, at : at + DEPTH]
        left_over += [x_ref[:, at + DEPTH : at + rows], blank]
    o_ref[:, count * DEPTH :] = jnp.concatenate(left_over, axis=1)


def pack_tokens(x, after, rows, count, block):
    tokens, channels = x.shape
    depth = count * (DEPTH + 2 * split_rows(rows)[2])
    return pl.pallas_call(
        functools.partial(pack_tokens_kernel, rows=rows, count=count),
        grid=(tokens // block,),
        in_specs=[
            pl.BlockSpec((block, channels), lambda i: (i, 0)),
            pl.BlockSpec(memory_space=pl.ANY),
        ],
        out_specs=pl.BlockSpec((block, depth), lambda i: (i, 0)),
        out_shape=jax.ShapeDtypeStruct((tokens, depth), BF),
        compiler_params=params(),
        cost_estimate=cost(0, 4 * x.size),
        name="pack_tokens",
    )(x, after)


def put(weights, at, step, value):
    weights[pl.ds(pl.multiple_of(at, step), value.shape[0]), :] = value


def put_rows(weights, at, piece, begin, end):
    offset = 0
    for ref, first, count in piece:
        low, high = max(begin, offset), min(end, offset + count)
        if low < high:
            put(weights, at + low - begin, 16, ref[first + low - offset : first + high - offset, :])
        offset += count


def fill_keys_values(weights, meta, slots, pieces, rows):
    third, shared, _ = split_rows(rows)
    for s in range(len(slots)):
        own, other, common = pieces[3 * s : 3 * s + 3]
        put_rows(weights, s * DEPTH + meta[0] * third, own, 0, third)
        put_rows(weights, s * DEPTH + (1 - meta[0]) * third, other, 0, third)
        put_rows(weights, s * DEPTH + 2 * third, common, 0, shared)


def fill_queries(weights, meta, slots, pieces, rows):
    half = DEPTH // 2
    for s in range(len(slots)):
        for piece, core in zip(pieces[2 * s : 2 * s + 2], (meta[1], 1 - meta[1])):
            put_rows(weights, s * DEPTH + core * half, piece, 0, half)


def fill_left_over(weights, meta, base, pieces, rows, of_keys):
    third, shared, spare = split_rows(rows)
    if of_keys:
        for s, piece in enumerate(pieces):
            at = base + meta[2 + s] * 2 * spare
            put_rows(weights, at, piece, shared, shared + 2 * spare)
        return
    half = DEPTH // 2
    for s in range(len(pieces) // 2):
        for piece, core in zip(pieces[2 * s : 2 * s + 2], (meta[1], 1 - meta[1])):
            put_rows(weights, base + (meta[2 + s] * 2 + core) * spare, piece, half, half + spare)


def token_columns(x_ref, rows, meta, slots, count, with_rest):
    taken = [x_ref[rows, pl.ds(pl.multiple_of(meta[2 + s] * DEPTH, DEPTH), DEPTH)] for s in slots]
    if with_rest:
        taken.append(x_ref[rows, count * DEPTH :])
    return jnp.concatenate(taken, axis=1)


def every_block(xs, block, run):
    tokens = xs[0].shape[0]
    for band, x_ref in enumerate(xs):

        def step(i, carry, band=band, x_ref=x_ref):
            at = pl.multiple_of(i * block, block)
            run(x_ref, pl.ds(at, block), pl.ds(pl.multiple_of(at + band * tokens, block), block))
            return carry

        lax.fori_loop(0, tokens // block, step, 0)


def project_kernel(meta, *refs, plan, where, finish):
    bands_in, slots, count, rows, of_keys, has_acc, with_rest, block = plan
    xs, refs = refs[:bands_in], refs[bands_in:]
    acc_ref, refs = (refs[0], refs[1:]) if has_acc else (None, refs)
    pieces, rest_pieces = (
        [[(refs[i], at, n) for i, at, n in piece] for piece in pieces] for pieces in where
    )
    refs = refs[1 + max(i for pieces in where for piece in pieces for i, _, _ in piece) :]
    weights, refs = refs[-1], refs[:-1]
    (fill_keys_values if of_keys else fill_queries)(weights, meta, slots, pieces, rows)
    if with_rest:
        fill_left_over(weights, meta, len(slots) * DEPTH, rest_pieces, rows, of_keys)

    def run(x_ref, rows_here, rows_of_all):
        x = token_columns(x_ref, rows_here, meta, slots, count, with_rest)
        total = dot(x, weights[...])
        if has_acc:
            total = total + acc_ref[rows_of_all, :]
        finish(refs, total, rows_of_all)

    every_block(xs, block, run)


def keep(refs, total, rows):
    refs[0][rows, :] = total


def keep_features(refs, total, rows):
    refs[0][rows, :] = jnp.maximum(total.astype(BF), 0)


def distinct(*lists):
    arrays, places = [], {}
    for array, _, _ in (part for pieces in lists for piece in pieces for part in piece):
        if id(array) not in places:
            places[id(array)] = len(arrays)
            arrays.append(array)
    where = tuple(
        tuple(tuple((places[id(a)], at, n) for a, at, n in piece) for piece in pieces)
        for pieces in lists
    )
    return arrays, where


def project(meta, xs, acc, pieces, rest_pieces, plan, finish, out, name):
    bands_in, slots, count, rows, of_keys, has_acc, with_rest, block = plan
    arrays, where = distinct(pieces, rest_pieces)
    wide = arrays[0].shape[1]
    depth = len(slots) * DEPTH + with_rest * count * 2 * split_rows(rows)[2]
    tokens = bands_in * xs[0].shape[0]
    operands = [*xs, *([acc] if has_acc else []), *arrays]
    in_place = has_acc and out.shape == acc.shape and out.dtype == acc.dtype
    return resident(
        functools.partial(project_kernel, plan=plan, where=where, finish=finish),
        meta,
        operands,
        [out],
        [pltpu.VMEM((depth, wide), BF)],
        2 * tokens * depth * wide,
        name,
        {1 + bands_in: 0} if in_place else None,
    )[0]


def states_kernel(meta, *refs, plan, where, heads_here):
    out_ref, values, weights = refs[-3:]
    wide = heads_here * HEAD
    values[...] = jnp.ones_like(values)
    out_ref[...] = jnp.zeros_like(out_ref)

    def finish(_, projected, rows):
        projected = projected.astype(BF)
        feats = jnp.maximum(projected[:, :wide], 0).T
        for h in range(heads_here):
            rows = slice(h * HEAD, (h + 1) * HEAD)
            values[:, :HEAD] = projected[:, wide + h * HEAD : wide + (h + 1) * HEAD]
            out_ref[rows, :] += dot(feats[rows, :], values[...])

    project_kernel(meta, *refs, plan=plan, where=where, finish=finish)


def block_states(meta, xs, acc, pieces, rest_pieces, plan, heads_here):
    wide = heads_here * HEAD
    bands_in, slots, count, rows, _, has_acc, with_rest, block = plan
    depth = len(slots) * DEPTH + with_rest * count * 2 * split_rows(rows)[2]
    tokens = bands_in * xs[0].shape[0]
    arrays, where = distinct(pieces, rest_pieces)
    return resident(
        functools.partial(states_kernel, plan=plan, where=where, heads_here=heads_here),
        meta,
        [*xs, acc, *arrays],
        [jax.ShapeDtypeStruct((wide, LANES), F32)],
        [
            pltpu.VMEM((block, LANES), BF),
            pltpu.VMEM((depth, 2 * wide), BF),
        ],
        2 * tokens * (depth * 2 * wide + wide * LANES),
        "states",
    )[0]


def bands():
    model = HEADS * HEAD
    found = []
    for left in range(0, model, 256):
        right = min(left + 256, model)
        heads = range(left // HEAD, -(-right // HEAD))
        low = heads[0] * HEAD // LANES * LANES
        high = min(ceil_to((heads[-1] + 1) * HEAD, LANES), model)
        found.append((left, right, low, high, heads))
    return found


def attend_kernel(
    meta, q_ref, mine_ref, theirs_ref, out_hbm, states, sums, held, sems, *, heads_here
):
    states[...] = jnp.zeros_like(states)
    mine, theirs = mine_ref[...], theirs_ref[...]
    parts = [jnp.where(meta[1] == k, mine, theirs) for k in range(HEADS // heads_here)]
    base = 0
    for left, right, low, high, heads in bands():
        for h in heads:
            at = (h % heads_here) * HEAD
            begin, end = max(h * HEAD, left), min((h + 1) * HEAD, right)
            rows = slice(base + h * HEAD - low, base + (h + 1) * HEAD - low)
            block = parts[h // heads_here][at : at + HEAD, begin - h * HEAD : end - h * HEAD]
            states[rows, begin - left : end - left] = block.astype(BF)
        base += high - low
    lane = lax.broadcasted_iota(jnp.int32, (HEAD, LANES), 1)
    for h in range(HEADS):
        at = (h % heads_here) * HEAD
        key_sums = parts[h // heads_here][at : at + HEAD, HEAD : HEAD + 1]
        key_sums = jnp.broadcast_to(key_sums, (HEAD, LANES))
        upper = key_sums.astype(BF).astype(F32)
        chosen = jnp.where(lane == h, upper, jnp.where(lane == h + 64, key_sums - upper, 0.0))
        sums[h * HEAD : (h + 1) * HEAD, :] = chosen.astype(BF)
    blocks, block = held.shape[0], held.shape[1]
    column = lax.broadcasted_iota(jnp.int32, (block, LANES), 1)
    shares = []
    for i in range(blocks):
        total = dot(q_ref[i * block : (i + 1) * block, :], sums[...])
        shares.append(1.0 / (total + pltpu.roll(total, 64, 1) + 1.0))

    def send(i):
        return pltpu.make_async_copy(held.at[i], out_hbm.at[pl.ds(i * block, block)], sems.at[i])

    for i in range(blocks):
        base = 0
        for left, right, low, high, _ in bands():
            q = q_ref[i * block : (i + 1) * block, low:high]
            numerator = dot(q, states[base : base + high - low, :])
            for at in range(left, right, LANES):
                width = min(LANES, right - at)
                head = sum((column + at >= h * HEAD).astype(jnp.int32) for h in range(1, HEADS))
                scale = jnp.take_along_axis(shares[i], head, axis=1)
                scaled = (numerator[:, at - left : at - left + LANES] * scale).astype(BF)
                held[i, :, at : at + width] = scaled[:, :width]
            base += high - low
        send(i).start()
    for i in range(blocks):
        send(i).wait()


def attend(meta, queries, mine, theirs, heads_here, block):
    tokens, model = queries.shape
    rows = sum(high - low for _, _, low, high, _ in bands())
    in_vmem = pl.BlockSpec(memory_space=pltpu.VMEM)
    return pl.pallas_call(
        functools.partial(attend_kernel, heads_here=heads_here),
        in_specs=[pl.BlockSpec(memory_space=pltpu.SMEM)] + [in_vmem] * 3,
        out_specs=pl.BlockSpec(memory_space=pl.ANY),
        scratch_shapes=[
            pltpu.VMEM((rows, 256), BF),
            pltpu.VMEM((model, LANES), BF),
            pltpu.VMEM((tokens // block, block, model), BF),
            pltpu.SemaphoreType.DMA((tokens // block,)),
        ],
        out_shape=jax.ShapeDtypeStruct((tokens, model), BF),
        compiler_params=pltpu.CompilerParams(vmem_limit_bytes=LIMIT),
        cost_estimate=cost(2 * tokens * model * 800, tokens * model * 4),
        name="attend",
    )(meta, queries, mine, theirs)


def swap_pairs(count):
    return [(i, i ^ 1) for i in range(count)]


def ring_steps(count):
    order = ring_order(count)
    forward = [(order[i], order[(i + 1) % count]) for i in range(count)]
    return forward, [(b, a) for a, b in forward]


def running_total(states, sums, count, alongside=None):
    reach, hop = 1, 0
    wide, room = states.shape[-1], sums.shape[-1]
    while reach < count:
        pairs = [(i, i + reach) for i in range(count - reach)]
        upper = sums.astype(BF)
        lower = (sums - upper.astype(F32)).astype(BF)
        sent = jnp.concatenate([states.astype(BF), upper, lower], axis=-1)
        got = lax.ppermute(sent, "tm", pairs)
        if alongside is not None:
            got = alongside(hop, got)
        got = got.astype(F32)
        states = states + got[..., :wide]
        sums = sums + (got[..., wide : wide + room] + got[..., wide + room :])
        reach, hop = reach * 2, hop + 1
    return states, sums


def tie(*values):
    return lax.optimization_barrier(values)


def ring_form(latents, proj_weight):
    frame_count, band_rows, column_count, channels = latents.shape
    rows = proj_weight.shape[0]
    third, shared, spare = split_rows(rows)
    common_rows = shared + 2 * spare
    count, groups = lax.axis_size("tm"), lax.axis_size("groups")
    heads_here = HEADS // 2
    tokens = frame_count * band_rows * column_count
    block = 960 if tokens % 960 == 0 else tokens
    small = 240 if tokens % 240 == 0 else tokens

    forward, backward = ring_steps(count)
    across, over = swap_pairs(groups), swap_pairs(2)
    last = count // 2

    def ring(value, up):
        return lax.ppermute(value, "tm", forward if up else backward)

    def plane_swap(up, down):
        value = jnp.concatenate([up[:third], down[common_rows:]], axis=0)
        return lax.ppermute(value, "groups", across)

    def core_swap(value):
        return lax.ppermute(value, "space", over)

    here = jnp.asarray(slot_table(count))[lax.axis_index("tm")]
    plane = lax.rem(lax.axis_index("groups"), 2)
    meta = jnp.concatenate([jnp.stack([plane, lax.axis_index("space")]), here]).astype(jnp.int32)

    up, down = pack_first(meta, proj_weight, heads_here)
    mine, theirs = pack_rest(meta, proj_weight, up)
    x = pack_tokens(latents.reshape(tokens, channels), mine, rows, count, small)

    ways = [(mine, mine)]
    half = DEPTH // 2 + spare
    mid = half // 2 // 16 * 16 + 16

    def next_queries():
        if len(ways) < last:
            ways.append((ring(ways[-1][0], True), ring(ways[-1][1], False)))
        elif len(ways) == last:
            ways.append((ring(ways[-1][0][:mid], True), ring(ways[-1][1][mid:], False)))

    def with_queries(*values):
        *values, up, down = tie(*values, *ways[-1])
        ways[-1] = up, down
        next_queries()
        return values

    def plan(bands_in, which, of_keys, has_acc, with_rest):
        return (bands_in, tuple(which), count, rows, of_keys, has_acc, with_rest, block)

    kv_shape = jax.ShapeDtypeStruct((2 * tokens, 2 * heads_here * HEAD), F32)

    def add_keys_values(acc, which):
        pieces = [part for s in which for part in slots[s]]
        settings = plan(2, which, True, acc is not None, False)
        return project(meta, both, acc, pieces, [], settings, keep, kv_shape, "kv_part")

    def thirds(up, down, up_other, down_other):
        common_up, common_down = [(up, third, common_rows)], [(down, 0, common_rows)]
        return [
            [[(up, 0, third)], [up_other], common_up],
            [[down_other], [(down, common_rows, third)], common_down],
        ]

    slots = thirds(up, down, (down, common_rows, third), (up, 0, third))[:1]
    some = common_rows // 2 // 16 * 16
    swapped, acc = None, None
    for step in range(1, last + 1):
        before = up, down
        full = step < last
        up = ring(up if full else up[: third + some], True)
        down = ring(down if full else down[some:], False)
        if step == 1:
            x = tie(x, up, down)[0]
            x_other = core_swap(x)
            both = (x, x_other)
        elif full:
            x_other, up, down, swapped = tie(x_other, up, down, swapped)
            both = (x, x_other)
        else:
            acc = add_keys_values(None, range(len(slots)))
            acc, up, down, swapped = with_queries(acc, up, down, swapped)
        if step > 1:
            slots += thirds(*before, (swapped, 0, third), (swapped, third, third))
        if full:
            swapped = plane_swap(up, down)
        if step + 1 == last:
            next_queries()
    rest = common_rows - some
    slots.append([[(up, 0, third)], [(down, rest, third)], [(up, third, some), (down, 0, rest)]])
    settings = plan(2, range(count - 3, count), True, True, True)
    pieces = [piece for slot in slots[count - 3 :] for piece in slot]
    commons = [slot[2] for slot in slots]
    payload = block_states(meta, both, acc, pieces, commons, settings, heads_here)
    (payload,) = with_queries(payload)

    found = [[[(mine, 0, half)], [(theirs, 0, half)]]]
    cut = 1 + 2 * ((count - 1) // 4 + (count > 4))

    def query_slots(step):
        if step < last:
            for value in ways[step]:
                found.append([[(value, 0, half)], [(core_swap(value), 0, half)]])
        else:
            value = jnp.concatenate(ways[step], axis=0)
            found.append([[(value, 0, half)], [(core_swap(value), 0, half)]])

    def project_queries(acc, which, finish, dtype, name):
        ends = which[-1] == count - 1
        pieces = [part for s in which for part in found[s]]
        every = [part for s in found for part in s] if ends else []
        settings = plan(1, which, False, acc is not None, ends)
        out = jax.ShapeDtypeStruct((tokens, HEADS * HEAD), dtype)
        return project(meta, (x,), acc, pieces, every, settings, finish, out, name)

    held = {}

    def alongside(hop, got):
        if hop == 0:
            query_slots(1)
            query_slots(2)
            (got,) = with_queries(got)
        if hop == 1:
            early = project_queries(None, range(cut), keep, F32, "q_early")
            query_slots(3)
            got, held["q"] = tie(got, early)
        if hop == 2:
            query_slots(4)
            late = project_queries(held["q"], range(cut, count), keep_features, BF, "q_late")
            got, held["q"] = tie(got, late)
        return got

    states, sums = payload[:, :HEAD], payload[:, HEAD : HEAD + 8]
    total = jnp.concatenate([*running_total(states, sums, count, alongside), sums], axis=1)
    out = attend(meta, held["q"], total, core_swap(total), heads_here, small)
    return out.reshape(frame_count, band_rows, column_count, HEADS * HEAD)


def gathered_form(latents, proj_weight):
    frame_count, band_rows, column_count, channels = latents.shape
    shard_rows = proj_weight.shape[0]
    band_count, band = lax.axis_size("space"), lax.axis_index("space")
    heads_here = HEADS // band_count
    own = proj_weight.reshape(shard_rows, 3, band_count, heads_here * HEAD)
    own = lax.dynamic_index_in_dim(own, band, 2, keepdims=False)
    own = own.reshape(shard_rows, 3 * heads_here * HEAD)
    weight = lax.all_gather(own, "tm", axis=0, tiled=True)
    tokens = lax.all_gather(latents, "space", axis=1, tiled=True)
    joined = tokens.shape[1]
    projected = dot(tokens.reshape(-1, channels), weight).astype(BF)
    split = projected.reshape(-1, 3, heads_here, HEAD)
    queries, feats, values = jax.nn.relu(split[:, 0]), jax.nn.relu(split[:, 1]), split[:, 2]
    states = jnp.einsum("nhe,nhf->hef", feats, values, preferred_element_type=F32)
    key_sums = jnp.sum(feats, axis=0, dtype=F32)
    states, key_sums = running_total(states, key_sums[:, :, None], lax.axis_size("tm"))
    states, key_sums = states.astype(BF), key_sums[:, :, 0]
    numerator = jnp.einsum("nhe,hef->nhf", queries, states, preferred_element_type=F32)
    denominator = jnp.einsum(
        "nhe,he->nh", queries.astype(F32), key_sums, precision=lax.Precision.HIGHEST
    )
    out = (numerator / (denominator[:, :, None] + 1.0)).astype(BF)
    out = out.reshape(frame_count, joined, column_count, heads_here * HEAD)
    return lax.all_to_all(out, "space", split_axis=1, concat_axis=3, tiled=True)


def on_device(latents, proj_weight):
    even = lax.axis_size("groups") % 2 == 0 and lax.axis_size("space") == 2
    if even and proj_weight.shape[0] // DEPTH == 1 and lax.axis_size("tm") == 8:
        return ring_form(latents, proj_weight)
    return gathered_form(latents, proj_weight)


def solution(mesh):
    return jax.shard_map(
        on_device,
        mesh=mesh,
        in_specs=(P(("groups", "tm"), "space", None, None), P("tm", None)),
        out_specs=P(("groups", "tm"), "space", None, None),
        check_vma=False,
    )
```

time: 114 us -> 113 us (level)
  waiting for transfers between devices: 31.6 us -> 45.3 us
  starting transfers between devices: 40.5 us -> 30.5 us
  Pallas kernels: 37.2 us -> 31.7 us
    ppermute x15 -> x16, waiting for transfers between devices: 11.5 us -> 19.3 us  [ring(): return lax.ppermute(value, 'tm', forward if up else backward)]
    ppermute x9, starting transfers between devices: 18.8 us -> 11.7 us  [core_swap(): return lax.ppermute(value, 'space', over)]
    ppermute x3, waiting for transfers between devices: 2.21 us -> 8.61 us  [running_total(): got = lax.ppermute(sent, 'tm', pairs)]
    ppermute x7 -> x3, starting transfers between devices: 5.05 us -> 0.96 us  [plane_swap(): return lax.ppermute(value, 'groups', across)]
    pallas_call x7 -> x6, Pallas kernels: 28.8 us -> 24.8 us  [resident(): pl.pallas_call(kernel, in_specs=[pl.BlockSpec(memory_space=pltpu.SMEM)] +...]
    ppermute x15 -> x16, starting transfers between devices: 10.6 us -> 12.7 us  [ring(): return lax.ppermute(value, 'tm', forward if up else backward)]
    pallas_call x1, Pallas kernels: 5.85 us -> 4.35 us  [attend(): pl.pallas_call(functools.partial(attend_kernel, heads_here=heads_here), i...]
    ppermute x7 -> x3, waiting for transfers between devices: 16.6 us -> 16.2 us  [plane_swap(): return lax.ppermute(value, 'groups', across)]
  transfers between devices with their start and end apart: 34 -> 31, of which waited for: 11 -> 11; matrix products, arithmetic and copies ran while one was open for 1% -> 1% of each run, Pallas kernels for 27% -> 23%
where the time goes in v3:
time: 113 us
  waiting for transfers between devices  45.3 us (40%)
  Pallas kernels  31.7 us (28%)
  starting transfers between devices  30.5 us (27%)
  local copies, waits for them, and re-layouts  2.83 us (3%)
  other arithmetic  1.99 us (2%)
    pallas_call x6, Pallas kernels, resident(): pl.pallas_call(kernel, in_specs=[pl.BlockSpec(memory_space=pltpu.SMEM)] +...  24.8 us
    ppermute x16, waiting for transfers between devices, ring(): return lax.ppermute(value, 'tm', forward if up else backward)  19.3 us
    ppermute x3, waiting for transfers between devices, plane_swap(): return lax.ppermute(value, 'groups', across)  16.2 us
    ppermute x16, starting transfers between devices, ring(): return lax.ppermute(value, 'tm', forward if up else backward)  12.7 us
    ppermute x9, starting transfers between devices, core_swap(): return lax.ppermute(value, 'space', over)  11.7 us
    ppermute x3, waiting for transfers between devices, running_total(): got = lax.ppermute(sent, 'tm', pairs)  8.61 us
    ppermute x3, starting transfers between devices, running_total(): got = lax.ppermute(sent, 'tm', pairs)  5.14 us
    pallas_call x1, Pallas kernels, attend(): pl.pallas_call(functools.partial(attend_kernel, heads_here=heads_here), i...  4.35 us
  transfers between devices with their start and end apart: 31, of which 11 were waited for; matrix products, arithmetic and copies ran while one was open for 1% of the time, Pallas kernels for 23%

profile of v3, /device:TPU:27, one launch (start us, length us, event | category | flops | bytes accessed | tf_op | source)
XLA Modules:
  0.0 112.8 jit_solution(16896131655048975637)
XLA Ops:
  0.0 0.8 dynamic-slice_bitcast_fusion
  0.9 1.8 %copy-done.1 = bf16[280,3360]{1,0:T(8,128)(2,1)S(1)} copy-done((bf16[280,3360]{1,0:T(8,128)(2,1)S(1)}, bf16[280,3360]{1,0:T(8,128)(2,1)}, u32[]{:S(2)}) %copy-start.1) | copy-done | bytes 1881624
  2.7 0.9 pack_first.1
  3.6 1.3 %collective-permute-start = (bf16[208,1120]{1,0:T(8,128)(2,1)S(1)}, bf16[208,1120]{1,0:T(8,128)(2,1)S(1)}, u32[]{:S(2)}, u32[]{:S(2)}) collective-permute-start(bf16[208,1120]{1,0:T(8,128)(2,1)S(1)} %get-tuple-element.34.after_ref.refs_2_.refs_8_), channel_id=1, source_target_pairs={{0,4},{4,8},{8,12},{12,14},{14,10},{10,6},{6,2},{2,0},{1,5},{5,9},... | collective-permute-start | bytes 1397768 | tf_op jit(solution)/shard_map/ppermute | solution.py:464
  4.9 0.2 collective-permute-start.1
  5.1 0.6 pack_rest.1
  5.8 2.6 %pack_tokens.1.refs_0_ = bf16[960,2304]{1,0:T(8,128)(2,1)S(1)} custom-call(bf16[960,2240]{1,0:T(8,128)(2,1)S(1)} %bitcast.6, bf16[144,1120]{1,0:T(8,128)(2,1)S(1)} %get-tuple-element.35.after_ref.refs_1_.refs_8_), custom_call_target="tpu_custom_call" | custom-call | bytes 8601600 | tf_op jit(solution)/shard_map/pack_tokens/pallas_call | solution.py:156
  8.4 7.1 %collective-permute-done.refs_4_.refs_9_ = bf16[208,1120]{1,0:T(8,128)(2,1)S(1)} collective-permute-done((bf16[208,1120]{1,0:T(8,128)(2,1)S(1)}, bf16[208,1120]{1,0:T(8,128)(2,1)S(1)}, u32[]{:S(2)}, u32[]{:S(2)}) %collective-permute-start) | collective-permute-done | bytes 465952 | tf_op jit(solution)/shard_map/ppermute | solution.py:464
  15.5 0.9 collective-permute-done.1.refs_6_.refs_10_
  16.4 1.9 %collective-permute-start.2 = (bf16[960,2304]{1,0:T(8,128)(2,1)S(1)}, bf16[960,2304]{1,0:T(8,128)(2,1)S(1)}, u32[]{:S(2)}, u32[]{:S(2)}) collective-permute-start(bf16[960,2304]{1,0:T(8,128)(2,1)S(1)} %pack_tokens.1.refs_0_), channel_id=1, source_target_pairs={{0,1},{1,0},{2,3},{3,2},{4,5},{5,4},{6,7},{7,6},{8,9},{9,8},{10,11... | collective-permute-start | bytes 13271048 | tf_op jit(solution)/shard_map/ppermute | solution.py:471
  18.5 1.3 %collective-permute-start.4 = (bf16[208,1120]{1,0:T(8,128)(2,1)S(1)}, bf16[208,1120]{1,0:T(8,128)(2,1)S(1)}, u32[]{:S(2)}, u32[]{:S(2)}) collective-permute-start(bf16[208,1120]{1,0:T(8,128)(2,1)S(1)} %collective-permute-done.1.refs_6_.refs_10_), channel_id=1, source_target_pairs={{4,0},{8,4},{12,8},{14,12},{10,14},{6,10},{2,6},{0,2},{5,1},{9,5},... | collective-permute-start | bytes 1397768 | tf_op jit(solution)/shard_map/ppermute | solution.py:464
  19.8 0.3 collective-permute-start.5
  20.2 9.3 %collective-permute-done.5.refs_5_ = bf16[160,1120]{1,0:T(8,128)(2,1)S(1)} collective-permute-done((bf16[160,1120]{1,0:T(8,128)(2,1)S(1)}, bf16[160,1120]{1,0:T(8,128)(2,1)S(1)}, u32[]{:S(2)}, u32[]{:S(2)}) %collective-permute-start.5) | collective-permute-done | bytes 358432 | tf_op jit(solution)/shard_map/ppermute | solution.py:468
  29.5 1.4 %collective-permute-done.3.refs_7_.refs_11_ = bf16[208,1120]{1,0:T(8,128)(2,1)S(1)} collective-permute-done((bf16[208,1120]{1,0:T(8,128)(2,1)S(1)}, bf16[208,1120]{1,0:T(8,128)(2,1)S(1)}, u32[]{:S(2)}, u32[]{:S(2)}) %collective-permute-start.3) | collective-permute-done | bytes 465952 | tf_op jit(solution)/shard_map/ppermute | solution.py:464
  30.9 1.1 %collective-permute-start.7 = (bf16[208,1120]{1,0:T(8,128)(2,1)S(1)}, bf16[208,1120]{1,0:T(8,128)(2,1)S(1)}, u32[]{:S(2)}, u32[]{:S(2)}) collective-permute-start(bf16[208,1120]{1,0:T(8,128)(2,1)S(1)} %collective-permute-done.4.refs_9_.refs_12_), channel_id=1, source_target_pairs={{4,0},{8,4},{12,8},{14,12},{10,14},{6,10},{2,6},{0,2},{5,1},{9,5},... | collective-permute-start | bytes 1397768 | tf_op jit(solution)/shard_map/ppermute | solution.py:464
  32.0 0.4 collective-permute-start.6
  32.5 0.3 collective-permute-start.8
  33.0 1.3 %collective-permute-start.13 = (bf16[144,1120]{1,0:T(8,128)(2,1)S(1)}, bf16[144,1120]{1,0:T(8,128)(2,1)S(1)}, u32[]{:S(2)}, u32[]{:S(2)}) collective-permute-start(bf16[144,1120]{1,0:T(8,128)(2,1)S(1)} %get-tuple-element.35.after_ref.refs_1_.refs_8_), channel_id=1, source_target_pairs={{4,0},{8,4},{12,8},{14,12},{10,14},{6,10},{2,6},{0,2},{5,1},{9,5},... | collective-permute-start | bytes 967688 | tf_op jit(solution)/shard_map/ppermute | solution.py:464
  34.3 6.8 %collective-permute-done.8.refs_8_ = bf16[160,1120]{1,0:T(8,128)(2,1)S(1)} collective-permute-done((bf16[160,1120]{1,0:T(8,128)(2,1)S(1)}, bf16[160,1120]{1,0:T(8,128)(2,1)S(1)}, u32[]{:S(2)}, u32[]{:S(2)}) %collective-permute-start.8) | collective-permute-done | bytes 358432 | tf_op jit(solution)/shard_map/ppermute | solution.py:468
  41.1 2.1 %collective-permute-done.6.refs_3_ = bf16[208,1120]{1,0:T(8,128)(2,1)S(1)} collective-permute-done((bf16[208,1120]{1,0:T(8,128)(2,1)S(1)}, bf16[208,1120]{1,0:T(8,128)(2,1)S(1)}, u32[]{:S(2)}, u32[]{:S(2)}) %collective-permute-start.6) | collective-permute-done | bytes 465952 | tf_op jit(solution)/shard_map/ppermute | solution.py:464
  43.3 0.5 collective-permute-start.9
  43.8 1.0 collective-permute-start.10
  44.8 0.3 collective-permute-start.11
  45.2 7.3 %kv_part.1.refs_2_ = f32[1920,1120]{1,0:T(8,128)S(1)} custom-call(s32[10]{0:T(128)S(1)} %pad_add_fusion.meta, bf16[960,2304]{1,0:T(8,128)(2,1)S(1)} %pack_tokens.1.refs_0_, bf16[960,2304]{1,0:T(8,128)(2,1)S(1)} %collective-permute-done.2.refs_1_, bf16[208,1120]{1,0:T(8,128)(2,1)S(1)} %get-tuple-element.34.after_ref.refs_2_.refs_8_, ...), custom_call_target="tpu_custom_call" | custom-call | flops 5505024000 | tf_op jit(solution)/shard_map/kv_part/pallas_call | solution.py:68
  52.5 4.9 %collective-permute-done.9.refs_6_ = bf16[144,1120]{1,0:T(8,128)(2,1)S(1)} collective-permute-done((bf16[144,1120]{1,0:T(8,128)(2,1)S(1)}, bf16[144,1120]{1,0:T(8,128)(2,1)S(1)}, u32[]{:S(2)}, u32[]{:S(2)}) %collective-permute-start.9) | collective-permute-done | bytes 322592 | tf_op jit(solution)/shard_map/ppermute | solution.py:464
  57.4 0.5 collective-permute-start.14
  57.9 1.0 collective-permute-start.15
  58.9 8.4 %states.1 = f32[560,128]{1,0:T(8,128)S(1)} custom-call(s32[10]{0:T(128)S(1)} %pad_add_fusion.meta, bf16[960,2304]{1,0:T(8,128)(2,1)S(1)} %pack_tokens.1.refs_0_, bf16[960,2304]{1,0:T(8,128)(2,1)S(1)} %collective-permute-done.2.refs_1_, f32[1920,1120]{1,0:T(8,128)S(1)} %kv_part.1.refs_2_, bf16[208,1120]{1,0:T(8,128)(2,1)S(1)} %collective-permute-done.6.refs_3_, ...), custom_call_target="tpu_custom_call" | custom-call | flops 4679270400 | tf_op jit(solution)/shard_map/states/pallas_call | solution.py:68
  67.3 0.5 collective-permute-start.17
  67.8 1.0 collective-permute-start.18
  69.2 2.4 %collective-permute-start.16 = (bf16[560,128]{1,0:T(8,128)(2,1)S(1)}, bf16[560,128]{1,0:T(8,128)(2,1)S(1)}, u32[]{:S(2)}, u32[]{:S(2)}) collective-permute-start(bf16[560,128]{1,0:T(8,128)(2,1)S(1)} %pad_maximum_fusion.4), channel_id=1, source_target_pairs={{0,2},{2,4},{4,6},{6,8},{8,10},{10,12},{12,14},{1,3},{3,5},{5,7},{... | collective-permute-start | bytes 430088 | tf_op jit(solution)/shard_map/ppermute | solution.py:434
  71.5 3.6 %collective-permute-start.20 = (bf16[144,1120]{1,0:T(8,128)(2,1)S(1)}, bf16[144,1120]{1,0:T(8,128)(2,1)S(1)}, u32[]{:S(2)}, u32[]{:S(2)}) collective-permute-start(bf16[144,1120]{1,0:T(8,128)(2,1)S(1)} %collective-permute-done.12.refs_3_.refs_10_), channel_id=1, source_target_pairs={{0,1},{1,0},{2,3},{3,2},{4,5},{5,4},{6,7},{7,6},{8,9},{9,8},{10,11... | collective-permute-start | bytes 967688 | tf_op jit(solution)/shard_map/ppermute | solution.py:471
  75.2 2.2 %collective-permute-done.16 = bf16[560,128]{1,0:T(8,128)(2,1)S(1)} collective-permute-done((bf16[560,128]{1,0:T(8,128)(2,1)S(1)}, bf16[560,128]{1,0:T(8,128)(2,1)S(1)}, u32[]{:S(2)}, u32[]{:S(2)}) %collective-permute-start.16) | collective-permute-done | bytes 143392 | tf_op jit(solution)/shard_map/ppermute | solution.py:434
  77.4 3.6 %collective-permute-start.22 = (bf16[144,1120]{1,0:T(8,128)(2,1)S(1)}, bf16[144,1120]{1,0:T(8,128)(2,1)S(1)}, u32[]{:S(2)}, u32[]{:S(2)}) collective-permute-start(bf16[144,1120]{1,0:T(8,128)(2,1)S(1)} %collective-permute-done.14.refs_7_.refs_14_), channel_id=1, source_target_pairs={{0,1},{1,0},{2,3},{3,2},{4,5},{5,4},{6,7},{7,6},{8,9},{9,8},{10,11... | collective-permute-start | bytes 967688 | tf_op jit(solution)/shard_map/ppermute | solution.py:471
  81.1 0.5 collective-permute-start.25
  81.6 0.3 subtract_convert_fusion.1
  82.3 1.3 %collective-permute-start.19 = (bf16[560,128]{1,0:T(8,128)(2,1)S(1)}, bf16[560,128]{1,0:T(8,128)(2,1)S(1)}, u32[]{:S(2)}, u32[]{:S(2)}) collective-permute-start(bf16[560,128]{1,0:T(8,128)(2,1)S(1)} %pad_maximum_fusion.5), channel_id=1, source_target_pairs={{0,4},{2,6},{4,8},{6,10},{8,12},{10,14},{1,5},{3,7},{5,9},{7,11},{... | collective-permute-start | bytes 430088 | tf_op jit(solution)/shard_map/ppermute | solution.py:434
  83.7 2.1 %collective-permute-start.28 = (bf16[64,1120]{1,0:T(8,128)(2,1)S(1)}, bf16[64,1120]{1,0:T(8,128)(2,1)S(1)}, u32[]{:S(2)}, u32[]{:S(2)}) collective-permute-start(bf16[64,1120]{1,0:T(8,128)(2,1)S(1)} %slice.80), channel_id=1, source_target_pairs={{4,0},{8,4},{12,8},{14,12},{10,14},{6,10},{2,6},{0,2},{5,1},{9,5},... | collective-permute-start | bytes 430088 | tf_op jit(solution)/shard_map/ppermute | solution.py:464
  85.8 4.1 %q_early.1.refs_1_ = f32[960,1120]{1,0:T(8,128)S(1)} custom-call(s32[10]{0:T(128)S(1)} %pad_add_fusion.meta, bf16[960,2304]{1,0:T(8,128)(2,1)S(1)} %pack_tokens.1.refs_0_, bf16[144,1120]{1,0:T(8,128)(2,1)S(1)} %get-tuple-element.35.after_ref.refs_1_.refs_8_, bf16[144,1120]{1,0:T(8,128)(2,1)S(1)} %get-tuple-element.56.refs_2_.refs_9_, ...), custom_call_target="tpu_custom_call" | custom-call | flops 2752512000 | tf_op jit(solution)/shard_map/q_early/pallas_call | solution.py:68
  90.0 0.2 subtract_convert_fusion
  90.2 2.8 %collective-permute-done.27 = bf16[80,1120]{1,0:T(8,128)(2,1)S(1)} collective-permute-done((bf16[80,1120]{1,0:T(8,128)(2,1)S(1)}, bf16[80,1120]{1,0:T(8,128)(2,1)S(1)}, u32[]{:S(2)}, u32[]{:S(2)}) %collective-permute-start.27) | collective-permute-done | bytes 179232 | tf_op jit(solution)/shard_map/ppermute | solution.py:464
  93.1 1.3 %collective-permute-start.29 = (bf16[144,1120]{1,0:T(8,128)(2,1)S(1)}, bf16[144,1120]{1,0:T(8,128)(2,1)S(1)}, u32[]{:S(2)}, u32[]{:S(2)}) collective-permute-start(bf16[144,1120]{1,0:T(8,128)(2,1)S(1)} %constant_dynamic-update-slice_fusion.refs_6_), channel_id=1, source_target_pairs={{0,1},{1,0},{2,3},{3,2},{4,5},{5,4},{6,7},{7,6},{8,9},{9,8},{10,11... | collective-permute-start | bytes 967688 | tf_op jit(solution)/shard_map/ppermute | solution.py:471
  94.6 1.5 %collective-permute-start.24 = (bf16[560,128]{1,0:T(8,128)(2,1)S(1)}, bf16[560,128]{1,0:T(8,128)(2,1)S(1)}, u32[]{:S(2)}, u32[]{:S(2)}) collective-permute-start(bf16[560,128]{1,0:T(8,128)(2,1)S(1)} %pad_maximum_fusion.6), channel_id=1, source_target_pairs={{0,8},{2,10},{4,12},{6,14},{1,9},{3,11},{5,13},{7,15},{16,24},{18,... | collective-permute-start | bytes 430088 | tf_op jit(solution)/shard_map/ppermute | solution.py:434
  96.2 3.5 %q_late.1.q_ref = bf16[960,1120]{1,0:T(8,128)(2,1)S(1)} custom-call(s32[10]{0:T(128)S(1)} %pad_add_fusion.meta, bf16[960,2304]{1,0:T(8,128)(2,1)S(1)} %pack_tokens.1.refs_0_, f32[960,1120]{1,0:T(8,128)S(1)} %q_early.1.refs_1_, bf16[144,1120]{1,0:T(8,128)(2,1)S(1)} %collective-permute-done.17.refs_2_, bf16[144,1120]{1,0:T(8,128)(2,1)S(1)} %collective-permute-done.25.refs_3_, ...), custom_call_target="tpu_custom_call" | custom-call | flops 2202009600 | tf_op jit(solution)/shard_map/q_late/pallas_call | solution.py:68
  99.7 6.4 %collective-permute-done.24 = bf16[560,128]{1,0:T(8,128)(2,1)S(1)} collective-permute-done((bf16[560,128]{1,0:T(8,128)(2,1)S(1)}, bf16[560,128]{1,0:T(8,128)(2,1)S(1)}, u32[]{:S(2)}, u32[]{:S(2)}) %collective-permute-start.24) | collective-permute-done | bytes 143392 | tf_op jit(solution)/shard_map/ppermute | solution.py:434
  106.6 0.5 collective-permute-start.30
  107.1 1.2 %collective-permute-done.30.theirs_ref = f32[560,128]{1,0:T(8,128)S(1)} collective-permute-done((f32[560,128]{1,0:T(8,128)S(1)}, f32[560,128]{1,0:T(8,128)S(1)}, u32[]{:S(2)}, u32[]{:S(2)}) %collective-permute-start.30) | collective-permute-done | bytes 286752 | tf_op jit(solution)/shard_map/ppermute | solution.py:471
  108.3 4.3 %attend.1 = bf16[960,1120]{1,0:T(8,128)(2,1)} custom-call(s32[10]{0:T(128)S(1)} %pad_add_fusion.meta, bf16[960,1120]{1,0:T(8,128)(2,1)S(1)} %q_late.1.q_ref, f32[560,128]{1,0:T(8,128)S(1)} %pad_maximum_fusion.3.mine_ref, f32[560,128]{1,0:T(8,128)S(1)} %collective-permute-done.30.theirs_ref), custom_call_target="tpu_custom_call" | custom-call | flops 1720320000 | bytes 4300800 | tf_op jit(solution)/shard_map/attend/pallas_call | solution.py:399
  (58 shorter events, 2.4 us)
Async XLA Ops:
  0.0 5.8 %copy-start = (bf16[2,6,80,2240]{3,2,1,0:T(8,128)(2,1)S(1)}, bf16[2,6,80,2240]{3,2,1,0:T(8,128)(2,1)}, u32[]{:S(2)}) copy-start(bf16[2,6,80,2240]{3,2,1,0:T(8,128)(2,1)} %param.3) | copy-start | bytes 12902404
  0.9 1.8 %copy-start.1 = (bf16[280,3360]{1,0:T(8,128)(2,1)S(1)}, bf16[280,3360]{1,0:T(8,128)(2,1)}, u32[]{:S(2)}) copy-start(bf16[280,3360]{1,0:T(8,128)(2,1)} %w_ref.3) | copy-start | bytes 5644804
  3.6 11.9 %collective-permute-start = (bf16[208,1120]{1,0:T(8,128)(2,1)S(1)}, bf16[208,1120]{1,0:T(8,128)(2,1)S(1)}, u32[]{:S(2)}, u32[]{:S(2)}) collective-permute-start(bf16[208,1120]{1,0:T(8,128)(2,1)S(1)} %get-tuple-element.34.after_ref.refs_2_.refs_8_), channel_id=1, source_target_pairs={{0,4},{4,8},{8,12},{12,14},{14,10},{10,6},{6,2},{2,0},{1,5},{5,9},... | collective-permute-start | bytes 1397768 | tf_op jit(solution)/shard_map/ppermute | solution.py:464
  4.9 11.5 %collective-permute-start.1 = (bf16[208,1120]{1,0:T(8,128)(2,1)S(1)}, bf16[208,1120]{1,0:T(8,128)(2,1)S(1)}, u32[]{:S(2)}, u32[]{:S(2)}) collective-permute-start(bf16[208,1120]{1,0:T(8,128)(2,1)S(1)} %get-tuple-element.36.refs_3_), channel_id=1, source_target_pairs={{4,0},{8,4},{12,8},{14,12},{10,14},{6,10},{2,6},{0,2},{5,1},{9,5},... | collective-permute-start | bytes 1397768 | tf_op jit(solution)/shard_map/ppermute | solution.py:464
  16.4 14.5 %collective-permute-start.2 = (bf16[960,2304]{1,0:T(8,128)(2,1)S(1)}, bf16[960,2304]{1,0:T(8,128)(2,1)S(1)}, u32[]{:S(2)}, u32[]{:S(2)}) collective-permute-start(bf16[960,2304]{1,0:T(8,128)(2,1)S(1)} %pack_tokens.1.refs_0_), channel_id=1, source_target_pairs={{0,1},{1,0},{2,3},{3,2},{4,5},{5,4},{6,7},{7,6},{8,9},{9,8},{10,11... | collective-permute-start | bytes 13271048 | tf_op jit(solution)/shard_map/ppermute | solution.py:471
  18.3 12.6 %collective-permute-start.3 = (bf16[208,1120]{1,0:T(8,128)(2,1)S(1)}, bf16[208,1120]{1,0:T(8,128)(2,1)S(1)}, u32[]{:S(2)}, u32[]{:S(2)}) collective-permute-start(bf16[208,1120]{1,0:T(8,128)(2,1)S(1)} %collective-permute-done.refs_4_.refs_9_), channel_id=1, source_target_pairs={{0,4},{4,8},{8,12},{12,14},{14,10},{10,6},{6,2},{2,0},{1,5},{5,9},... | collective-permute-start | bytes 1397768 | tf_op jit(solution)/shard_map/ppermute | solution.py:464
  18.5 12.4 %collective-permute-start.4 = (bf16[208,1120]{1,0:T(8,128)(2,1)S(1)}, bf16[208,1120]{1,0:T(8,128)(2,1)S(1)}, u32[]{:S(2)}, u32[]{:S(2)}) collective-permute-start(bf16[208,1120]{1,0:T(8,128)(2,1)S(1)} %collective-permute-done.1.refs_6_.refs_10_), channel_id=1, source_target_pairs={{4,0},{8,4},{12,8},{14,12},{10,14},{6,10},{2,6},{0,2},{5,1},{9,5},... | collective-permute-start | bytes 1397768 | tf_op jit(solution)/shard_map/ppermute | solution.py:464
  19.8 9.6 %collective-permute-start.5 = (bf16[160,1120]{1,0:T(8,128)(2,1)S(1)}, bf16[160,1120]{1,0:T(8,128)(2,1)S(1)}, u32[]{:S(2)}, u32[]{:S(2)}) collective-permute-start(bf16[160,1120]{1,0:T(8,128)(2,1)S(1)} %pad_maximum_fusion), channel_id=1, source_target_pairs={{0,16},{16,0},{1,17},{17,1},{2,18},{18,2},{3,19},{19,3},{4,20},{20... | collective-permute-start | bytes 1075208 | tf_op jit(solution)/shard_map/ppermute | solution.py:468
  30.9 12.3 %collective-permute-start.7 = (bf16[208,1120]{1,0:T(8,128)(2,1)S(1)}, bf16[208,1120]{1,0:T(8,128)(2,1)S(1)}, u32[]{:S(2)}, u32[]{:S(2)}) collective-permute-start(bf16[208,1120]{1,0:T(8,128)(2,1)S(1)} %collective-permute-done.4.refs_9_.refs_12_), channel_id=1, source_target_pairs={{4,0},{8,4},{12,8},{14,12},{10,14},{6,10},{2,6},{0,2},{5,1},{9,5},... | collective-permute-start | bytes 1397768 | tf_op jit(solution)/shard_map/ppermute | solution.py:464
  32.0 11.1 %collective-permute-start.6 = (bf16[208,1120]{1,0:T(8,128)(2,1)S(1)}, bf16[208,1120]{1,0:T(8,128)(2,1)S(1)}, u32[]{:S(2)}, u32[]{:S(2)}) collective-permute-start(bf16[208,1120]{1,0:T(8,128)(2,1)S(1)} %collective-permute-done.3.refs_7_.refs_11_), channel_id=1, source_target_pairs={{0,4},{4,8},{8,12},{12,14},{14,10},{10,6},{6,2},{2,0},{1,5},{5,9},... | collective-permute-start | bytes 1397768 | tf_op jit(solution)/shard_map/ppermute | solution.py:464
  32.5 8.6 %collective-permute-start.8 = (bf16[160,1120]{1,0:T(8,128)(2,1)S(1)}, bf16[160,1120]{1,0:T(8,128)(2,1)S(1)}, u32[]{:S(2)}, u32[]{:S(2)}) collective-permute-start(bf16[160,1120]{1,0:T(8,128)(2,1)S(1)} %pad_maximum_fusion.1), channel_id=1, source_target_pairs={{0,16},{16,0},{1,17},{17,1},{2,18},{18,2},{3,19},{19,3},{4,20},{20... | collective-permute-start | bytes 1075208 | tf_op jit(solution)/shard_map/ppermute | solution.py:468
  32.8 19.6 %collective-permute-start.12 = (bf16[144,1120]{1,0:T(8,128)(2,1)S(1)}, bf16[144,1120]{1,0:T(8,128)(2,1)S(1)}, u32[]{:S(2)}, u32[]{:S(2)}) collective-permute-start(bf16[144,1120]{1,0:T(8,128)(2,1)S(1)} %get-tuple-element.35.after_ref.refs_1_.refs_8_), channel_id=1, source_target_pairs={{0,4},{4,8},{8,12},{12,14},{14,10},{10,6},{6,2},{2,0},{1,5},{5,9},... | collective-permute-start | bytes 967688 | tf_op jit(solution)/shard_map/ppermute | solution.py:464
  33.0 19.5 %collective-permute-start.13 = (bf16[144,1120]{1,0:T(8,128)(2,1)S(1)}, bf16[144,1120]{1,0:T(8,128)(2,1)S(1)}, u32[]{:S(2)}, u32[]{:S(2)}) collective-permute-start(bf16[144,1120]{1,0:T(8,128)(2,1)S(1)} %get-tuple-element.35.after_ref.refs_1_.refs_8_), channel_id=1, source_target_pairs={{4,0},{8,4},{12,8},{14,12},{10,14},{6,10},{2,6},{0,2},{5,1},{9,5},... | collective-permute-start | bytes 967688 | tf_op jit(solution)/shard_map/ppermute | solution.py:464
  43.3 14.1 %collective-permute-start.9 = (bf16[144,1120]{1,0:T(8,128)(2,1)S(1)}, bf16[144,1120]{1,0:T(8,128)(2,1)S(1)}, u32[]{:S(2)}, u32[]{:S(2)}) collective-permute-start(bf16[144,1120]{1,0:T(8,128)(2,1)S(1)} %slice.67), channel_id=1, source_target_pairs={{0,4},{4,8},{8,12},{12,14},{14,10},{10,6},{6,2},{2,0},{1,5},{5,9},... | collective-permute-start | bytes 967688 | tf_op jit(solution)/shard_map/ppermute | solution.py:464
  43.8 13.6 %collective-permute-start.10 = (bf16[144,1120]{1,0:T(8,128)(2,1)S(1)}, bf16[144,1120]{1,0:T(8,128)(2,1)S(1)}, u32[]{:S(2)}, u32[]{:S(2)}) collective-permute-start(bf16[144,1120]{1,0:T(8,128)(2,1)S(1)} %slice.68), channel_id=1, source_target_pairs={{4,0},{8,4},{12,8},{14,12},{10,14},{6,10},{2,6},{0,2},{5,1},{9,5},... | collective-permute-start | bytes 967688 | tf_op jit(solution)/shard_map/ppermute | solution.py:464
  44.8 12.6 %collective-permute-start.11 = (bf16[160,1120]{1,0:T(8,128)(2,1)S(1)}, bf16[160,1120]{1,0:T(8,128)(2,1)S(1)}, u32[]{:S(2)}, u32[]{:S(2)}) collective-permute-start(bf16[160,1120]{1,0:T(8,128)(2,1)S(1)} %pad_maximum_fusion.2), channel_id=1, source_target_pairs={{0,16},{16,0},{1,17},{17,1},{2,18},{18,2},{3,19},{19,3},{4,20},{20... | collective-permute-start | bytes 1075208 | tf_op jit(solution)/shard_map/ppermute | solution.py:468
  57.4 9.9 %collective-permute-start.14 = (bf16[144,1120]{1,0:T(8,128)(2,1)S(1)}, bf16[144,1120]{1,0:T(8,128)(2,1)S(1)}, u32[]{:S(2)}, u32[]{:S(2)}) collective-permute-start(bf16[144,1120]{1,0:T(8,128)(2,1)S(1)} %collective-permute-done.12.refs_3_.refs_10_), channel_id=1, source_target_pairs={{0,4},{4,8},{8,12},{12,14},{14,10},{10,6},{6,2},{2,0},{1,5},{5,9},... | collective-permute-start | bytes 967688 | tf_op jit(solution)/shard_map/ppermute | solution.py:464
  57.9 9.4 %collective-permute-start.15 = (bf16[144,1120]{1,0:T(8,128)(2,1)S(1)}, bf16[144,1120]{1,0:T(8,128)(2,1)S(1)}, u32[]{:S(2)}, u32[]{:S(2)}) collective-permute-start(bf16[144,1120]{1,0:T(8,128)(2,1)S(1)} %collective-permute-done.13.refs_5_.refs_12_), channel_id=1, source_target_pairs={{4,0},{8,4},{12,8},{14,12},{10,14},{6,10},{2,6},{0,2},{5,1},{9,5},... | collective-permute-start | bytes 967688 | tf_op jit(solution)/shard_map/ppermute | solution.py:464
  67.3 13.8 %collective-permute-start.17 = (bf16[144,1120]{1,0:T(8,128)(2,1)S(1)}, bf16[144,1120]{1,0:T(8,128)(2,1)S(1)}, u32[]{:S(2)}, u32[]{:S(2)}) collective-permute-start(bf16[144,1120]{1,0:T(8,128)(2,1)S(1)} %collective-permute-done.14.refs_7_.refs_14_), channel_id=1, source_target_pairs={{0,4},{4,8},{8,12},{12,14},{14,10},{10,6},{6,2},{2,0},{1,5},{5,9},... | collective-permute-start | bytes 967688 | tf_op jit(solution)/shard_map/ppermute | solution.py:464
  67.8 13.3 %collective-permute-start.18 = (bf16[144,1120]{1,0:T(8,128)(2,1)S(1)}, bf16[144,1120]{1,0:T(8,128)(2,1)S(1)}, u32[]{:S(2)}, u32[]{:S(2)}) collective-permute-start(bf16[144,1120]{1,0:T(8,128)(2,1)S(1)} %collective-permute-done.15.refs_9_.refs_16_), channel_id=1, source_target_pairs={{4,0},{8,4},{12,8},{14,12},{10,14},{6,10},{2,6},{0,2},{5,1},{9,5},... | collective-permute-start | bytes 967688 | tf_op jit(solution)/shard_map/ppermute | solution.py:464
  69.2 8.3 %collective-permute-start.16 = (bf16[560,128]{1,0:T(8,128)(2,1)S(1)}, bf16[560,128]{1,0:T(8,128)(2,1)S(1)}, u32[]{:S(2)}, u32[]{:S(2)}) collective-permute-start(bf16[560,128]{1,0:T(8,128)(2,1)S(1)} %pad_maximum_fusion.4), channel_id=1, source_target_pairs={{0,2},{2,4},{4,6},{6,8},{8,10},{10,12},{12,14},{1,3},{3,5},{5,7},{... | collective-permute-start | bytes 430088 | tf_op jit(solution)/shard_map/ppermute | solution.py:434
  71.5 10.6 %collective-permute-start.20 = (bf16[144,1120]{1,0:T(8,128)(2,1)S(1)}, bf16[144,1120]{1,0:T(8,128)(2,1)S(1)}, u32[]{:S(2)}, u32[]{:S(2)}) collective-permute-start(bf16[144,1120]{1,0:T(8,128)(2,1)S(1)} %collective-permute-done.12.refs_3_.refs_10_), channel_id=1, source_target_pairs={{0,1},{1,0},{2,3},{3,2},{4,5},{5,4},{6,7},{7,6},{8,9},{9,8},{10,11... | collective-permute-start | bytes 967688 | tf_op jit(solution)/shard_map/ppermute | solution.py:471
  75.1 7.2 %collective-permute-start.21 = (bf16[144,1120]{1,0:T(8,128)(2,1)S(1)}, bf16[144,1120]{1,0:T(8,128)(2,1)S(1)}, u32[]{:S(2)}, u32[]{:S(2)}) collective-permute-start(bf16[144,1120]{1,0:T(8,128)(2,1)S(1)} %collective-permute-done.13.refs_5_.refs_12_), channel_id=1, source_target_pairs={{0,1},{1,0},{2,3},{3,2},{4,5},{5,4},{6,7},{7,6},{8,9},{9,8},{10,11... | collective-permute-start | bytes 967688 | tf_op jit(solution)/shard_map/ppermute | solution.py:471
  77.4 6.2 %collective-permute-start.22 = (bf16[144,1120]{1,0:T(8,128)(2,1)S(1)}, bf16[144,1120]{1,0:T(8,128)(2,1)S(1)}, u32[]{:S(2)}, u32[]{:S(2)}) collective-permute-start(bf16[144,1120]{1,0:T(8,128)(2,1)S(1)} %collective-permute-done.14.refs_7_.refs_14_), channel_id=1, source_target_pairs={{0,1},{1,0},{2,3},{3,2},{4,5},{5,4},{6,7},{7,6},{8,9},{9,8},{10,11... | collective-permute-start | bytes 967688 | tf_op jit(solution)/shard_map/ppermute | solution.py:471
  81.1 2.6 %collective-permute-start.23 = (bf16[144,1120]{1,0:T(8,128)(2,1)S(1)}, bf16[144,1120]{1,0:T(8,128)(2,1)S(1)}, u32[]{:S(2)}, u32[]{:S(2)}) collective-permute-start(bf16[144,1120]{1,0:T(8,128)(2,1)S(1)} %collective-permute-done.15.refs_9_.refs_16_), channel_id=1, source_target_pairs={{0,1},{1,0},{2,3},{3,2},{4,5},{5,4},{6,7},{7,6},{8,9},{9,8},{10,11... | collective-permute-start | bytes 967688 | tf_op jit(solution)/shard_map/ppermute | solution.py:471
  81.1 15.1 %collective-permute-start.25 = (bf16[144,1120]{1,0:T(8,128)(2,1)S(1)}, bf16[144,1120]{1,0:T(8,128)(2,1)S(1)}, u32[]{:S(2)}, u32[]{:S(2)}) collective-permute-start(bf16[144,1120]{1,0:T(8,128)(2,1)S(1)} %collective-permute-done.17.refs_2_), channel_id=1, source_target_pairs={{0,1},{1,0},{2,3},{3,2},{4,5},{5,4},{6,7},{7,6},{8,9},{9,8},{10,11... | collective-permute-start | bytes 967688 | tf_op jit(solution)/shard_map/ppermute | solution.py:471
  82.2 14.0 %collective-permute-start.26 = (bf16[144,1120]{1,0:T(8,128)(2,1)S(1)}, bf16[144,1120]{1,0:T(8,128)(2,1)S(1)}, u32[]{:S(2)}, u32[]{:S(2)}) collective-permute-start(bf16[144,1120]{1,0:T(8,128)(2,1)S(1)} %collective-permute-done.18.refs_4_), channel_id=1, source_target_pairs={{0,1},{1,0},{2,3},{3,2},{4,5},{5,4},{6,7},{7,6},{8,9},{9,8},{10,11... | collective-permute-start | bytes 967688 | tf_op jit(solution)/shard_map/ppermute | solution.py:471
  82.3 7.6 %collective-permute-start.19 = (bf16[560,128]{1,0:T(8,128)(2,1)S(1)}, bf16[560,128]{1,0:T(8,128)(2,1)S(1)}, u32[]{:S(2)}, u32[]{:S(2)}) collective-permute-start(bf16[560,128]{1,0:T(8,128)(2,1)S(1)} %pad_maximum_fusion.5), channel_id=1, source_target_pairs={{0,4},{2,6},{4,8},{6,10},{8,12},{10,14},{1,5},{3,7},{5,9},{7,11},{... | collective-permute-start | bytes 430088 | tf_op jit(solution)/shard_map/ppermute | solution.py:434
  83.6 9.4 %collective-permute-start.27 = (bf16[80,1120]{1,0:T(8,128)(2,1)S(1)}, bf16[80,1120]{1,0:T(8,128)(2,1)S(1)}, u32[]{:S(2)}, u32[]{:S(2)}) collective-permute-start(bf16[80,1120]{1,0:T(8,128)(2,1)S(1)} %slice.79), channel_id=1, source_target_pairs={{0,4},{4,8},{8,12},{12,14},{14,10},{10,6},{6,2},{2,0},{1,5},{5,9},... | collective-permute-start | bytes 537608 | tf_op jit(solution)/shard_map/ppermute | solution.py:464
  83.7 9.4 %collective-permute-start.28 = (bf16[64,1120]{1,0:T(8,128)(2,1)S(1)}, bf16[64,1120]{1,0:T(8,128)(2,1)S(1)}, u32[]{:S(2)}, u32[]{:S(2)}) collective-permute-start(bf16[64,1120]{1,0:T(8,128)(2,1)S(1)} %slice.80), channel_id=1, source_target_pairs={{4,0},{8,4},{12,8},{14,12},{10,14},{6,10},{2,6},{0,2},{5,1},{9,5},... | collective-permute-start | bytes 430088 | tf_op jit(solution)/shard_map/ppermute | solution.py:464
  93.1 3.1 %collective-permute-start.29 = (bf16[144,1120]{1,0:T(8,128)(2,1)S(1)}, bf16[144,1120]{1,0:T(8,128)(2,1)S(1)}, u32[]{:S(2)}, u32[]{:S(2)}) collective-permute-start(bf16[144,1120]{1,0:T(8,128)(2,1)S(1)} %constant_dynamic-update-slice_fusion.refs_6_), channel_id=1, source_target_pairs={{0,1},{1,0},{2,3},{3,2},{4,5},{5,4},{6,7},{7,6},{8,9},{9,8},{10,11... | collective-permute-start | bytes 967688 | tf_op jit(solution)/shard_map/ppermute | solution.py:471
  94.6 11.4 %collective-permute-start.24 = (bf16[560,128]{1,0:T(8,128)(2,1)S(1)}, bf16[560,128]{1,0:T(8,128)(2,1)S(1)}, u32[]{:S(2)}, u32[]{:S(2)}) collective-permute-start(bf16[560,128]{1,0:T(8,128)(2,1)S(1)} %pad_maximum_fusion.6), channel_id=1, source_target_pairs={{0,8},{2,10},{4,12},{6,14},{1,9},{3,11},{5,13},{7,15},{16,24},{18,... | collective-permute-start | bytes 430088 | tf_op jit(solution)/shard_map/ppermute | solution.py:434
  106.6 1.7 %collective-permute-start.30 = (f32[560,128]{1,0:T(8,128)S(1)}, f32[560,128]{1,0:T(8,128)S(1)}, u32[]{:S(2)}, u32[]{:S(2)}) collective-permute-start(f32[560,128]{1,0:T(8,128)S(1)} %pad_maximum_fusion.3.mine_ref), channel_id=1, source_target_pairs={{0,1},{1,0},{2,3},{3,2},{4,5},{5,4},{6,7},{7,6},{8,9},{9,8},{10,11... | collective-permute-start | bytes 860168 | tf_op jit(solution)/shard_map/ppermute | solution.py:471

commit v4 on v3

--- a/solution.py
+++ b/solution.py
@@ -523,18 +523,22 @@
             x = tie(x, up, down)[0]
             x_other = core_swap(x)
             both = (x, x_other)
-        elif full:
+        elif step + 1 < last:
             x_other, up, down, swapped = tie(x_other, up, down, swapped)
             both = (x, x_other)
+        elif full:
+            next_queries()
+            acc = add_keys_values(None, range(len(slots)))
+            _, up, down, swapped = tie(acc, up, down, swapped)
         else:
-            acc = add_keys_values(None, range(len(slots)))
-            acc, up, down, swapped = with_queries(acc, up, down, swapped)
+            acc, *ways[-1] = tie(acc, *ways[-1])
+            acc = add_keys_values(acc, range(len(slots) - 2, len(slots)))
+            acc, up, down, swapped = tie(acc, up, down, swapped)
+            next_queries()
         if step > 1:
             slots += thirds(*before, (swapped, 0, third), (swapped, third, third))
         if full:
             swapped = plane_swap(up, down)
-        if step + 1 == last:
-            next_queries()
     rest = common_rows - some
     slots.append([[(up, 0, third)], [(down, rest, third)], [(up, third, some), (down, 0, rest)]])
     settings = plan(2, range(count - 3, count), True, True, True)

time: 113 us -> 111 us (0.982)
  waiting for transfers between devices: 45.3 us -> 39.5 us
  starting transfers between devices: 30.5 us -> 33.5 us
    ppermute x3, waiting for transfers between devices: 16.2 us -> 11.5 us  [plane_swap(): return lax.ppermute(value, 'groups', across)]
    ppermute x9, starting transfers between devices: 11.7 us -> 14.6 us  [core_swap(): return lax.ppermute(value, 'space', over)]
    ppermute x16, waiting for transfers between devices: 19.3 us -> 18.1 us  [ring(): return lax.ppermute(value, 'tm', forward if up else backward)]
    pallas_call x6 -> x7, Pallas kernels: 24.8 us -> 25.7 us  [resident(): pl.pallas_call(kernel, in_specs=[pl.BlockSpec(memory_space=pltpu.SMEM)] +...]
  transfers between devices with their start and end apart: 31 -> 31, of which waited for: 11 -> 11; matrix products, arithmetic and copies ran while one was open for 1% -> 1% of each run, Pallas kernels for 23% -> 25%
where the time goes in v4:
time: 111 us
  waiting for transfers between devices  39.5 us (36%)
  starting transfers between devices  33.5 us (30%)
  Pallas kernels  32.7 us (29%)
  local copies, waits for them, and re-layouts  2.83 us (3%)
  other arithmetic  1.98 us (2%)
    pallas_call x7, Pallas kernels, resident(): pl.pallas_call(kernel, in_specs=[pl.BlockSpec(memory_space=pltpu.SMEM)] +...  25.7 us
    ppermute x16, waiting for transfers between devices, ring(): return lax.ppermute(value, 'tm', forward if up else backward)  18.1 us
    ppermute x9, starting transfers between devices, core_swap(): return lax.ppermute(value, 'space', over)  14.6 us
    ppermute x16, starting transfers between devices, ring(): return lax.ppermute(value, 'tm', forward if up else backward)  12.1 us
    ppermute x3, waiting for transfers between devices, plane_swap(): return lax.ppermute(value, 'groups', across)  11.5 us
    ppermute x3, waiting for transfers between devices, running_total(): got = lax.ppermute(sent, 'tm', pairs)  8.73 us
    ppermute x3, starting transfers between devices, running_total(): got = lax.ppermute(sent, 'tm', pairs)  5.85 us
    pallas_call x1, Pallas kernels, attend(): pl.pallas_call(functools.partial(attend_kernel, heads_here=heads_here), i...  4.39 us
  transfers between devices with their start and end apart: 31, of which 11 were waited for; matrix products, arithmetic and copies ran while one was open for 1% of the time, Pallas kernels for 25%

profile of v4, /device:TPU:27, one launch (start us, length us, event | category | flops | bytes accessed | tf_op | source)
XLA Modules:
  0.0 111.1 jit_solution(3453704508858862339)
XLA Ops:
  0.0 0.8 dynamic-slice_bitcast_fusion
  0.9 1.8 %copy-done.1 = bf16[280,3360]{1,0:T(8,128)(2,1)S(1)} copy-done((bf16[280,3360]{1,0:T(8,128)(2,1)S(1)}, bf16[280,3360]{1,0:T(8,128)(2,1)}, u32[]{:S(2)}) %copy-start.1) | copy-done | bytes 1881624
  2.7 0.9 pack_first.1
  3.6 0.2 collective-permute-start.1
  3.8 1.3 %collective-permute-start = (bf16[208,1120]{1,0:T(8,128)(2,1)S(1)}, bf16[208,1120]{1,0:T(8,128)(2,1)S(1)}, u32[]{:S(2)}, u32[]{:S(2)}) collective-permute-start(bf16[208,1120]{1,0:T(8,128)(2,1)S(1)} %get-tuple-element.34.after_ref.refs_2_.refs_8_), channel_id=1, source_target_pairs={{0,4},{4,8},{8,12},{12,14},{14,10},{10,6},{6,2},{2,0},{1,5},{5,9},... | collective-permute-start | bytes 1397768 | tf_op jit(solution)/shard_map/ppermute | solution.py:464
  5.1 0.6 pack_rest.1
  5.8 2.6 %pack_tokens.1.refs_0_ = bf16[960,2304]{1,0:T(8,128)(2,1)S(1)} custom-call(bf16[960,2240]{1,0:T(8,128)(2,1)S(1)} %bitcast.6, bf16[144,1120]{1,0:T(8,128)(2,1)S(1)} %get-tuple-element.35.after_ref.refs_1_.refs_8_), custom_call_target="tpu_custom_call" | custom-call | bytes 8601600 | tf_op jit(solution)/shard_map/pack_tokens/pallas_call | solution.py:156
  8.4 7.1 %collective-permute-done.1.refs_6_.refs_10_ = bf16[208,1120]{1,0:T(8,128)(2,1)S(1)} collective-permute-done((bf16[208,1120]{1,0:T(8,128)(2,1)S(1)}, bf16[208,1120]{1,0:T(8,128)(2,1)S(1)}, u32[]{:S(2)}, u32[]{:S(2)}) %collective-permute-start.1) | collective-permute-done | bytes 465952 | tf_op jit(solution)/shard_map/ppermute | solution.py:464
  15.5 1.7 %collective-permute-start.2 = (bf16[960,2304]{1,0:T(8,128)(2,1)S(1)}, bf16[960,2304]{1,0:T(8,128)(2,1)S(1)}, u32[]{:S(2)}, u32[]{:S(2)}) collective-permute-start(bf16[960,2304]{1,0:T(8,128)(2,1)S(1)} %pack_tokens.1.refs_0_), channel_id=1, source_target_pairs={{0,1},{1,0},{2,3},{3,2},{4,5},{5,4},{6,7},{7,6},{8,9},{9,8},{10,11... | collective-permute-start | bytes 13271048 | tf_op jit(solution)/shard_map/ppermute | solution.py:471
  17.5 1.3 %collective-permute-start.3 = (bf16[208,1120]{1,0:T(8,128)(2,1)S(1)}, bf16[208,1120]{1,0:T(8,128)(2,1)S(1)}, u32[]{:S(2)}, u32[]{:S(2)}) collective-permute-start(bf16[208,1120]{1,0:T(8,128)(2,1)S(1)} %collective-permute-done.refs_4_.refs_9_), channel_id=1, source_target_pairs={{0,4},{4,8},{8,12},{12,14},{14,10},{10,6},{6,2},{2,0},{1,5},{5,9},... | collective-permute-start | bytes 1397768 | tf_op jit(solution)/shard_map/ppermute | solution.py:464
  18.9 0.3 collective-permute-start.5
  19.2 9.3 %collective-permute-done.5.refs_5_ = bf16[160,1120]{1,0:T(8,128)(2,1)S(1)} collective-permute-done((bf16[160,1120]{1,0:T(8,128)(2,1)S(1)}, bf16[160,1120]{1,0:T(8,128)(2,1)S(1)}, u32[]{:S(2)}, u32[]{:S(2)}) %collective-permute-start.5) | collective-permute-done | bytes 358432 | tf_op jit(solution)/shard_map/ppermute | solution.py:468
  28.5 1.4 %collective-permute-done.4.refs_5_.refs_12_ = bf16[208,1120]{1,0:T(8,128)(2,1)S(1)} collective-permute-done((bf16[208,1120]{1,0:T(8,128)(2,1)S(1)}, bf16[208,1120]{1,0:T(8,128)(2,1)S(1)}, u32[]{:S(2)}, u32[]{:S(2)}) %collective-permute-start.4) | collective-permute-done | bytes 465952 | tf_op jit(solution)/shard_map/ppermute | solution.py:464
  29.9 1.3 %collective-permute-start.8 = (bf16[208,1120]{1,0:T(8,128)(2,1)S(1)}, bf16[208,1120]{1,0:T(8,128)(2,1)S(1)}, u32[]{:S(2)}, u32[]{:S(2)}) collective-permute-start(bf16[208,1120]{1,0:T(8,128)(2,1)S(1)} %collective-permute-done.3.refs_3_.refs_11_), channel_id=1, source_target_pairs={{0,4},{4,8},{8,12},{12,14},{14,10},{10,6},{6,2},{2,0},{1,5},{5,9},... | collective-permute-start | bytes 1397768 | tf_op jit(solution)/shard_map/ppermute | solution.py:464
  31.3 0.2 collective-permute-start.9
  31.5 0.3 collective-permute-start.10
  32.0 1.3 %collective-permute-start.6 = (bf16[144,1120]{1,0:T(8,128)(2,1)S(1)}, bf16[144,1120]{1,0:T(8,128)(2,1)S(1)}, u32[]{:S(2)}, u32[]{:S(2)}) collective-permute-start(bf16[144,1120]{1,0:T(8,128)(2,1)S(1)} %get-tuple-element.35.after_ref.refs_1_.refs_8_), channel_id=1, source_target_pairs={{0,4},{4,8},{8,12},{12,14},{14,10},{10,6},{6,2},{2,0},{1,5},{5,9},... | collective-permute-start | bytes 967688 | tf_op jit(solution)/shard_map/ppermute | solution.py:464
  33.3 4.7 %kv_part.2.refs_2_ = f32[1920,1120]{1,0:T(8,128)S(1)} custom-call(s32[10]{0:T(128)S(1)} %pad_add_fusion.meta, bf16[960,2304]{1,0:T(8,128)(2,1)S(1)} %pack_tokens.1.refs_0_, bf16[960,2304]{1,0:T(8,128)(2,1)S(1)} %collective-permute-done.2.refs_1_, bf16[208,1120]{1,0:T(8,128)(2,1)S(1)} %get-tuple-element.34.after_ref.refs_2_.refs_8_, ...), custom_call_target="tpu_custom_call" | custom-call | flops 3303014400 | tf_op jit(solution)/shard_map/kv_part/pallas_call | solution.py:68
  38.0 2.1 %collective-permute-done.10.refs_4_ = bf16[160,1120]{1,0:T(8,128)(2,1)S(1)} collective-permute-done((bf16[160,1120]{1,0:T(8,128)(2,1)S(1)}, bf16[160,1120]{1,0:T(8,128)(2,1)S(1)}, u32[]{:S(2)}, u32[]{:S(2)}) %collective-permute-start.10) | collective-permute-done | bytes 358432 | tf_op jit(solution)/shard_map/ppermute | solution.py:468
  40.1 1.3 %collective-permute-done.8.refs_3_ = bf16[208,1120]{1,0:T(8,128)(2,1)S(1)} collective-permute-done((bf16[208,1120]{1,0:T(8,128)(2,1)S(1)}, bf16[208,1120]{1,0:T(8,128)(2,1)S(1)}, u32[]{:S(2)}, u32[]{:S(2)}) %collective-permute-start.8) | collective-permute-done | bytes 465952 | tf_op jit(solution)/shard_map/ppermute | solution.py:464
  41.4 1.1 collective-permute-done.9.refs_5_
  42.6 0.3 collective-permute-start.13
  42.9 0.2 collective-permute-start.12
  43.2 1.3 %collective-permute-start.11 = (bf16[144,1120]{1,0:T(8,128)(2,1)S(1)}, bf16[144,1120]{1,0:T(8,128)(2,1)S(1)}, u32[]{:S(2)}, u32[]{:S(2)}) collective-permute-start(bf16[144,1120]{1,0:T(8,128)(2,1)S(1)} %slice.67), channel_id=1, source_target_pairs={{0,4},{4,8},{8,12},{12,14},{14,10},{10,6},{6,2},{2,0},{1,5},{5,9},... | collective-permute-start | bytes 967688 | tf_op jit(solution)/shard_map/ppermute | solution.py:464
  44.5 5.1 %collective-permute-done.7.refs_5_.refs_12_ = bf16[144,1120]{1,0:T(8,128)(2,1)S(1)} collective-permute-done((bf16[144,1120]{1,0:T(8,128)(2,1)S(1)}, bf16[144,1120]{1,0:T(8,128)(2,1)S(1)}, u32[]{:S(2)}, u32[]{:S(2)}) %collective-permute-start.7) | collective-permute-done | bytes 322592 | tf_op jit(solution)/shard_map/ppermute | solution.py:464
  49.6 1.2 %collective-permute-start.14 = (bf16[144,1120]{1,0:T(8,128)(2,1)S(1)}, bf16[144,1120]{1,0:T(8,128)(2,1)S(1)}, u32[]{:S(2)}, u32[]{:S(2)}) collective-permute-start(bf16[144,1120]{1,0:T(8,128)(2,1)S(1)} %collective-permute-done.6.refs_3_.refs_10_), channel_id=1, source_target_pairs={{0,4},{4,8},{8,12},{12,14},{14,10},{10,6},{6,2},{2,0},{1,5},{5,9},... | collective-permute-start | bytes 967688 | tf_op jit(solution)/shard_map/ppermute | solution.py:464
  50.8 0.3 collective-permute-start.15
  51.1 3.5 %kv_part.3.refs_2_ = f32[1920,1120]{1,0:T(8,128)S(1)} custom-call(s32[10]{0:T(128)S(1)} %pad_add_fusion.meta, bf16[960,2304]{1,0:T(8,128)(2,1)S(1)} %pack_tokens.1.refs_0_, bf16[960,2304]{1,0:T(8,128)(2,1)S(1)} %collective-permute-done.2.refs_1_, f32[1920,1120]{1,0:T(8,128)S(1)} %kv_part.2.refs_2_, ...), custom_call_target="tpu_custom_call", output_to_operand_aliasing={{}: (3, {})} | custom-call | flops 2202009600 | tf_op jit(solution)/shard_map/kv_part/pallas_call | solution.py:68
  54.6 2.1 %collective-permute-done.12.refs_7_ = bf16[144,1120]{1,0:T(8,128)(2,1)S(1)} collective-permute-done((bf16[144,1120]{1,0:T(8,128)(2,1)S(1)}, bf16[144,1120]{1,0:T(8,128)(2,1)S(1)}, u32[]{:S(2)}, u32[]{:S(2)}) %collective-permute-start.12) | collective-permute-done | bytes 322592 | tf_op jit(solution)/shard_map/ppermute | solution.py:464
  56.7 8.4 %states.1 = f32[560,128]{1,0:T(8,128)S(1)} custom-call(s32[10]{0:T(128)S(1)} %pad_add_fusion.meta, bf16[960,2304]{1,0:T(8,128)(2,1)S(1)} %pack_tokens.1.refs_0_, bf16[960,2304]{1,0:T(8,128)(2,1)S(1)} %collective-permute-done.2.refs_1_, f32[1920,1120]{1,0:T(8,128)S(1)} %kv_part.3.refs_2_, bf16[208,1120]{1,0:T(8,128)(2,1)S(1)} %collective-permute-done.8.refs_3_, ...), custom_call_target="tpu_custom_call" | custom-call | flops 4679270400 | tf_op jit(solution)/shard_map/states/pallas_call | solution.py:68
  65.1 1.2 %collective-permute-start.17 = (bf16[144,1120]{1,0:T(8,128)(2,1)S(1)}, bf16[144,1120]{1,0:T(8,128)(2,1)S(1)}, u32[]{:S(2)}, u32[]{:S(2)}) collective-permute-start(bf16[144,1120]{1,0:T(8,128)(2,1)S(1)} %collective-permute-done.14.refs_7_.refs_14_), channel_id=1, source_target_pairs={{0,4},{4,8},{8,12},{12,14},{14,10},{10,6},{6,2},{2,0},{1,5},{5,9},... | collective-permute-start | bytes 967688 | tf_op jit(solution)/shard_map/ppermute | solution.py:464
  66.3 0.3 collective-permute-start.18
  67.0 3.1 %collective-permute-start.16 = (bf16[560,128]{1,0:T(8,128)(2,1)S(1)}, bf16[560,128]{1,0:T(8,128)(2,1)S(1)}, u32[]{:S(2)}, u32[]{:S(2)}) collective-permute-start(bf16[560,128]{1,0:T(8,128)(2,1)S(1)} %pad_maximum_fusion.4), channel_id=1, source_target_pairs={{0,2},{2,4},{4,6},{6,8},{8,10},{10,12},{12,14},{1,3},{3,5},{5,7},{... | collective-permute-start | bytes 430088 | tf_op jit(solution)/shard_map/ppermute | solution.py:434
  70.1 5.1 %collective-permute-start.20 = (bf16[144,1120]{1,0:T(8,128)(2,1)S(1)}, bf16[144,1120]{1,0:T(8,128)(2,1)S(1)}, u32[]{:S(2)}, u32[]{:S(2)}) collective-permute-start(bf16[144,1120]{1,0:T(8,128)(2,1)S(1)} %collective-permute-done.6.refs_3_.refs_10_), channel_id=1, source_target_pairs={{0,1},{1,0},{2,3},{3,2},{4,5},{5,4},{6,7},{7,6},{8,9},{9,8},{10,11... | collective-permute-start | bytes 967688 | tf_op jit(solution)/shard_map/ppermute | solution.py:471
  75.2 5.3 %collective-permute-start.22 = (bf16[144,1120]{1,0:T(8,128)(2,1)S(1)}, bf16[144,1120]{1,0:T(8,128)(2,1)S(1)}, u32[]{:S(2)}, u32[]{:S(2)}) collective-permute-start(bf16[144,1120]{1,0:T(8,128)(2,1)S(1)} %collective-permute-done.14.refs_7_.refs_14_), channel_id=1, source_target_pairs={{0,1},{1,0},{2,3},{3,2},{4,5},{5,4},{6,7},{7,6},{8,9},{9,8},{10,11... | collective-permute-start | bytes 967688 | tf_op jit(solution)/shard_map/ppermute | solution.py:471
  80.6 0.6 collective-permute-start.25
  81.2 0.3 subtract_convert_fusion.1
  82.0 1.3 %collective-permute-start.27 = (bf16[80,1120]{1,0:T(8,128)(2,1)S(1)}, bf16[80,1120]{1,0:T(8,128)(2,1)S(1)}, u32[]{:S(2)}, u32[]{:S(2)}) collective-permute-start(bf16[80,1120]{1,0:T(8,128)(2,1)S(1)} %slice.79), channel_id=1, source_target_pairs={{0,4},{4,8},{8,12},{12,14},{14,10},{10,6},{6,2},{2,0},{1,5},{5,9},... | collective-permute-start | bytes 537608 | tf_op jit(solution)/shard_map/ppermute | solution.py:464
  83.3 1.5 %collective-permute-start.19 = (bf16[560,128]{1,0:T(8,128)(2,1)S(1)}, bf16[560,128]{1,0:T(8,128)(2,1)S(1)}, u32[]{:S(2)}, u32[]{:S(2)}) collective-permute-start(bf16[560,128]{1,0:T(8,128)(2,1)S(1)} %pad_maximum_fusion.5), channel_id=1, source_target_pairs={{0,4},{2,6},{4,8},{6,10},{8,12},{10,14},{1,5},{3,7},{5,9},{7,11},{... | collective-permute-start | bytes 430088 | tf_op jit(solution)/shard_map/ppermute | solution.py:434
  84.8 4.1 %q_early.1.refs_1_ = f32[960,1120]{1,0:T(8,128)S(1)} custom-call(s32[10]{0:T(128)S(1)} %pad_add_fusion.meta, bf16[960,2304]{1,0:T(8,128)(2,1)S(1)} %pack_tokens.1.refs_0_, bf16[144,1120]{1,0:T(8,128)(2,1)S(1)} %get-tuple-element.35.after_ref.refs_1_.refs_8_, bf16[144,1120]{1,0:T(8,128)(2,1)S(1)} %get-tuple-element.56.refs_2_.refs_9_, ...), custom_call_target="tpu_custom_call" | custom-call | flops 2752512000 | tf_op jit(solution)/shard_map/q_early/pallas_call | solution.py:68
  88.9 2.0 %collective-permute-done.19 = bf16[560,128]{1,0:T(8,128)(2,1)S(1)} collective-permute-done((bf16[560,128]{1,0:T(8,128)(2,1)S(1)}, bf16[560,128]{1,0:T(8,128)(2,1)S(1)}, u32[]{:S(2)}, u32[]{:S(2)}) %collective-permute-start.19) | collective-permute-done | bytes 143392 | tf_op jit(solution)/shard_map/ppermute | solution.py:434
  91.3 1.2 %collective-permute-start.29 = (bf16[144,1120]{1,0:T(8,128)(2,1)S(1)}, bf16[144,1120]{1,0:T(8,128)(2,1)S(1)}, u32[]{:S(2)}, u32[]{:S(2)}) collective-permute-start(bf16[144,1120]{1,0:T(8,128)(2,1)S(1)} %constant_dynamic-update-slice_fusion.refs_6_), channel_id=1, source_target_pairs={{0,1},{1,0},{2,3},{3,2},{4,5},{5,4},{6,7},{7,6},{8,9},{9,8},{10,11... | collective-permute-start | bytes 967688 | tf_op jit(solution)/shard_map/ppermute | solution.py:471
  92.7 1.3 %collective-permute-start.24 = (bf16[560,128]{1,0:T(8,128)(2,1)S(1)}, bf16[560,128]{1,0:T(8,128)(2,1)S(1)}, u32[]{:S(2)}, u32[]{:S(2)}) collective-permute-start(bf16[560,128]{1,0:T(8,128)(2,1)S(1)} %pad_maximum_fusion.6), channel_id=1, source_target_pairs={{0,8},{2,10},{4,12},{6,14},{1,9},{3,11},{5,13},{7,15},{16,24},{18,... | collective-permute-start | bytes 430088 | tf_op jit(solution)/shard_map/ppermute | solution.py:434
  94.0 3.5 %q_late.1.q_ref = bf16[960,1120]{1,0:T(8,128)(2,1)S(1)} custom-call(s32[10]{0:T(128)S(1)} %pad_add_fusion.meta, bf16[960,2304]{1,0:T(8,128)(2,1)S(1)} %pack_tokens.1.refs_0_, f32[960,1120]{1,0:T(8,128)S(1)} %q_early.1.refs_1_, bf16[144,1120]{1,0:T(8,128)(2,1)S(1)} %collective-permute-done.17.refs_2_, bf16[144,1120]{1,0:T(8,128)(2,1)S(1)} %collective-permute-done.25.refs_3_, ...), custom_call_target="tpu_custom_call" | custom-call | flops 2202009600 | tf_op jit(solution)/shard_map/q_late/pallas_call | solution.py:68
  97.5 6.7 %collective-permute-done.24 = bf16[560,128]{1,0:T(8,128)(2,1)S(1)} collective-permute-done((bf16[560,128]{1,0:T(8,128)(2,1)S(1)}, bf16[560,128]{1,0:T(8,128)(2,1)S(1)}, u32[]{:S(2)}, u32[]{:S(2)}) %collective-permute-start.24) | collective-permute-done | bytes 143392 | tf_op jit(solution)/shard_map/ppermute | solution.py:434
  104.8 0.5 collective-permute-start.30
  105.3 1.2 %collective-permute-done.30.theirs_ref = f32[560,128]{1,0:T(8,128)S(1)} collective-permute-done((f32[560,128]{1,0:T(8,128)S(1)}, f32[560,128]{1,0:T(8,128)S(1)}, u32[]{:S(2)}, u32[]{:S(2)}) %collective-permute-start.30) | collective-permute-done | bytes 286752 | tf_op jit(solution)/shard_map/ppermute | solution.py:471
  106.5 4.4 %attend.1 = bf16[960,1120]{1,0:T(8,128)(2,1)} custom-call(s32[10]{0:T(128)S(1)} %pad_add_fusion.meta, bf16[960,1120]{1,0:T(8,128)(2,1)S(1)} %q_late.1.q_ref, f32[560,128]{1,0:T(8,128)S(1)} %pad_maximum_fusion.3.mine_ref, f32[560,128]{1,0:T(8,128)S(1)} %collective-permute-done.30.theirs_ref), custom_call_target="tpu_custom_call" | custom-call | flops 1720320000 | bytes 4300800 | tf_op jit(solution)/shard_map/attend/pallas_call | solution.py:399
  (59 shorter events, 2.7 us)
Async XLA Ops:
  0.0 5.8 %copy-start = (bf16[2,6,80,2240]{3,2,1,0:T(8,128)(2,1)S(1)}, bf16[2,6,80,2240]{3,2,1,0:T(8,128)(2,1)}, u32[]{:S(2)}) copy-start(bf16[2,6,80,2240]{3,2,1,0:T(8,128)(2,1)} %param.3) | copy-start | bytes 12902404
  0.9 1.8 %copy-start.1 = (bf16[280,3360]{1,0:T(8,128)(2,1)S(1)}, bf16[280,3360]{1,0:T(8,128)(2,1)}, u32[]{:S(2)}) copy-start(bf16[280,3360]{1,0:T(8,128)(2,1)} %w_ref.3) | copy-start | bytes 5644804
  3.6 11.9 %collective-permute-start.1 = (bf16[208,1120]{1,0:T(8,128)(2,1)S(1)}, bf16[208,1120]{1,0:T(8,128)(2,1)S(1)}, u32[]{:S(2)}, u32[]{:S(2)}) collective-permute-start(bf16[208,1120]{1,0:T(8,128)(2,1)S(1)} %get-tuple-element.36.refs_3_), channel_id=1, source_target_pairs={{4,0},{8,4},{12,8},{14,12},{10,14},{6,10},{2,6},{0,2},{5,1},{9,5},... | collective-permute-start | bytes 1397768 | tf_op jit(solution)/shard_map/ppermute | solution.py:464
  3.8 11.7 %collective-permute-start = (bf16[208,1120]{1,0:T(8,128)(2,1)S(1)}, bf16[208,1120]{1,0:T(8,128)(2,1)S(1)}, u32[]{:S(2)}, u32[]{:S(2)}) collective-permute-start(bf16[208,1120]{1,0:T(8,128)(2,1)S(1)} %get-tuple-element.34.after_ref.refs_2_.refs_8_), channel_id=1, source_target_pairs={{0,4},{4,8},{8,12},{12,14},{14,10},{10,6},{6,2},{2,0},{1,5},{5,9},... | collective-permute-start | bytes 1397768 | tf_op jit(solution)/shard_map/ppermute | solution.py:464
  15.5 14.4 %collective-permute-start.2 = (bf16[960,2304]{1,0:T(8,128)(2,1)S(1)}, bf16[960,2304]{1,0:T(8,128)(2,1)S(1)}, u32[]{:S(2)}, u32[]{:S(2)}) collective-permute-start(bf16[960,2304]{1,0:T(8,128)(2,1)S(1)} %pack_tokens.1.refs_0_), channel_id=1, source_target_pairs={{0,1},{1,0},{2,3},{3,2},{4,5},{5,4},{6,7},{7,6},{8,9},{9,8},{10,11... | collective-permute-start | bytes 13271048 | tf_op jit(solution)/shard_map/ppermute | solution.py:471
  17.2 12.6 %collective-permute-start.4 = (bf16[208,1120]{1,0:T(8,128)(2,1)S(1)}, bf16[208,1120]{1,0:T(8,128)(2,1)S(1)}, u32[]{:S(2)}, u32[]{:S(2)}) collective-permute-start(bf16[208,1120]{1,0:T(8,128)(2,1)S(1)} %collective-permute-done.1.refs_6_.refs_10_), channel_id=1, source_target_pairs={{4,0},{8,4},{12,8},{14,12},{10,14},{6,10},{2,6},{0,2},{5,1},{9,5},... | collective-permute-start | bytes 1397768 | tf_op jit(solution)/shard_map/ppermute | solution.py:464
  17.5 12.4 %collective-permute-start.3 = (bf16[208,1120]{1,0:T(8,128)(2,1)S(1)}, bf16[208,1120]{1,0:T(8,128)(2,1)S(1)}, u32[]{:S(2)}, u32[]{:S(2)}) collective-permute-start(bf16[208,1120]{1,0:T(8,128)(2,1)S(1)} %collective-permute-done.refs_4_.refs_9_), channel_id=1, source_target_pairs={{0,4},{4,8},{8,12},{12,14},{14,10},{10,6},{6,2},{2,0},{1,5},{5,9},... | collective-permute-start | bytes 1397768 | tf_op jit(solution)/shard_map/ppermute | solution.py:464
  18.9 9.6 %collective-permute-start.5 = (bf16[160,1120]{1,0:T(8,128)(2,1)S(1)}, bf16[160,1120]{1,0:T(8,128)(2,1)S(1)}, u32[]{:S(2)}, u32[]{:S(2)}) collective-permute-start(bf16[160,1120]{1,0:T(8,128)(2,1)S(1)} %pad_maximum_fusion), channel_id=1, source_target_pairs={{0,16},{16,0},{1,17},{17,1},{2,18},{18,2},{3,19},{19,3},{4,20},{20... | collective-permute-start | bytes 1075208 | tf_op jit(solution)/shard_map/ppermute | solution.py:468
  29.9 11.5 %collective-permute-start.8 = (bf16[208,1120]{1,0:T(8,128)(2,1)S(1)}, bf16[208,1120]{1,0:T(8,128)(2,1)S(1)}, u32[]{:S(2)}, u32[]{:S(2)}) collective-permute-start(bf16[208,1120]{1,0:T(8,128)(2,1)S(1)} %collective-permute-done.3.refs_3_.refs_11_), channel_id=1, source_target_pairs={{0,4},{4,8},{8,12},{12,14},{14,10},{10,6},{6,2},{2,0},{1,5},{5,9},... | collective-permute-start | bytes 1397768 | tf_op jit(solution)/shard_map/ppermute | solution.py:464
  31.3 11.2 %collective-permute-start.9 = (bf16[208,1120]{1,0:T(8,128)(2,1)S(1)}, bf16[208,1120]{1,0:T(8,128)(2,1)S(1)}, u32[]{:S(2)}, u32[]{:S(2)}) collective-permute-start(bf16[208,1120]{1,0:T(8,128)(2,1)S(1)} %collective-permute-done.4.refs_5_.refs_12_), channel_id=1, source_target_pairs={{4,0},{8,4},{12,8},{14,12},{10,14},{6,10},{2,6},{0,2},{5,1},{9,5},... | collective-permute-start | bytes 1397768 | tf_op jit(solution)/shard_map/ppermute | solution.py:464
  31.5 8.6 %collective-permute-start.10 = (bf16[160,1120]{1,0:T(8,128)(2,1)S(1)}, bf16[160,1120]{1,0:T(8,128)(2,1)S(1)}, u32[]{:S(2)}, u32[]{:S(2)}) collective-permute-start(bf16[160,1120]{1,0:T(8,128)(2,1)S(1)} %pad_maximum_fusion.1), channel_id=1, source_target_pairs={{0,16},{16,0},{1,17},{17,1},{2,18},{18,2},{3,19},{19,3},{4,20},{20... | collective-permute-start | bytes 1075208 | tf_op jit(solution)/shard_map/ppermute | solution.py:468
  31.9 17.7 %collective-permute-start.7 = (bf16[144,1120]{1,0:T(8,128)(2,1)S(1)}, bf16[144,1120]{1,0:T(8,128)(2,1)S(1)}, u32[]{:S(2)}, u32[]{:S(2)}) collective-permute-start(bf16[144,1120]{1,0:T(8,128)(2,1)S(1)} %get-tuple-element.35.after_ref.refs_1_.refs_8_), channel_id=1, source_target_pairs={{4,0},{8,4},{12,8},{14,12},{10,14},{6,10},{2,6},{0,2},{5,1},{9,5},... | collective-permute-start | bytes 967688 | tf_op jit(solution)/shard_map/ppermute | solution.py:464
  32.0 17.6 %collective-permute-start.6 = (bf16[144,1120]{1,0:T(8,128)(2,1)S(1)}, bf16[144,1120]{1,0:T(8,128)(2,1)S(1)}, u32[]{:S(2)}, u32[]{:S(2)}) collective-permute-start(bf16[144,1120]{1,0:T(8,128)(2,1)S(1)} %get-tuple-element.35.after_ref.refs_1_.refs_8_), channel_id=1, source_target_pairs={{0,4},{4,8},{8,12},{12,14},{14,10},{10,6},{6,2},{2,0},{1,5},{5,9},... | collective-permute-start | bytes 967688 | tf_op jit(solution)/shard_map/ppermute | solution.py:464
  42.6 14.1 %collective-permute-start.13 = (bf16[160,1120]{1,0:T(8,128)(2,1)S(1)}, bf16[160,1120]{1,0:T(8,128)(2,1)S(1)}, u32[]{:S(2)}, u32[]{:S(2)}) collective-permute-start(bf16[160,1120]{1,0:T(8,128)(2,1)S(1)} %pad_maximum_fusion.2), channel_id=1, source_target_pairs={{0,16},{16,0},{1,17},{17,1},{2,18},{18,2},{3,19},{19,3},{4,20},{20... | collective-permute-start | bytes 1075208 | tf_op jit(solution)/shard_map/ppermute | solution.py:468
  42.9 13.8 %collective-permute-start.12 = (bf16[144,1120]{1,0:T(8,128)(2,1)S(1)}, bf16[144,1120]{1,0:T(8,128)(2,1)S(1)}, u32[]{:S(2)}, u32[]{:S(2)}) collective-permute-start(bf16[144,1120]{1,0:T(8,128)(2,1)S(1)} %slice.68), channel_id=1, source_target_pairs={{4,0},{8,4},{12,8},{14,12},{10,14},{6,10},{2,6},{0,2},{5,1},{9,5},... | collective-permute-start | bytes 967688 | tf_op jit(solution)/shard_map/ppermute | solution.py:464
  43.2 13.5 %collective-permute-start.11 = (bf16[144,1120]{1,0:T(8,128)(2,1)S(1)}, bf16[144,1120]{1,0:T(8,128)(2,1)S(1)}, u32[]{:S(2)}, u32[]{:S(2)}) collective-permute-start(bf16[144,1120]{1,0:T(8,128)(2,1)S(1)} %slice.67), channel_id=1, source_target_pairs={{0,4},{4,8},{8,12},{12,14},{14,10},{10,6},{6,2},{2,0},{1,5},{5,9},... | collective-permute-start | bytes 967688 | tf_op jit(solution)/shard_map/ppermute | solution.py:464
  49.6 15.5 %collective-permute-start.14 = (bf16[144,1120]{1,0:T(8,128)(2,1)S(1)}, bf16[144,1120]{1,0:T(8,128)(2,1)S(1)}, u32[]{:S(2)}, u32[]{:S(2)}) collective-permute-start(bf16[144,1120]{1,0:T(8,128)(2,1)S(1)} %collective-permute-done.6.refs_3_.refs_10_), channel_id=1, source_target_pairs={{0,4},{4,8},{8,12},{12,14},{14,10},{10,6},{6,2},{2,0},{1,5},{5,9},... | collective-permute-start | bytes 967688 | tf_op jit(solution)/shard_map/ppermute | solution.py:464
  50.8 14.3 %collective-permute-start.15 = (bf16[144,1120]{1,0:T(8,128)(2,1)S(1)}, bf16[144,1120]{1,0:T(8,128)(2,1)S(1)}, u32[]{:S(2)}, u32[]{:S(2)}) collective-permute-start(bf16[144,1120]{1,0:T(8,128)(2,1)S(1)} %collective-permute-done.7.refs_5_.refs_12_), channel_id=1, source_target_pairs={{4,0},{8,4},{12,8},{14,12},{10,14},{6,10},{2,6},{0,2},{5,1},{9,5},... | collective-permute-start | bytes 967688 | tf_op jit(solution)/shard_map/ppermute | solution.py:464
  65.1 15.4 %collective-permute-start.17 = (bf16[144,1120]{1,0:T(8,128)(2,1)S(1)}, bf16[144,1120]{1,0:T(8,128)(2,1)S(1)}, u32[]{:S(2)}, u32[]{:S(2)}) collective-permute-start(bf16[144,1120]{1,0:T(8,128)(2,1)S(1)} %collective-permute-done.14.refs_7_.refs_14_), channel_id=1, source_target_pairs={{0,4},{4,8},{8,12},{12,14},{14,10},{10,6},{6,2},{2,0},{1,5},{5,9},... | collective-permute-start | bytes 967688 | tf_op jit(solution)/shard_map/ppermute | solution.py:464
  66.3 14.2 %collective-permute-start.18 = (bf16[144,1120]{1,0:T(8,128)(2,1)S(1)}, bf16[144,1120]{1,0:T(8,128)(2,1)S(1)}, u32[]{:S(2)}, u32[]{:S(2)}) collective-permute-start(bf16[144,1120]{1,0:T(8,128)(2,1)S(1)} %collective-permute-done.15.refs_9_.refs_16_), channel_id=1, source_target_pairs={{4,0},{8,4},{12,8},{14,12},{10,14},{6,10},{2,6},{0,2},{5,1},{9,5},... | collective-permute-start | bytes 967688 | tf_op jit(solution)/shard_map/ppermute | solution.py:464
  67.0 8.2 %collective-permute-start.16 = (bf16[560,128]{1,0:T(8,128)(2,1)S(1)}, bf16[560,128]{1,0:T(8,128)(2,1)S(1)}, u32[]{:S(2)}, u32[]{:S(2)}) collective-permute-start(bf16[560,128]{1,0:T(8,128)(2,1)S(1)} %pad_maximum_fusion.4), channel_id=1, source_target_pairs={{0,2},{2,4},{4,6},{6,8},{8,10},{10,12},{12,14},{1,3},{3,5},{5,7},{... | collective-permute-start | bytes 430088 | tf_op jit(solution)/shard_map/ppermute | solution.py:434
  70.1 11.6 %collective-permute-start.20 = (bf16[144,1120]{1,0:T(8,128)(2,1)S(1)}, bf16[144,1120]{1,0:T(8,128)(2,1)S(1)}, u32[]{:S(2)}, u32[]{:S(2)}) collective-permute-start(bf16[144,1120]{1,0:T(8,128)(2,1)S(1)} %collective-permute-done.6.refs_3_.refs_10_), channel_id=1, source_target_pairs={{0,1},{1,0},{2,3},{3,2},{4,5},{5,4},{6,7},{7,6},{8,9},{9,8},{10,11... | collective-permute-start | bytes 967688 | tf_op jit(solution)/shard_map/ppermute | solution.py:471
  75.1 6.6 %collective-permute-start.21 = (bf16[144,1120]{1,0:T(8,128)(2,1)S(1)}, bf16[144,1120]{1,0:T(8,128)(2,1)S(1)}, u32[]{:S(2)}, u32[]{:S(2)}) collective-permute-start(bf16[144,1120]{1,0:T(8,128)(2,1)S(1)} %collective-permute-done.7.refs_5_.refs_12_), channel_id=1, source_target_pairs={{0,1},{1,0},{2,3},{3,2},{4,5},{5,4},{6,7},{7,6},{8,9},{9,8},{10,11... | collective-permute-start | bytes 967688 | tf_op jit(solution)/shard_map/ppermute | solution.py:471
  75.2 6.8 %collective-permute-start.22 = (bf16[144,1120]{1,0:T(8,128)(2,1)S(1)}, bf16[144,1120]{1,0:T(8,128)(2,1)S(1)}, u32[]{:S(2)}, u32[]{:S(2)}) collective-permute-start(bf16[144,1120]{1,0:T(8,128)(2,1)S(1)} %collective-permute-done.14.refs_7_.refs_14_), channel_id=1, source_target_pairs={{0,1},{1,0},{2,3},{3,2},{4,5},{5,4},{6,7},{7,6},{8,9},{9,8},{10,11... | collective-permute-start | bytes 967688 | tf_op jit(solution)/shard_map/ppermute | solution.py:471
  80.5 2.8 %collective-permute-start.23 = (bf16[144,1120]{1,0:T(8,128)(2,1)S(1)}, bf16[144,1120]{1,0:T(8,128)(2,1)S(1)}, u32[]{:S(2)}, u32[]{:S(2)}) collective-permute-start(bf16[144,1120]{1,0:T(8,128)(2,1)S(1)} %collective-permute-done.15.refs_9_.refs_16_), channel_id=1, source_target_pairs={{0,1},{1,0},{2,3},{3,2},{4,5},{5,4},{6,7},{7,6},{8,9},{9,8},{10,11... | collective-permute-start | bytes 967688 | tf_op jit(solution)/shard_map/ppermute | solution.py:471
  80.6 13.4 %collective-permute-start.25 = (bf16[144,1120]{1,0:T(8,128)(2,1)S(1)}, bf16[144,1120]{1,0:T(8,128)(2,1)S(1)}, u32[]{:S(2)}, u32[]{:S(2)}) collective-permute-start(bf16[144,1120]{1,0:T(8,128)(2,1)S(1)} %collective-permute-done.17.refs_2_), channel_id=1, source_target_pairs={{0,1},{1,0},{2,3},{3,2},{4,5},{5,4},{6,7},{7,6},{8,9},{9,8},{10,11... | collective-permute-start | bytes 967688 | tf_op jit(solution)/shard_map/ppermute | solution.py:471
  81.7 12.3 %collective-permute-start.26 = (bf16[144,1120]{1,0:T(8,128)(2,1)S(1)}, bf16[144,1120]{1,0:T(8,128)(2,1)S(1)}, u32[]{:S(2)}, u32[]{:S(2)}) collective-permute-start(bf16[144,1120]{1,0:T(8,128)(2,1)S(1)} %collective-permute-done.18.refs_4_), channel_id=1, source_target_pairs={{0,1},{1,0},{2,3},{3,2},{4,5},{5,4},{6,7},{7,6},{8,9},{9,8},{10,11... | collective-permute-start | bytes 967688 | tf_op jit(solution)/shard_map/ppermute | solution.py:471
  81.8 9.5 %collective-permute-start.28 = (bf16[64,1120]{1,0:T(8,128)(2,1)S(1)}, bf16[64,1120]{1,0:T(8,128)(2,1)S(1)}, u32[]{:S(2)}, u32[]{:S(2)}) collective-permute-start(bf16[64,1120]{1,0:T(8,128)(2,1)S(1)} %slice.80), channel_id=1, source_target_pairs={{4,0},{8,4},{12,8},{14,12},{10,14},{6,10},{2,6},{0,2},{5,1},{9,5},... | collective-permute-start | bytes 430088 | tf_op jit(solution)/shard_map/ppermute | solution.py:464
  82.0 9.2 %collective-permute-start.27 = (bf16[80,1120]{1,0:T(8,128)(2,1)S(1)}, bf16[80,1120]{1,0:T(8,128)(2,1)S(1)}, u32[]{:S(2)}, u32[]{:S(2)}) collective-permute-start(bf16[80,1120]{1,0:T(8,128)(2,1)S(1)} %slice.79), channel_id=1, source_target_pairs={{0,4},{4,8},{8,12},{12,14},{14,10},{10,6},{6,2},{2,0},{1,5},{5,9},... | collective-permute-start | bytes 537608 | tf_op jit(solution)/shard_map/ppermute | solution.py:464
  83.3 7.6 %collective-permute-start.19 = (bf16[560,128]{1,0:T(8,128)(2,1)S(1)}, bf16[560,128]{1,0:T(8,128)(2,1)S(1)}, u32[]{:S(2)}, u32[]{:S(2)}) collective-permute-start(bf16[560,128]{1,0:T(8,128)(2,1)S(1)} %pad_maximum_fusion.5), channel_id=1, source_target_pairs={{0,4},{2,6},{4,8},{6,10},{8,12},{10,14},{1,5},{3,7},{5,9},{7,11},{... | collective-permute-start | bytes 430088 | tf_op jit(solution)/shard_map/ppermute | solution.py:434
  91.3 2.8 %collective-permute-start.29 = (bf16[144,1120]{1,0:T(8,128)(2,1)S(1)}, bf16[144,1120]{1,0:T(8,128)(2,1)S(1)}, u32[]{:S(2)}, u32[]{:S(2)}) collective-permute-start(bf16[144,1120]{1,0:T(8,128)(2,1)S(1)} %constant_dynamic-update-slice_fusion.refs_6_), channel_id=1, source_target_pairs={{0,1},{1,0},{2,3},{3,2},{4,5},{5,4},{6,7},{7,6},{8,9},{9,8},{10,11... | collective-permute-start | bytes 967688 | tf_op jit(solution)/shard_map/ppermute | solution.py:471
  92.7 11.5 %collective-permute-start.24 = (bf16[560,128]{1,0:T(8,128)(2,1)S(1)}, bf16[560,128]{1,0:T(8,128)(2,1)S(1)}, u32[]{:S(2)}, u32[]{:S(2)}) collective-permute-start(bf16[560,128]{1,0:T(8,128)(2,1)S(1)} %pad_maximum_fusion.6), channel_id=1, source_target_pairs={{0,8},{2,10},{4,12},{6,14},{1,9},{3,11},{5,13},{7,15},{16,24},{18,... | collective-permute-start | bytes 430088 | tf_op jit(solution)/shard_map/ppermute | solution.py:434
  104.8 1.7 %collective-permute-start.30 = (f32[560,128]{1,0:T(8,128)S(1)}, f32[560,128]{1,0:T(8,128)S(1)}, u32[]{:S(2)}, u32[]{:S(2)}) collective-permute-start(f32[560,128]{1,0:T(8,128)S(1)} %pad_maximum_fusion.3.mine_ref), channel_id=1, source_target_pairs={{0,1},{1,0},{2,3},{3,2},{4,5},{5,4},{6,7},{7,6},{8,9},{9,8},{10,11... | collective-permute-start | bytes 860168 | tf_op jit(solution)/shard_map/ppermute | solution.py:471

commit v5 on v4

--- a/solution.py
+++ b/solution.py
@@ -58,7 +58,7 @@
 
 
 def split_rows(rows):
-    third = DEPTH // 48 * 16
+    third = ceil_to(DEPTH // 3, 16)
     spare = ceil_to((rows - DEPTH + 1) // 2, 16)
     return third, DEPTH - 2 * third, spare
 
@@ -424,21 +424,36 @@
 
 
 def running_total(states, sums, count, alongside=None):
-    reach, hop = 1, 0
     wide, room = states.shape[-1], sums.shape[-1]
-    while reach < count:
-        pairs = [(i, i + reach) for i in range(count - reach)]
+    hops = []
+
+    def send(values, pairs):
+        states, sums = values
         upper = sums.astype(BF)
         lower = (sums - upper.astype(F32)).astype(BF)
-        sent = jnp.concatenate([states.astype(BF), upper, lower], axis=-1)
-        got = lax.ppermute(sent, "tm", pairs)
+        got = lax.ppermute(jnp.concatenate([states.astype(BF), upper, lower], axis=-1), "tm", pairs)
         if alongside is not None:
-            got = alongside(hop, got)
+            got = alongside(len(hops), got)
+        hops.append(got)
         got = got.astype(F32)
-        states = states + got[..., :wide]
-        sums = sums + (got[..., wide : wide + room] + got[..., wide + room :])
-        reach, hop = reach * 2, hop + 1
-    return states, sums
+        return got[..., :wide], got[..., wide : wide + room] + got[..., wide + room :]
+
+    def add(one, two):
+        return one[0] + two[0], one[1] + two[1]
+
+    window, total = (states, sums), (states, sums)
+    stride = 1
+    if count % 2 == 0:
+        stride = 2
+        partner = send(window, swap_pairs(count))
+        window = add(window, partner)
+        second = lax.rem(lax.axis_index("tm"), 2) == 1
+        total = tuple(jnp.where(second, both, own) for both, own in zip(window, total))
+    while stride < count:
+        got = send(window, [(i, i + stride) for i in range(count - stride)])
+        total, window = add(total, got), add(window, got)
+        stride *= 2
+    return total
 
 
 def tie(*values):

time: 111 us -> 110 us (level)
  waiting for transfers between devices: 39.5 us -> 34.2 us
  local copies, waits for them, and re-layouts: 2.83 us -> 5.1 us
  starting transfers between devices: 33.5 us -> 35.1 us
    ppermute x3, waiting for transfers between devices: 11.5 us -> 1.9 us  [plane_swap(): return lax.ppermute(value, 'groups', across)]
    ppermute x16, waiting for transfers between devices: 18.1 us -> 24.7 us  [ring(): return lax.ppermute(value, 'tm', forward if up else backward)]
    ppermute x3, waiting for transfers between devices: 8.73 us -> 6.45 us  [send(): lax.ppermute(jnp.concatenate([states.astype(BF), upper, lower], axis=-1),...]
    unnamed x5 -> x9, local copies, waits for them, and re-layouts: 1.78 us -> 4.03 us
    ppermute x9, starting transfers between devices: 14.6 us -> 16.7 us  [core_swap(): return lax.ppermute(value, 'space', over)]
    ppermute x3, starting transfers between devices: 5.85 us -> 4.27 us  [send(): lax.ppermute(jnp.concatenate([states.astype(BF), upper, lower], axis=-1),...]
    ppermute x3, starting transfers between devices: 0.96 us -> 2.08 us  [plane_swap(): return lax.ppermute(value, 'groups', across)]
  transfers between devices with their start and end apart: 31 -> 31, of which waited for: 11 -> 9; matrix products, arithmetic and copies ran while one was open for 1% -> 1% of each run, Pallas kernels for 25% -> 25%
where the time goes in v5:
time: 110 us
  starting transfers between devices  35.1 us (32%)
  waiting for transfers between devices  34.2 us (31%)
  Pallas kernels  32.6 us (30%)
  local copies, waits for them, and re-layouts  5.1 us (5%)
  other arithmetic  2.23 us (2%)
    pallas_call x7, Pallas kernels, resident(): pl.pallas_call(kernel, in_specs=[pl.BlockSpec(memory_space=pltpu.SMEM)] +...  25.6 us
    ppermute x16, waiting for transfers between devices, ring(): return lax.ppermute(value, 'tm', forward if up else backward)  24.7 us
    ppermute x9, starting transfers between devices, core_swap(): return lax.ppermute(value, 'space', over)  16.7 us
    ppermute x16, starting transfers between devices, ring(): return lax.ppermute(value, 'tm', forward if up else backward)  12 us
    ppermute x3, waiting for transfers between devices, send(): lax.ppermute(jnp.concatenate([states.astype(BF), upper, lower], axis=-1),...  6.45 us
    pallas_call x1, Pallas kernels, attend(): pl.pallas_call(functools.partial(attend_kernel, heads_here=heads_here), i...  4.39 us
    ppermute x3, starting transfers between devices, send(): lax.ppermute(jnp.concatenate([states.astype(BF), upper, lower], axis=-1),...  4.27 us
    unnamed x9, local copies, waits for them, and re-layouts  4.03 us
  transfers between devices with their start and end apart: 31, of which 9 were waited for; matrix products, arithmetic and copies ran while one was open for 1% of the time, Pallas kernels for 25%

profile of v5, /device:TPU:27, one launch (start us, length us, event | category | flops | bytes accessed | tf_op | source)
XLA Modules:
  0.0 109.8 jit_solution(17209589045966122080)
XLA Ops:
  0.0 0.8 dynamic-slice_bitcast_fusion
  0.9 1.8 %copy-done.3 = bf16[280,3360]{1,0:T(8,128)(2,1)S(1)} copy-done((bf16[280,3360]{1,0:T(8,128)(2,1)S(1)}, bf16[280,3360]{1,0:T(8,128)(2,1)}, u32[]{:S(2)}) %copy-start.3) | copy-done | bytes 1881624
  2.7 0.9 pack_first.1
  3.6 0.2 collective-permute-start.1
  3.8 1.3 %collective-permute-start = (bf16[192,1120]{1,0:T(8,128)(2,1)S(1)}, bf16[192,1120]{1,0:T(8,128)(2,1)S(1)}, u32[]{:S(2)}, u32[]{:S(2)}) collective-permute-start(bf16[192,1120]{1,0:T(8,128)(2,1)S(1)} %get-tuple-element.34.after_ref.refs_2_.refs_8_), channel_id=1, source_target_pairs={{0,4},{4,8},{8,12},{12,14},{14,10},{10,6},{6,2},{2,0},{1,5},{5,9},... | collective-permute-start | bytes 1290248 | tf_op jit(solution)/shard_map/ppermute | solution.py:479
  5.1 0.6 pack_rest.1
  5.7 2.6 %pack_tokens.1.refs_0_ = bf16[960,2304]{1,0:T(8,128)(2,1)S(1)} custom-call(bf16[960,2240]{1,0:T(8,128)(2,1)S(1)} %bitcast.6, bf16[144,1120]{1,0:T(8,128)(2,1)S(1)} %get-tuple-element.35.after_ref.refs_1_.refs_8_), custom_call_target="tpu_custom_call" | custom-call | bytes 8601600 | tf_op jit(solution)/shard_map/pack_tokens/pallas_call | solution.py:156
  8.4 6.3 %collective-permute-done.1.refs_6_.refs_10_ = bf16[192,1120]{1,0:T(8,128)(2,1)S(1)} collective-permute-done((bf16[192,1120]{1,0:T(8,128)(2,1)S(1)}, bf16[192,1120]{1,0:T(8,128)(2,1)S(1)}, u32[]{:S(2)}, u32[]{:S(2)}) %collective-permute-start.1) | collective-permute-done | bytes 430112 | tf_op jit(solution)/shard_map/ppermute | solution.py:479
  14.7 1.7 %collective-permute-start.2 = (bf16[960,2304]{1,0:T(8,128)(2,1)S(1)}, bf16[960,2304]{1,0:T(8,128)(2,1)S(1)}, u32[]{:S(2)}, u32[]{:S(2)}) collective-permute-start(bf16[960,2304]{1,0:T(8,128)(2,1)S(1)} %pack_tokens.1.refs_0_), channel_id=1, source_target_pairs={{0,1},{1,0},{2,3},{3,2},{4,5},{5,4},{6,7},{7,6},{8,9},{9,8},{10,11... | collective-permute-start | bytes 13271048 | tf_op jit(solution)/shard_map/ppermute | solution.py:486
  16.5 0.2 collective-permute-start.4
  16.7 0.3 collective-permute-start.5
  17.0 1.3 %collective-permute-start.3 = (bf16[192,1120]{1,0:T(8,128)(2,1)S(1)}, bf16[192,1120]{1,0:T(8,128)(2,1)S(1)}, u32[]{:S(2)}, u32[]{:S(2)}) collective-permute-start(bf16[192,1120]{1,0:T(8,128)(2,1)S(1)} %collective-permute-done.refs_4_.refs_9_), channel_id=1, source_target_pairs={{0,4},{4,8},{8,12},{12,14},{14,10},{10,6},{6,2},{2,0},{1,5},{5,9},... | collective-permute-start | bytes 1290248 | tf_op jit(solution)/shard_map/ppermute | solution.py:479
  18.3 10.1 %collective-permute-done.4.refs_5_.refs_12_ = bf16[192,1120]{1,0:T(8,128)(2,1)S(1)} collective-permute-done((bf16[192,1120]{1,0:T(8,128)(2,1)S(1)}, bf16[192,1120]{1,0:T(8,128)(2,1)S(1)}, u32[]{:S(2)}, u32[]{:S(2)}) %collective-permute-start.4) | collective-permute-done | bytes 430112 | tf_op jit(solution)/shard_map/ppermute | solution.py:479
  28.5 1.1 collective-permute-start.10
  29.5 1.3 %collective-permute-start.8 = (bf16[192,1120]{1,0:T(8,128)(2,1)S(1)}, bf16[192,1120]{1,0:T(8,128)(2,1)S(1)}, u32[]{:S(2)}, u32[]{:S(2)}) collective-permute-start(bf16[192,1120]{1,0:T(8,128)(2,1)S(1)} %collective-permute-done.3.refs_3_.refs_11_), channel_id=1, source_target_pairs={{0,4},{4,8},{8,12},{12,14},{14,10},{10,6},{6,2},{2,0},{1,5},{5,9},... | collective-permute-start | bytes 1290248 | tf_op jit(solution)/shard_map/ppermute | solution.py:479
  31.2 1.3 %collective-permute-start.6 = (bf16[144,1120]{1,0:T(8,128)(2,1)S(1)}, bf16[144,1120]{1,0:T(8,128)(2,1)S(1)}, u32[]{:S(2)}, u32[]{:S(2)}) collective-permute-start(bf16[144,1120]{1,0:T(8,128)(2,1)S(1)} %get-tuple-element.35.after_ref.refs_1_.refs_8_), channel_id=1, source_target_pairs={{0,4},{4,8},{8,12},{12,14},{14,10},{10,6},{6,2},{2,0},{1,5},{5,9},... | collective-permute-start | bytes 967688 | tf_op jit(solution)/shard_map/ppermute | solution.py:479
  32.4 4.6 %kv_part.2.refs_2_ = f32[1920,1120]{1,0:T(8,128)S(1)} custom-call(s32[10]{0:T(128)S(1)} %pad_add_fusion.meta, bf16[960,2304]{1,0:T(8,128)(2,1)S(1)} %pack_tokens.1.refs_0_, bf16[960,2304]{1,0:T(8,128)(2,1)S(1)} %collective-permute-done.2.refs_1_, bf16[192,1120]{1,0:T(8,128)(2,1)S(1)} %get-tuple-element.34.after_ref.refs_2_.refs_8_, ...), custom_call_target="tpu_custom_call" | custom-call | flops 3303014400 | tf_op jit(solution)/shard_map/kv_part/pallas_call | solution.py:68
  37.1 1.9 %collective-permute-done.10.refs_4_ = bf16[192,1120]{1,0:T(8,128)(2,1)S(1)} collective-permute-done((bf16[192,1120]{1,0:T(8,128)(2,1)S(1)}, bf16[192,1120]{1,0:T(8,128)(2,1)S(1)}, u32[]{:S(2)}, u32[]{:S(2)}) %collective-permute-start.10) | collective-permute-done | bytes 430112 | tf_op jit(solution)/shard_map/ppermute | solution.py:483
  39.0 0.5 collective-permute-done.8.refs_3_
  39.5 1.0 collective-permute-done.9.refs_5_
  40.6 0.8 collective-permute-start.13
  41.4 0.2 collective-permute-start.12
  41.6 1.3 %collective-permute-start.11 = (bf16[144,1120]{1,0:T(8,128)(2,1)S(1)}, bf16[144,1120]{1,0:T(8,128)(2,1)S(1)}, u32[]{:S(2)}, u32[]{:S(2)}) collective-permute-start(bf16[144,1120]{1,0:T(8,128)(2,1)S(1)} %slice.67), channel_id=1, source_target_pairs={{0,4},{4,8},{8,12},{12,14},{14,10},{10,6},{6,2},{2,0},{1,5},{5,9},... | collective-permute-start | bytes 967688 | tf_op jit(solution)/shard_map/ppermute | solution.py:479
  42.9 4.7 %collective-permute-done.7.refs_5_.refs_12_ = bf16[144,1120]{1,0:T(8,128)(2,1)S(1)} collective-permute-done((bf16[144,1120]{1,0:T(8,128)(2,1)S(1)}, bf16[144,1120]{1,0:T(8,128)(2,1)S(1)}, u32[]{:S(2)}, u32[]{:S(2)}) %collective-permute-start.7) | collective-permute-done | bytes 322592 | tf_op jit(solution)/shard_map/ppermute | solution.py:479
  47.6 1.3 %collective-permute-start.14 = (bf16[144,1120]{1,0:T(8,128)(2,1)S(1)}, bf16[144,1120]{1,0:T(8,128)(2,1)S(1)}, u32[]{:S(2)}, u32[]{:S(2)}) collective-permute-start(bf16[144,1120]{1,0:T(8,128)(2,1)S(1)} %collective-permute-done.6.refs_3_.refs_10_), channel_id=1, source_target_pairs={{0,4},{4,8},{8,12},{12,14},{14,10},{10,6},{6,2},{2,0},{1,5},{5,9},... | collective-permute-start | bytes 967688 | tf_op jit(solution)/shard_map/ppermute | solution.py:479
  49.1 3.5 %kv_part.3.refs_2_ = f32[1920,1120]{1,0:T(8,128)S(1)} custom-call(s32[10]{0:T(128)S(1)} %pad_add_fusion.meta, bf16[960,2304]{1,0:T(8,128)(2,1)S(1)} %pack_tokens.1.refs_0_, bf16[960,2304]{1,0:T(8,128)(2,1)S(1)} %collective-permute-done.2.refs_1_, f32[1920,1120]{1,0:T(8,128)S(1)} %kv_part.2.refs_2_, ...), custom_call_target="tpu_custom_call", output_to_operand_aliasing={{}: (3, {})} | custom-call | flops 2202009600 | tf_op jit(solution)/shard_map/kv_part/pallas_call | solution.py:68
  52.6 2.1 %collective-permute-done.12.refs_7_ = bf16[144,1120]{1,0:T(8,128)(2,1)S(1)} collective-permute-done((bf16[144,1120]{1,0:T(8,128)(2,1)S(1)}, bf16[144,1120]{1,0:T(8,128)(2,1)S(1)}, u32[]{:S(2)}, u32[]{:S(2)}) %collective-permute-start.12) | collective-permute-done | bytes 322592 | tf_op jit(solution)/shard_map/ppermute | solution.py:479
  54.7 8.3 %states.1 = f32[560,128]{1,0:T(8,128)S(1)} custom-call(s32[10]{0:T(128)S(1)} %pad_add_fusion.meta, bf16[960,2304]{1,0:T(8,128)(2,1)S(1)} %pack_tokens.1.refs_0_, bf16[960,2304]{1,0:T(8,128)(2,1)S(1)} %collective-permute-done.2.refs_1_, f32[1920,1120]{1,0:T(8,128)S(1)} %kv_part.3.refs_2_, bf16[192,1120]{1,0:T(8,128)(2,1)S(1)} %collective-permute-done.8.refs_3_, ...), custom_call_target="tpu_custom_call" | custom-call | flops 4679270400 | tf_op jit(solution)/shard_map/states/pallas_call | solution.py:68
  63.1 1.5 %collective-permute-start.17 = (bf16[144,1120]{1,0:T(8,128)(2,1)S(1)}, bf16[144,1120]{1,0:T(8,128)(2,1)S(1)}, u32[]{:S(2)}, u32[]{:S(2)}) collective-permute-start(bf16[144,1120]{1,0:T(8,128)(2,1)S(1)} %collective-permute-done.14.refs_7_.refs_14_), channel_id=1, source_target_pairs={{0,4},{4,8},{8,12},{12,14},{14,10},{10,6},{6,2},{2,0},{1,5},{5,9},... | collective-permute-start | bytes 967688 | tf_op jit(solution)/shard_map/ppermute | solution.py:479
  64.9 1.5 %collective-permute-start.16 = (bf16[560,128]{1,0:T(8,128)(2,1)S(1)}, bf16[560,128]{1,0:T(8,128)(2,1)S(1)}, u32[]{:S(2)}, u32[]{:S(2)}) collective-permute-start(bf16[560,128]{1,0:T(8,128)(2,1)S(1)} %pad_maximum_fusion.4), channel_id=1, source_target_pairs={{0,2},{2,0},{4,6},{6,4},{8,10},{10,8},{12,14},{14,12},{1,3},{3,1},... | collective-permute-start | bytes 430088 | tf_op jit(solution)/shard_map/ppermute | solution.py:434
  66.4 6.2 %collective-permute-start.20 = (bf16[144,1120]{1,0:T(8,128)(2,1)S(1)}, bf16[144,1120]{1,0:T(8,128)(2,1)S(1)}, u32[]{:S(2)}, u32[]{:S(2)}) collective-permute-start(bf16[144,1120]{1,0:T(8,128)(2,1)S(1)} %collective-permute-done.6.refs_3_.refs_10_), channel_id=1, source_target_pairs={{0,1},{1,0},{2,3},{3,2},{4,5},{5,4},{6,7},{7,6},{8,9},{9,8},{10,11... | collective-permute-start | bytes 967688 | tf_op jit(solution)/shard_map/ppermute | solution.py:486
  72.7 6.2 %collective-permute-start.22 = (bf16[144,1120]{1,0:T(8,128)(2,1)S(1)}, bf16[144,1120]{1,0:T(8,128)(2,1)S(1)}, u32[]{:S(2)}, u32[]{:S(2)}) collective-permute-start(bf16[144,1120]{1,0:T(8,128)(2,1)S(1)} %collective-permute-done.14.refs_7_.refs_14_), channel_id=1, source_target_pairs={{0,1},{1,0},{2,3},{3,2},{4,5},{5,4},{6,7},{7,6},{8,9},{9,8},{10,11... | collective-permute-start | bytes 967688 | tf_op jit(solution)/shard_map/ppermute | solution.py:486
  78.9 0.6 collective-permute-start.25
  79.5 0.3 subtract_convert_fusion.1
  80.2 1.4 %collective-permute-start.27 = (bf16[80,1120]{1,0:T(8,128)(2,1)S(1)}, bf16[80,1120]{1,0:T(8,128)(2,1)S(1)}, u32[]{:S(2)}, u32[]{:S(2)}) collective-permute-start(bf16[80,1120]{1,0:T(8,128)(2,1)S(1)} %slice.79), channel_id=1, source_target_pairs={{0,4},{4,8},{8,12},{12,14},{14,10},{10,6},{6,2},{2,0},{1,5},{5,9},... | collective-permute-start | bytes 537608 | tf_op jit(solution)/shard_map/ppermute | solution.py:479
  81.6 1.5 %collective-permute-start.19 = (bf16[560,128]{1,0:T(8,128)(2,1)S(1)}, bf16[560,128]{1,0:T(8,128)(2,1)S(1)}, u32[]{:S(2)}, u32[]{:S(2)}) collective-permute-start(bf16[560,128]{1,0:T(8,128)(2,1)S(1)} %pad_maximum_fusion.5), channel_id=1, source_target_pairs={{0,4},{2,6},{4,8},{6,10},{8,12},{10,14},{1,5},{3,7},{5,9},{7,11},{... | collective-permute-start | bytes 430088 | tf_op jit(solution)/shard_map/ppermute | solution.py:434
  83.1 2.2 %copy-done.1 = bf16[960,2304]{1,0:T(8,128)(2,1)S(1)} copy-done((bf16[960,2304]{1,0:T(8,128)(2,1)S(1)}, bf16[960,2304]{1,0:T(8,128)(2,1)}, u32[]{:S(2)}) %copy-start.1) | copy-done | bytes 4423704
  85.4 4.1 %q_early.1.refs_1_ = f32[960,1120]{1,0:T(8,128)S(1)} custom-call(s32[10]{0:T(128)S(1)} %pad_add_fusion.meta, bf16[960,2304]{1,0:T(8,128)(2,1)S(1)} %copy-done.1, bf16[144,1120]{1,0:T(8,128)(2,1)S(1)} %get-tuple-element.35.after_ref.refs_1_.refs_8_, bf16[144,1120]{1,0:T(8,128)(2,1)S(1)} %get-tuple-element.56.refs_2_.refs_9_, ...), custom_call_target="tpu_custom_call" | custom-call | flops 2752512000 | tf_op jit(solution)/shard_map/q_early/pallas_call | solution.py:68
  89.7 1.1 collective-permute-start.29
  90.7 0.2 add_convert_fusion.1
  91.1 1.3 %collective-permute-start.24 = (bf16[560,128]{1,0:T(8,128)(2,1)S(1)}, bf16[560,128]{1,0:T(8,128)(2,1)S(1)}, u32[]{:S(2)}, u32[]{:S(2)}) collective-permute-start(bf16[560,128]{1,0:T(8,128)(2,1)S(1)} %pad_maximum_fusion.6), channel_id=1, source_target_pairs={{0,8},{2,10},{4,12},{6,14},{1,9},{3,11},{5,13},{7,15},{16,24},{18,... | collective-permute-start | bytes 430088 | tf_op jit(solution)/shard_map/ppermute | solution.py:434
  92.4 3.5 %q_late.1.q_ref = bf16[960,1120]{1,0:T(8,128)(2,1)S(1)} custom-call(s32[10]{0:T(128)S(1)} %pad_add_fusion.meta, bf16[960,2304]{1,0:T(8,128)(2,1)S(1)} %copy-done.1, f32[960,1120]{1,0:T(8,128)S(1)} %q_early.1.refs_1_, bf16[144,1120]{1,0:T(8,128)(2,1)S(1)} %collective-permute-done.17.refs_2_, bf16[144,1120]{1,0:T(8,128)(2,1)S(1)} %collective-permute-done.25.refs_3_, ...), custom_call_target="tpu_custom_call" | custom-call | flops 2202009600 | tf_op jit(solution)/shard_map/q_late/pallas_call | solution.py:68
  95.9 6.4 %collective-permute-done.24 = bf16[560,128]{1,0:T(8,128)(2,1)S(1)} collective-permute-done((bf16[560,128]{1,0:T(8,128)(2,1)S(1)}, bf16[560,128]{1,0:T(8,128)(2,1)S(1)}, u32[]{:S(2)}, u32[]{:S(2)}) %collective-permute-start.24) | collective-permute-done | bytes 143392 | tf_op jit(solution)/shard_map/ppermute | solution.py:434
  102.5 0.4 fusion
  102.9 0.2 pad_maximum_fusion.3.mine_ref
  103.2 0.9 collective-permute-start.30
  104.0 1.2 %collective-permute-done.30.theirs_ref = f32[560,128]{1,0:T(8,128)S(1)} collective-permute-done((f32[560,128]{1,0:T(8,128)S(1)}, f32[560,128]{1,0:T(8,128)S(1)}, u32[]{:S(2)}, u32[]{:S(2)}) %collective-permute-start.30) | collective-permute-done | bytes 286752 | tf_op jit(solution)/shard_map/ppermute | solution.py:486
  105.2 4.4 %attend.1 = bf16[960,1120]{1,0:T(8,128)(2,1)} custom-call(s32[10]{0:T(128)S(1)} %pad_add_fusion.meta, bf16[960,1120]{1,0:T(8,128)(2,1)S(1)} %q_late.1.q_ref, f32[560,128]{1,0:T(8,128)S(1)} %pad_maximum_fusion.3.mine_ref, f32[560,128]{1,0:T(8,128)S(1)} %collective-permute-done.30.theirs_ref), custom_call_target="tpu_custom_call" | custom-call | flops 1720320000 | bytes 4300800 | tf_op jit(solution)/shard_map/attend/pallas_call | solution.py:399
  (63 shorter events, 2.1 us)
Async XLA Ops:
  0.0 5.7 %copy-start.2 = (bf16[2,6,80,2240]{3,2,1,0:T(8,128)(2,1)S(1)}, bf16[2,6,80,2240]{3,2,1,0:T(8,128)(2,1)}, u32[]{:S(2)}) copy-start(bf16[2,6,80,2240]{3,2,1,0:T(8,128)(2,1)} %param.3) | copy-start | bytes 12902404
  0.9 1.8 %copy-start.3 = (bf16[280,3360]{1,0:T(8,128)(2,1)S(1)}, bf16[280,3360]{1,0:T(8,128)(2,1)}, u32[]{:S(2)}) copy-start(bf16[280,3360]{1,0:T(8,128)(2,1)} %w_ref.3) | copy-start | bytes 5644804
  3.6 11.1 %collective-permute-start.1 = (bf16[192,1120]{1,0:T(8,128)(2,1)S(1)}, bf16[192,1120]{1,0:T(8,128)(2,1)S(1)}, u32[]{:S(2)}, u32[]{:S(2)}) collective-permute-start(bf16[192,1120]{1,0:T(8,128)(2,1)S(1)} %get-tuple-element.36.refs_3_), channel_id=1, source_target_pairs={{4,0},{8,4},{12,8},{14,12},{10,14},{6,10},{2,6},{0,2},{5,1},{9,5},... | collective-permute-start | bytes 1290248 | tf_op jit(solution)/shard_map/ppermute | solution.py:479
  3.8 10.9 %collective-permute-start = (bf16[192,1120]{1,0:T(8,128)(2,1)S(1)}, bf16[192,1120]{1,0:T(8,128)(2,1)S(1)}, u32[]{:S(2)}, u32[]{:S(2)}) collective-permute-start(bf16[192,1120]{1,0:T(8,128)(2,1)S(1)} %get-tuple-element.34.after_ref.refs_2_.refs_8_), channel_id=1, source_target_pairs={{0,4},{4,8},{8,12},{12,14},{14,10},{10,6},{6,2},{2,0},{1,5},{5,9},... | collective-permute-start | bytes 1290248 | tf_op jit(solution)/shard_map/ppermute | solution.py:479
  8.4 46.4 %copy-start = (bf16[960,2304]{1,0:T(8,128)(2,1)}, bf16[960,2304]{1,0:T(8,128)(2,1)S(1)}, u32[]{:S(2)}) copy-start(bf16[960,2304]{1,0:T(8,128)(2,1)S(1)} %pack_tokens.1.refs_0_) | copy-start | bytes 13271044
  14.7 13.7 %collective-permute-start.2 = (bf16[960,2304]{1,0:T(8,128)(2,1)S(1)}, bf16[960,2304]{1,0:T(8,128)(2,1)S(1)}, u32[]{:S(2)}, u32[]{:S(2)}) collective-permute-start(bf16[960,2304]{1,0:T(8,128)(2,1)S(1)} %pack_tokens.1.refs_0_), channel_id=1, source_target_pairs={{0,1},{1,0},{2,3},{3,2},{4,5},{5,4},{6,7},{7,6},{8,9},{9,8},{10,11... | collective-permute-start | bytes 13271048 | tf_op jit(solution)/shard_map/ppermute | solution.py:486
  16.5 11.9 %collective-permute-start.4 = (bf16[192,1120]{1,0:T(8,128)(2,1)S(1)}, bf16[192,1120]{1,0:T(8,128)(2,1)S(1)}, u32[]{:S(2)}, u32[]{:S(2)}) collective-permute-start(bf16[192,1120]{1,0:T(8,128)(2,1)S(1)} %collective-permute-done.1.refs_6_.refs_10_), channel_id=1, source_target_pairs={{4,0},{8,4},{12,8},{14,12},{10,14},{6,10},{2,6},{0,2},{5,1},{9,5},... | collective-permute-start | bytes 1290248 | tf_op jit(solution)/shard_map/ppermute | solution.py:479
  16.7 11.6 %collective-permute-start.5 = (bf16[192,1120]{1,0:T(8,128)(2,1)S(1)}, bf16[192,1120]{1,0:T(8,128)(2,1)S(1)}, u32[]{:S(2)}, u32[]{:S(2)}) collective-permute-start(bf16[192,1120]{1,0:T(8,128)(2,1)S(1)} %pad_maximum_fusion), channel_id=1, source_target_pairs={{0,16},{16,0},{1,17},{17,1},{2,18},{18,2},{3,19},{19,3},{4,20},{20... | collective-permute-start | bytes 1290248 | tf_op jit(solution)/shard_map/ppermute | solution.py:483
  17.0 11.4 %collective-permute-start.3 = (bf16[192,1120]{1,0:T(8,128)(2,1)S(1)}, bf16[192,1120]{1,0:T(8,128)(2,1)S(1)}, u32[]{:S(2)}, u32[]{:S(2)}) collective-permute-start(bf16[192,1120]{1,0:T(8,128)(2,1)S(1)} %collective-permute-done.refs_4_.refs_9_), channel_id=1, source_target_pairs={{0,4},{4,8},{8,12},{12,14},{14,10},{10,6},{6,2},{2,0},{1,5},{5,9},... | collective-permute-start | bytes 1290248 | tf_op jit(solution)/shard_map/ppermute | solution.py:479
  28.5 10.5 %collective-permute-start.10 = (bf16[192,1120]{1,0:T(8,128)(2,1)S(1)}, bf16[192,1120]{1,0:T(8,128)(2,1)S(1)}, u32[]{:S(2)}, u32[]{:S(2)}) collective-permute-start(bf16[192,1120]{1,0:T(8,128)(2,1)S(1)} %pad_maximum_fusion.1), channel_id=1, source_target_pairs={{0,16},{16,0},{1,17},{17,1},{2,18},{18,2},{3,19},{19,3},{4,20},{20... | collective-permute-start | bytes 1290248 | tf_op jit(solution)/shard_map/ppermute | solution.py:483
  29.5 10.0 %collective-permute-start.8 = (bf16[192,1120]{1,0:T(8,128)(2,1)S(1)}, bf16[192,1120]{1,0:T(8,128)(2,1)S(1)}, u32[]{:S(2)}, u32[]{:S(2)}) collective-permute-start(bf16[192,1120]{1,0:T(8,128)(2,1)S(1)} %collective-permute-done.3.refs_3_.refs_11_), channel_id=1, source_target_pairs={{0,4},{4,8},{8,12},{12,14},{14,10},{10,6},{6,2},{2,0},{1,5},{5,9},... | collective-permute-start | bytes 1290248 | tf_op jit(solution)/shard_map/ppermute | solution.py:479
  30.8 9.7 %collective-permute-start.9 = (bf16[192,1120]{1,0:T(8,128)(2,1)S(1)}, bf16[192,1120]{1,0:T(8,128)(2,1)S(1)}, u32[]{:S(2)}, u32[]{:S(2)}) collective-permute-start(bf16[192,1120]{1,0:T(8,128)(2,1)S(1)} %collective-permute-done.4.refs_5_.refs_12_), channel_id=1, source_target_pairs={{4,0},{8,4},{12,8},{14,12},{10,14},{6,10},{2,6},{0,2},{5,1},{9,5},... | collective-permute-start | bytes 1290248 | tf_op jit(solution)/shard_map/ppermute | solution.py:479
  31.0 16.6 %collective-permute-start.7 = (bf16[144,1120]{1,0:T(8,128)(2,1)S(1)}, bf16[144,1120]{1,0:T(8,128)(2,1)S(1)}, u32[]{:S(2)}, u32[]{:S(2)}) collective-permute-start(bf16[144,1120]{1,0:T(8,128)(2,1)S(1)} %get-tuple-element.35.after_ref.refs_1_.refs_8_), channel_id=1, source_target_pairs={{4,0},{8,4},{12,8},{14,12},{10,14},{6,10},{2,6},{0,2},{5,1},{9,5},... | collective-permute-start | bytes 967688 | tf_op jit(solution)/shard_map/ppermute | solution.py:479
  31.2 16.5 %collective-permute-start.6 = (bf16[144,1120]{1,0:T(8,128)(2,1)S(1)}, bf16[144,1120]{1,0:T(8,128)(2,1)S(1)}, u32[]{:S(2)}, u32[]{:S(2)}) collective-permute-start(bf16[144,1120]{1,0:T(8,128)(2,1)S(1)} %get-tuple-element.35.after_ref.refs_1_.refs_8_), channel_id=1, source_target_pairs={{0,4},{4,8},{8,12},{12,14},{14,10},{10,6},{6,2},{2,0},{1,5},{5,9},... | collective-permute-start | bytes 967688 | tf_op jit(solution)/shard_map/ppermute | solution.py:479
  40.6 14.1 %collective-permute-start.13 = (bf16[192,1120]{1,0:T(8,128)(2,1)S(1)}, bf16[192,1120]{1,0:T(8,128)(2,1)S(1)}, u32[]{:S(2)}, u32[]{:S(2)}) collective-permute-start(bf16[192,1120]{1,0:T(8,128)(2,1)S(1)} %pad_maximum_fusion.2), channel_id=1, source_target_pairs={{0,16},{16,0},{1,17},{17,1},{2,18},{18,2},{3,19},{19,3},{4,20},{20... | collective-permute-start | bytes 1290248 | tf_op jit(solution)/shard_map/ppermute | solution.py:483
  41.4 13.3 %collective-permute-start.12 = (bf16[144,1120]{1,0:T(8,128)(2,1)S(1)}, bf16[144,1120]{1,0:T(8,128)(2,1)S(1)}, u32[]{:S(2)}, u32[]{:S(2)}) collective-permute-start(bf16[144,1120]{1,0:T(8,128)(2,1)S(1)} %slice.68), channel_id=1, source_target_pairs={{4,0},{8,4},{12,8},{14,12},{10,14},{6,10},{2,6},{0,2},{5,1},{9,5},... | collective-permute-start | bytes 967688 | tf_op jit(solution)/shard_map/ppermute | solution.py:479
  41.6 13.1 %collective-permute-start.11 = (bf16[144,1120]{1,0:T(8,128)(2,1)S(1)}, bf16[144,1120]{1,0:T(8,128)(2,1)S(1)}, u32[]{:S(2)}, u32[]{:S(2)}) collective-permute-start(bf16[144,1120]{1,0:T(8,128)(2,1)S(1)} %slice.67), channel_id=1, source_target_pairs={{0,4},{4,8},{8,12},{12,14},{14,10},{10,6},{6,2},{2,0},{1,5},{5,9},... | collective-permute-start | bytes 967688 | tf_op jit(solution)/shard_map/ppermute | solution.py:479
  47.6 15.4 %collective-permute-start.14 = (bf16[144,1120]{1,0:T(8,128)(2,1)S(1)}, bf16[144,1120]{1,0:T(8,128)(2,1)S(1)}, u32[]{:S(2)}, u32[]{:S(2)}) collective-permute-start(bf16[144,1120]{1,0:T(8,128)(2,1)S(1)} %collective-permute-done.6.refs_3_.refs_10_), channel_id=1, source_target_pairs={{0,4},{4,8},{8,12},{12,14},{14,10},{10,6},{6,2},{2,0},{1,5},{5,9},... | collective-permute-start | bytes 967688 | tf_op jit(solution)/shard_map/ppermute | solution.py:479
  48.9 14.1 %collective-permute-start.15 = (bf16[144,1120]{1,0:T(8,128)(2,1)S(1)}, bf16[144,1120]{1,0:T(8,128)(2,1)S(1)}, u32[]{:S(2)}, u32[]{:S(2)}) collective-permute-start(bf16[144,1120]{1,0:T(8,128)(2,1)S(1)} %collective-permute-done.7.refs_5_.refs_12_), channel_id=1, source_target_pairs={{4,0},{8,4},{12,8},{14,12},{10,14},{6,10},{2,6},{0,2},{5,1},{9,5},... | collective-permute-start | bytes 967688 | tf_op jit(solution)/shard_map/ppermute | solution.py:479
  63.1 15.8 %collective-permute-start.17 = (bf16[144,1120]{1,0:T(8,128)(2,1)S(1)}, bf16[144,1120]{1,0:T(8,128)(2,1)S(1)}, u32[]{:S(2)}, u32[]{:S(2)}) collective-permute-start(bf16[144,1120]{1,0:T(8,128)(2,1)S(1)} %collective-permute-done.14.refs_7_.refs_14_), channel_id=1, source_target_pairs={{0,4},{4,8},{8,12},{12,14},{14,10},{10,6},{6,2},{2,0},{1,5},{5,9},... | collective-permute-start | bytes 967688 | tf_op jit(solution)/shard_map/ppermute | solution.py:479
  64.5 14.4 %collective-permute-start.18 = (bf16[144,1120]{1,0:T(8,128)(2,1)S(1)}, bf16[144,1120]{1,0:T(8,128)(2,1)S(1)}, u32[]{:S(2)}, u32[]{:S(2)}) collective-permute-start(bf16[144,1120]{1,0:T(8,128)(2,1)S(1)} %collective-permute-done.15.refs_9_.refs_16_), channel_id=1, source_target_pairs={{4,0},{8,4},{12,8},{14,12},{10,14},{6,10},{2,6},{0,2},{5,1},{9,5},... | collective-permute-start | bytes 967688 | tf_op jit(solution)/shard_map/ppermute | solution.py:479
  64.9 7.7 %collective-permute-start.16 = (bf16[560,128]{1,0:T(8,128)(2,1)S(1)}, bf16[560,128]{1,0:T(8,128)(2,1)S(1)}, u32[]{:S(2)}, u32[]{:S(2)}) collective-permute-start(bf16[560,128]{1,0:T(8,128)(2,1)S(1)} %pad_maximum_fusion.4), channel_id=1, source_target_pairs={{0,2},{2,0},{4,6},{6,4},{8,10},{10,8},{12,14},{14,12},{1,3},{3,1},... | collective-permute-start | bytes 430088 | tf_op jit(solution)/shard_map/ppermute | solution.py:434
  66.4 13.6 %collective-permute-start.20 = (bf16[144,1120]{1,0:T(8,128)(2,1)S(1)}, bf16[144,1120]{1,0:T(8,128)(2,1)S(1)}, u32[]{:S(2)}, u32[]{:S(2)}) collective-permute-start(bf16[144,1120]{1,0:T(8,128)(2,1)S(1)} %collective-permute-done.6.refs_3_.refs_10_), channel_id=1, source_target_pairs={{0,1},{1,0},{2,3},{3,2},{4,5},{5,4},{6,7},{7,6},{8,9},{9,8},{10,11... | collective-permute-start | bytes 967688 | tf_op jit(solution)/shard_map/ppermute | solution.py:486
  72.7 7.4 %collective-permute-start.21 = (bf16[144,1120]{1,0:T(8,128)(2,1)S(1)}, bf16[144,1120]{1,0:T(8,128)(2,1)S(1)}, u32[]{:S(2)}, u32[]{:S(2)}) collective-permute-start(bf16[144,1120]{1,0:T(8,128)(2,1)S(1)} %collective-permute-done.7.refs_5_.refs_12_), channel_id=1, source_target_pairs={{0,1},{1,0},{2,3},{3,2},{4,5},{5,4},{6,7},{7,6},{8,9},{9,8},{10,11... | collective-permute-start | bytes 967688 | tf_op jit(solution)/shard_map/ppermute | solution.py:486
  72.7 7.5 %collective-permute-start.22 = (bf16[144,1120]{1,0:T(8,128)(2,1)S(1)}, bf16[144,1120]{1,0:T(8,128)(2,1)S(1)}, u32[]{:S(2)}, u32[]{:S(2)}) collective-permute-start(bf16[144,1120]{1,0:T(8,128)(2,1)S(1)} %collective-permute-done.14.refs_7_.refs_14_), channel_id=1, source_target_pairs={{0,1},{1,0},{2,3},{3,2},{4,5},{5,4},{6,7},{7,6},{8,9},{9,8},{10,11... | collective-permute-start | bytes 967688 | tf_op jit(solution)/shard_map/ppermute | solution.py:486
  78.9 2.8 %collective-permute-start.23 = (bf16[144,1120]{1,0:T(8,128)(2,1)S(1)}, bf16[144,1120]{1,0:T(8,128)(2,1)S(1)}, u32[]{:S(2)}, u32[]{:S(2)}) collective-permute-start(bf16[144,1120]{1,0:T(8,128)(2,1)S(1)} %collective-permute-done.15.refs_9_.refs_16_), channel_id=1, source_target_pairs={{0,1},{1,0},{2,3},{3,2},{4,5},{5,4},{6,7},{7,6},{8,9},{9,8},{10,11... | collective-permute-start | bytes 967688 | tf_op jit(solution)/shard_map/ppermute | solution.py:486
  78.9 13.5 %collective-permute-start.25 = (bf16[144,1120]{1,0:T(8,128)(2,1)S(1)}, bf16[144,1120]{1,0:T(8,128)(2,1)S(1)}, u32[]{:S(2)}, u32[]{:S(2)}) collective-permute-start(bf16[144,1120]{1,0:T(8,128)(2,1)S(1)} %collective-permute-done.17.refs_2_), channel_id=1, source_target_pairs={{0,1},{1,0},{2,3},{3,2},{4,5},{5,4},{6,7},{7,6},{8,9},{9,8},{10,11... | collective-permute-start | bytes 967688 | tf_op jit(solution)/shard_map/ppermute | solution.py:486
  80.0 12.4 %collective-permute-start.26 = (bf16[144,1120]{1,0:T(8,128)(2,1)S(1)}, bf16[144,1120]{1,0:T(8,128)(2,1)S(1)}, u32[]{:S(2)}, u32[]{:S(2)}) collective-permute-start(bf16[144,1120]{1,0:T(8,128)(2,1)S(1)} %collective-permute-done.18.refs_4_), channel_id=1, source_target_pairs={{0,1},{1,0},{2,3},{3,2},{4,5},{5,4},{6,7},{7,6},{8,9},{9,8},{10,11... | collective-permute-start | bytes 967688 | tf_op jit(solution)/shard_map/ppermute | solution.py:486
  80.1 9.5 %collective-permute-start.28 = (bf16[64,1120]{1,0:T(8,128)(2,1)S(1)}, bf16[64,1120]{1,0:T(8,128)(2,1)S(1)}, u32[]{:S(2)}, u32[]{:S(2)}) collective-permute-start(bf16[64,1120]{1,0:T(8,128)(2,1)S(1)} %slice.80), channel_id=1, source_target_pairs={{4,0},{8,4},{12,8},{14,12},{10,14},{6,10},{2,6},{0,2},{5,1},{9,5},... | collective-permute-start | bytes 430088 | tf_op jit(solution)/shard_map/ppermute | solution.py:479
  80.2 9.4 %collective-permute-start.27 = (bf16[80,1120]{1,0:T(8,128)(2,1)S(1)}, bf16[80,1120]{1,0:T(8,128)(2,1)S(1)}, u32[]{:S(2)}, u32[]{:S(2)}) collective-permute-start(bf16[80,1120]{1,0:T(8,128)(2,1)S(1)} %slice.79), channel_id=1, source_target_pairs={{0,4},{4,8},{8,12},{12,14},{14,10},{10,6},{6,2},{2,0},{1,5},{5,9},... | collective-permute-start | bytes 537608 | tf_op jit(solution)/shard_map/ppermute | solution.py:479
  81.6 7.9 %collective-permute-start.19 = (bf16[560,128]{1,0:T(8,128)(2,1)S(1)}, bf16[560,128]{1,0:T(8,128)(2,1)S(1)}, u32[]{:S(2)}, u32[]{:S(2)}) collective-permute-start(bf16[560,128]{1,0:T(8,128)(2,1)S(1)} %pad_maximum_fusion.5), channel_id=1, source_target_pairs={{0,4},{2,6},{4,8},{6,10},{8,12},{10,14},{1,5},{3,7},{5,9},{7,11},{... | collective-permute-start | bytes 430088 | tf_op jit(solution)/shard_map/ppermute | solution.py:434
  83.1 2.3 %copy-start.1 = (bf16[960,2304]{1,0:T(8,128)(2,1)S(1)}, bf16[960,2304]{1,0:T(8,128)(2,1)}, u32[]{:S(2)}) copy-start(bf16[960,2304]{1,0:T(8,128)(2,1)} %copy-done) | copy-start | bytes 13271044
  89.7 2.8 %collective-permute-start.29 = (bf16[144,1120]{1,0:T(8,128)(2,1)S(1)}, bf16[144,1120]{1,0:T(8,128)(2,1)S(1)}, u32[]{:S(2)}, u32[]{:S(2)}) collective-permute-start(bf16[144,1120]{1,0:T(8,128)(2,1)S(1)} %constant_dynamic-update-slice_fusion.refs_6_), channel_id=1, source_target_pairs={{0,1},{1,0},{2,3},{3,2},{4,5},{5,4},{6,7},{7,6},{8,9},{9,8},{10,11... | collective-permute-start | bytes 967688 | tf_op jit(solution)/shard_map/ppermute | solution.py:486
  91.1 11.2 %collective-permute-start.24 = (bf16[560,128]{1,0:T(8,128)(2,1)S(1)}, bf16[560,128]{1,0:T(8,128)(2,1)S(1)}, u32[]{:S(2)}, u32[]{:S(2)}) collective-permute-start(bf16[560,128]{1,0:T(8,128)(2,1)S(1)} %pad_maximum_fusion.6), channel_id=1, source_target_pairs={{0,8},{2,10},{4,12},{6,14},{1,9},{3,11},{5,13},{7,15},{16,24},{18,... | collective-permute-start | bytes 430088 | tf_op jit(solution)/shard_map/ppermute | solution.py:434
  103.2 2.1 %collective-permute-start.30 = (f32[560,128]{1,0:T(8,128)S(1)}, f32[560,128]{1,0:T(8,128)S(1)}, u32[]{:S(2)}, u32[]{:S(2)}) collective-permute-start(f32[560,128]{1,0:T(8,128)S(1)} %pad_maximum_fusion.3.mine_ref), channel_id=1, source_target_pairs={{0,1},{1,0},{2,3},{3,2},{4,5},{5,4},{6,7},{7,6},{8,9},{9,8},{10,11... | collective-permute-start | bytes 860168 | tf_op jit(solution)/shard_map/ppermute | solution.py:486
